TPU v7x, 512 devices: a whole 4x8x8 slice. The times are simulated.
512 devices in a mesh: seq: 128 (over z, x, y_lo), head: 4 (over y_hi, core).
Axes of the slice: x: 4, y: 8 (y_hi: 2, y_lo: 4; y = y_hi * 4 + y_lo), z: 8, core: 2. Of those that a mesh axis runs over, the one named last changes fastest.
Arguments:
- queries: bfloat16 [32768, 2048], P(('seq', 'head')), may hold values from -70 to 70
- keys: bfloat16 [32768, 2048], P(('seq', 'head')), may hold values from -21 to 21
- values: bfloat16 [32768, 2048], P(('seq', 'head')), may hold values from -16 to 16
- cotangent: bfloat16 [32768, 2048], P(('seq', 'head')), may hold values from -16 to 16
Outputs:
- output: bfloat16 [32768, 2048], P(('seq', 'head'))
- query_grads: bfloat16 [32768, 2048], P(('seq', 'head'))
- key_grads: bfloat16 [32768, 2048], P(('seq', 'head'))
- value_grads: bfloat16 [32768, 2048], P(('seq', 'head'))
All inputs are finite; a program needn't handle non-finite values.
Results may differ from a plain program's by a relative error of at most 0.011.
Values may be sent and summed in bfloat16 or wider, within the bound.
No kernel may reach another device: no remote copies, remote signals or barrier semaphores. Data moves between devices by JAX's collectives and lax.ppermute only.
A program may use at most 64 MiB of HBM per device.

v0:
```python
import functools
import math

import jax
import jax.numpy as jnp
from jax import lax
from jax.sharding import PartitionSpec as P

DH = 128
BLOCK = 128


NEG_FILL = -1e30
LOG_TWO = math.log(2.0)


def padded_2(block, sides, width):
    for axis, dim in sides:
        count = lax.axis_size(axis)
        forward = [(i, i + 1) for i in range(count - 1)]
        backward = [(target, source) for source, target in forward]
        low = lax.ppermute(
            lax.slice_in_dim(block, block.shape[dim] - width, None, axis=dim), axis, forward
        )
        high = lax.ppermute(lax.slice_in_dim(block, 0, width, axis=dim), axis, backward)
        block = jnp.concatenate([low, block, high], axis=dim)
    return block


def partner_2(array, axis, stride):
    return lax.ppermute(array, axis, [(i, i ^ 1 << stride) for i in range(lax.axis_size(axis))])


def halve_rows(x):
    shape = x.shape
    pairs = x.reshape(shape[:2] + (shape[2] // 2, 2) + shape[3:]).astype(jnp.float32)
    return ((pairs[:, :, :, 0] + pairs[:, :, :, 1]) * 0.5).astype(jnp.bfloat16)


def spread_rows(grad):
    return jnp.repeat(grad * 0.5, 2, axis=2)


def group_rows(x, groups):
    shape = x.shape
    return x.reshape(shape[:1] + (groups, shape[1] // groups) + shape[2:])


def head_major(x, heads_here):
    return x.reshape(x.shape[0], heads_here, DH).transpose(1, 0, 2)


def token_major(x):
    return x.transpose(1, 0, 2).reshape(x.shape[1], x.shape[0] * x.shape[2])


def on_device(queries, keys, values, cotangent):
    q_in, k_in, v_in, dy_in = (
        lax.all_to_all(queries, "head", split_axis=1, concat_axis=0, tiled=True),
        lax.all_to_all(keys, "head", split_axis=1, concat_axis=0, tiled=True),
        lax.all_to_all(values, "head", split_axis=1, concat_axis=0, tiled=True),
        lax.all_to_all(cotangent, "head", split_axis=1, concat_axis=0, tiled=True),
    )
    tokens_here, features_here = q_in.shape
    heads_here = features_here // DH
    blocks_here = tokens_here // BLOCK
    local_levels = blocks_here.bit_length() - 1
    seq_count = lax.axis_size("seq")
    far_count = seq_count.bit_length() - 1
    place = lax.axis_index("seq")
    scale = DH ** (-0.5)
    query = head_major(q_in, heads_here)
    grad_out = head_major(dy_in, heads_here)
    pair = jnp.stack((head_major(k_in, heads_here), head_major(v_in, heads_here)), 0)
    padded = padded_2(pair, (("seq", 2),), BLOCK)
    extended = padded.reshape((2, heads_here, blocks_here + 2, BLOCK, DH))
    window = jnp.concatenate(
        (extended[:, :, :-2], extended[:, :, 1:-1], extended[:, :, 2:]), axis=3
    )
    lane = jnp.arange(3 * BLOCK) // BLOCK
    row_block = jnp.arange(blocks_here)
    left_gap = (row_block[:, None] == 0) & (lane[None, :] == 0) & (place == 0)
    right_gap = (
        (row_block[:, None] == blocks_here - 1) & (lane[None, :] == 2) & (place == seq_count - 1)
    )
    allowed = jnp.logical_not(left_gap | right_gap)[None, :, None, :]
    levels = [(window, 0.0, allowed)]
    coarse = pair
    coarse = halve_rows(coarse)
    own = coarse
    pair_slots = []
    for bit in range(far_count):
        partner = partner_2(own, "seq", bit)
        pair_slots.append(len(levels))
        levels.append((partner[:, :, None], (local_levels + bit) * LOG_TWO, None))
        if bit + 1 < far_count:
            upper = place // 2**bit % 2 == 1
            joined = jnp.where(
                upper, jnp.concatenate((partner, own), 2), jnp.concatenate((own, partner), 2)
            )
            own = halve_rows(joined)
    flat_scores = []
    for keyset, shift_by, allow in levels:
        grouped = group_rows(query, keyset.shape[2])
        score = (
            jnp.einsum("hgqd,hgkd->hgqk", grouped, keyset[0], preferred_element_type=jnp.float32)
            * scale
            + shift_by
        )
        if allow is not None:
            score = jnp.where(allow, score, NEG_FILL)
        flat_scores.append(score.reshape(heads_here, tokens_here, -1))
    row_max = functools.reduce(jnp.maximum, [jnp.max(score, axis=-1) for score in flat_scores])
    raised = [jnp.exp(score - row_max[..., None]) for score in flat_scores]
    total = functools.reduce(jnp.add, [jnp.sum(item, axis=-1) for item in raised])
    weights = [item / total[..., None] for item in raised]
    rounded = [item.astype(jnp.bfloat16) for item in weights]
    attended = jnp.zeros((heads_here, tokens_here, DH), jnp.float32)
    for (keyset, shift_by, allow), light in zip(levels, rounded):
        groups = keyset.shape[2]
        attended = attended + jnp.einsum(
            "hgqk,hgkd->hgqd",
            group_rows(light, groups),
            keyset[1],
            preferred_element_type=jnp.float32,
        ).reshape(heads_here, tokens_here, DH)
    output = attended.astype(jnp.bfloat16)
    delta = jnp.sum(grad_out.astype(jnp.float32) * attended, axis=-1)
    query_grad = jnp.zeros((heads_here, tokens_here, DH), jnp.float32)
    level_grads = []
    for (keyset, shift_by, allow), weight, light in zip(levels, weights, rounded):
        groups = keyset.shape[2]
        grouped_query = group_rows(query, groups)
        grouped_grad = group_rows(grad_out, groups)
        pushed = jnp.einsum(
            "hgqd,hgkd->hgqk", grouped_grad, keyset[1], preferred_element_type=jnp.float32
        )
        score_grad = (
            group_rows(weight, groups) * (pushed - group_rows(delta, groups)[..., None]) * scale
        ).astype(jnp.bfloat16)
        query_grad = query_grad + jnp.einsum(
            "hgqk,hgkd->hgqd", score_grad, keyset[0], preferred_element_type=jnp.float32
        ).reshape(heads_here, tokens_here, DH)
        key_grad = jnp.einsum(
            "hgqk,hgqd->hgkd", score_grad, grouped_query, preferred_element_type=jnp.float32
        )
        value_grad = jnp.einsum(
            "hgqk,hgqd->hgkd",
            group_rows(light, groups),
            grouped_grad,
            preferred_element_type=jnp.float32,
        )
        level_grads.append(jnp.stack((key_grad, value_grad), 0))
    near = level_grads[0]
    padding = ((0, 0), (0, 0))
    lead = ((0, 0), (0, 0))
    spread_back = (
        jnp.pad(near[:, :, :, :BLOCK], lead + ((0, 2),) + padding)
        + jnp.pad(near[:, :, :, BLOCK : 2 * BLOCK], lead + ((1, 1),) + padding)
        + jnp.pad(near[:, :, :, 2 * BLOCK :], lead + ((2, 0),) + padding)
    )
    interior = spread_back[:, :, 1:-1].reshape((2, heads_here, tokens_here, DH))
    rims = jnp.concatenate((spread_back[:, :, 0], spread_back[:, :, -1]), 2)
    returned = padded_2(rims, (("seq", 2),), BLOCK)
    interior = (
        interior.at[:, :, :BLOCK]
        .add(returned[:, :, :BLOCK])
        .at[:, :, -BLOCK:]
        .add(returned[:, :, -BLOCK:])
    )
    carry = None
    for bit in reversed(range(far_count)):
        sibling_grad = level_grads[pair_slots[bit]][:, :, 0]
        upper = place // 2**bit % 2 == 1
        if carry is None:
            message = sibling_grad
            kept = None
        else:
            doubled = spread_rows(carry)
            low_half = doubled[:, :, :BLOCK]
            high_half = doubled[:, :, BLOCK:]
            kept = jnp.where(upper, high_half, low_half)
            message = jnp.where(upper, low_half, high_half) + sibling_grad
        received = partner_2(message, "seq", bit)
        carry = received if kept is None else kept + received
    down = carry
    down = spread_rows(down)
    grads_pair = interior + down
    output_rows = token_major(output)
    query_out = token_major(query_grad.astype(jnp.bfloat16))
    key_out = token_major(grads_pair[0].astype(jnp.bfloat16))
    value_out = token_major(grads_pair[1].astype(jnp.bfloat16))
    return (
        lax.all_to_all(output_rows, "head", split_axis=0, concat_axis=1, tiled=True),
        lax.all_to_all(query_out, "head", split_axis=0, concat_axis=1, tiled=True),
        lax.all_to_all(key_out, "head", split_axis=0, concat_axis=1, tiled=True),
        lax.all_to_all(value_out, "head", split_axis=0, concat_axis=1, tiled=True),
    )


def solution(mesh):
    placed = (
        P(("seq", "head"), None),
        P(("seq", "head"), None),
        P(("seq", "head"), None),
        P(("seq", "head"), None),
    )
    return jax.shard_map(
        on_device,
        mesh=mesh,
        in_specs=placed,
        out_specs=(
            P(("seq", "head"), None),
            P(("seq", "head"), None),
            P(("seq", "head"), None),
            P(("seq", "head"), None),
        ),
        check_vma=False,
    )
```

profile of v0, /device:TPU:6, one launch (start us, length us, event | category | flops | bytes accessed | tf_op | source)
XLA Modules:
  0.0 408.9 jit_solution(6486206127963080716)
XLA Ops:
  2.4 7.1 %all-to-all-start.1 = ((bf16[64,4,512]{2,0,1:T(8,128)(2,1)}), bf16[64,4,512]{2,0,1:T(8,128)(2,1)S(1)}, u32[]{:S(2)}, u32[]{:S(2)}) async-start(bf16[64,4,512]{2,0,1:T(8,128)(2,1)} %bitcast.494), calls=%async_computation.1 | async-start | bytes 524288 | tf_op jit(solution)/shard_map/all_to_all | solution.py:61
  11.1 8.4 %all-to-all-done.1 = bf16[64,4,512]{2,0,1:T(8,128)(2,1)S(1)} async-done(((bf16[64,4,512]{2,0,1:T(8,128)(2,1)}), bf16[64,4,512]{2,0,1:T(8,128)(2,1)S(1)}, u32[]{:S(2)}, u32[]{:S(2)}) %all-to-all-start.1) | async-done | bytes 262176 | tf_op jit(solution)/shard_map/all_to_all | solution.py:61
  19.5 3.4 all-to-all-start
  23.8 11.9 %all-to-all-done = bf16[64,4,512]{2,0,1:T(8,128)(2,1)S(1)} async-done(((bf16[64,4,512]{2,0,1:T(8,128)(2,1)}), bf16[64,4,512]{2,0,1:T(8,128)(2,1)S(1)}, u32[]{:S(2)}, u32[]{:S(2)}) %all-to-all-start) | async-done | bytes 262176 | tf_op jit(solution)/shard_map/all_to_all | solution.py:60
  35.7 3.4 all-to-all-start.4
  39.3 2.7 collective-permute-start.2
  43.9 5.1 %collective-permute-start.1 = (bf16[2,4,128,128]{3,1,2,0:T(4,128)(2,1)}, bf16[2,4,128,128]{3,1,2,0:T(4,128)(2,1)}, u32[]{:S(2)}, u32[]{:S(2)}) collective-permute-start(bf16[2,4,128,128]{3,1,2,0:T(4,128)(2,1)} %get-tuple-element.47), channel_id=1, source_target_pairs={{4,0},{8,4},{12,8},{16,12},{20,16},{24,20},{28,24},{32,28},{36,32}... | collective-permute-start | bytes 786440 | tf_op jit(solution)/shard_map/ppermute | solution.py:25
  54.0 6.9 %all-to-all-start.2 = ((bf16[64,4,512]{2,0,1:T(8,128)(2,1)}), bf16[64,4,512]{2,0,1:T(8,128)(2,1)S(1)}, u32[]{:S(2)}, u32[]{:S(2)}) async-start(bf16[64,4,512]{2,0,1:T(8,128)(2,1)} %bitcast.493), calls=%async_computation.2 | async-start | bytes 524288 | tf_op jit(solution)/shard_map/all_to_all | solution.py:59
  60.9 3.0 collective-permute-start.3
  65.7 8.7 %all-to-all-done.2 = bf16[64,4,512]{2,0,1:T(8,128)(2,1)S(1)} async-done(((bf16[64,4,512]{2,0,1:T(8,128)(2,1)}), bf16[64,4,512]{2,0,1:T(8,128)(2,1)S(1)}, u32[]{:S(2)}, u32[]{:S(2)}) %all-to-all-start.2) | async-done | bytes 262176 | tf_op jit(solution)/shard_map/all_to_all | solution.py:59
  76.6 7.0 %collective-permute-done.3 = bf16[2,4,128,128]{3,2,1,0:T(8,128)(2,1)S(1)} collective-permute-done((bf16[2,4,128,128]{3,2,1,0:T(8,128)(2,1)S(1)}, bf16[2,4,128,128]{3,2,1,0:T(8,128)(2,1)S(1)}, u32[]{:S(2)}, u32[]{:S(2)}) %collective-permute-start.3) | collective-permute-done | bytes 262176 | tf_op jit(solution)/shard_map/ppermute | solution.py:31
  84.8 2.7 collective-permute-start.4
  88.0 6.7 %collective-permute-done.4 = bf16[2,4,128,128]{3,2,1,0:T(8,128)(2,1)S(1)} collective-permute-done((bf16[2,4,128,128]{3,2,1,0:T(8,128)(2,1)S(1)}, bf16[2,4,128,128]{3,2,1,0:T(8,128)(2,1)S(1)}, u32[]{:S(2)}, u32[]{:S(2)}) %collective-permute-start.4) | collective-permute-done | bytes 262176 | tf_op jit(solution)/shard_map/ppermute | solution.py:31
  95.7 3.3 collective-permute-start.5
  100.6 5.5 %collective-permute-done.5 = bf16[2,4,128,128]{3,2,1,0:T(8,128)(2,1)S(1)} collective-permute-done((bf16[2,4,128,128]{3,2,1,0:T(8,128)(2,1)S(1)}, bf16[2,4,128,128]{3,2,1,0:T(8,128)(2,1)S(1)}, u32[]{:S(2)}, u32[]{:S(2)}) %collective-permute-start.5) | collective-permute-done | bytes 262176 | tf_op jit(solution)/shard_map/ppermute | solution.py:31
  107.8 4.3 %collective-permute-start.6 = (bf16[2,4,128,128]{3,2,1,0:T(8,128)(2,1)}, bf16[2,4,128,128]{3,2,1,0:T(8,128)(2,1)}, u32[]{:S(2)}, u32[]{:S(2)}) collective-permute-start(bf16[2,4,128,128]{3,2,1,0:T(8,128)(2,1)} %fusion.94), channel_id=1, source_target_pairs={{0,64},{4,68},{8,72},{12,76},{16,80},{20,84},{24,88},{28,92},{32,9... | collective-permute-start | bytes 786440 | tf_op jit(solution)/shard_map/ppermute | solution.py:31
  113.4 3.3 collective-permute-done.6
  119.2 6.1 %collective-permute-start.7 = (bf16[2,4,128,128]{3,2,1,0:T(8,128)(2,1)S(1)}, bf16[2,4,128,128]{3,2,1,0:T(8,128)(2,1)}, u32[]{:S(2)}, u32[]{:S(2)}) collective-permute-start(bf16[2,4,128,128]{3,2,1,0:T(8,128)(2,1)S(1)} %fusion.95), channel_id=1, source_target_pairs={{0,128},{4,132},{8,136},{12,140},{16,144},{20,148},{24,152},{28,15... | collective-permute-start | bytes 786440 | tf_op jit(solution)/shard_map/ppermute | solution.py:31
  126.6 7.8 %collective-permute-done.7 = bf16[2,4,128,128]{3,2,1,0:T(8,128)(2,1)} collective-permute-done((bf16[2,4,128,128]{3,2,1,0:T(8,128)(2,1)S(1)}, bf16[2,4,128,128]{3,2,1,0:T(8,128)(2,1)}, u32[]{:S(2)}, u32[]{:S(2)}) %collective-permute-start.7) | collective-permute-done | bytes 262176 | tf_op jit(solution)/shard_map/ppermute | solution.py:31
  137.7 9.0 %collective-permute-start.8 = (bf16[2,4,128,128]{3,2,1,0:T(8,128)(2,1)}, bf16[2,4,128,128]{3,2,1,0:T(8,128)(2,1)}, u32[]{:S(2)}, u32[]{:S(2)}) collective-permute-start(bf16[2,4,128,128]{3,2,1,0:T(8,128)(2,1)} %fusion.96), channel_id=1, source_target_pairs={{0,256},{4,260},{8,264},{12,268},{16,272},{20,276},{24,280},{28,28... | collective-permute-start | bytes 786440 | tf_op jit(solution)/shard_map/ppermute | solution.py:31
  146.7 1.9 fusion.202
  148.7 1.9 fusion.201
  150.6 7.0 %collective-permute-done.8 = bf16[2,4,128,128]{3,2,1,0:T(8,128)(2,1)} collective-permute-done((bf16[2,4,128,128]{3,2,1,0:T(8,128)(2,1)}, bf16[2,4,128,128]{3,2,1,0:T(8,128)(2,1)}, u32[]{:S(2)}, u32[]{:S(2)}) %collective-permute-start.8) | collective-permute-done | bytes 262176 | tf_op jit(solution)/shard_map/ppermute | solution.py:31
  157.6 1.9 fusion.200
  159.6 2.1 fusion.77
  171.4 2.0 copy.145
  182.0 4.0 all-to-all-start.3
  186.1 1.9 convolution_bitcast_fusion
  190.9 3.7 collective-permute-start.9
  198.3 4.8 %collective-permute-start.11 = (f32[2,4,128,128]{3,2,1,0:T(8,128)S(1)}, f32[2,4,128,128]{3,2,1,0:T(8,128)S(1)}, u32[]{:S(2)}, u32[]{:S(2)}) collective-permute-start(f32[2,4,128,128]{3,2,1,0:T(8,128)S(1)} %maximum_bitcast_fusion), channel_id=1, source_target_pairs={{0,256},{4,260},{8,264},{12,268},{16,272},{20,276},{24,280},{28,28... | collective-permute-start | bytes 1572872 | tf_op jit(solution)/shard_map/ppermute | solution.py:31
  206.8 20.5 %collective-permute-done.11 = f32[2,4,128,128]{3,2,1,0:T(8,128)S(1)} collective-permute-done((f32[2,4,128,128]{3,2,1,0:T(8,128)S(1)}, f32[2,4,128,128]{3,2,1,0:T(8,128)S(1)}, u32[]{:S(2)}, u32[]{:S(2)}) %collective-permute-start.11) | collective-permute-done | bytes 524320 | tf_op jit(solution)/shard_map/ppermute | solution.py:31
  227.8 11.8 %collective-permute-start.12 = (f32[2,4,128,128]{3,2,1,0:T(8,128)S(1)}, f32[2,4,128,128]{3,2,1,0:T(8,128)S(1)}, u32[]{:S(2)}, u32[]{:S(2)}) collective-permute-start(f32[2,4,128,128]{3,2,1,0:T(8,128)S(1)} %fusion.70), channel_id=1, source_target_pairs={{0,128},{4,132},{8,136},{12,140},{16,144},{20,148},{24,152},{28,15... | collective-permute-start | bytes 1572872 | tf_op jit(solution)/shard_map/ppermute | solution.py:31
  241.3 16.4 %collective-permute-done.12 = f32[2,4,128,128]{3,2,1,0:T(8,128)S(1)} collective-permute-done((f32[2,4,128,128]{3,2,1,0:T(8,128)S(1)}, f32[2,4,128,128]{3,2,1,0:T(8,128)S(1)}, u32[]{:S(2)}, u32[]{:S(2)}) %collective-permute-start.12) | collective-permute-done | bytes 524320 | tf_op jit(solution)/shard_map/ppermute | solution.py:31
  261.8 12.2 %collective-permute-done.13 = f32[2,4,128,128]{3,2,1,0:T(8,128)S(1)} collective-permute-done((f32[2,4,128,128]{3,2,1,0:T(8,128)S(1)}, f32[2,4,128,128]{3,2,1,0:T(8,128)S(1)}, u32[]{:S(2)}, u32[]{:S(2)}) %collective-permute-start.13) | collective-permute-done | bytes 524320 | tf_op jit(solution)/shard_map/ppermute | solution.py:31
  274.5 2.1 collective-permute-start.14
  277.5 13.4 %collective-permute-done.14 = f32[2,4,128,128]{3,2,1,0:T(8,128)S(1)} collective-permute-done((f32[2,4,128,128]{3,2,1,0:T(8,128)S(1)}, f32[2,4,128,128]{3,2,1,0:T(8,128)S(1)}, u32[]{:S(2)}, u32[]{:S(2)}) %collective-permute-start.14) | collective-permute-done | bytes 524320 | tf_op jit(solution)/shard_map/ppermute | solution.py:31
  291.5 2.1 collective-permute-start.15
  294.3 11.3 %collective-permute-done.15 = f32[2,4,128,128]{3,2,1,0:T(8,128)S(1)} collective-permute-done((f32[2,4,128,128]{3,2,1,0:T(8,128)S(1)}, f32[2,4,128,128]{3,2,1,0:T(8,128)S(1)}, u32[]{:S(2)}, u32[]{:S(2)}) %collective-permute-start.15) | collective-permute-done | bytes 524320 | tf_op jit(solution)/shard_map/ppermute | solution.py:31
  311.3 3.4 collective-permute-start.10
  314.7 16.2 %collective-permute-done.16 = f32[2,4,128,128]{3,2,1,0:T(8,128)S(1)} collective-permute-done((f32[2,4,128,128]{3,2,1,0:T(8,128)}, f32[2,4,128,128]{3,2,1,0:T(8,128)S(1)}, u32[]{:S(2)}, u32[]{:S(2)}) %collective-permute-start.16) | collective-permute-done | bytes 524320 | tf_op jit(solution)/shard_map/ppermute | solution.py:31
  331.6 12.9 %collective-permute-start.17 = (f32[2,4,128,128]{3,2,1,0:T(8,128)S(1)}, f32[2,4,128,128]{3,2,1,0:T(8,128)S(1)}, u32[]{:S(2)}, u32[]{:S(2)}) collective-permute-start(f32[2,4,128,128]{3,2,1,0:T(8,128)S(1)} %fusion.75), channel_id=1, source_target_pairs={{0,4},{4,0},{8,12},{12,8},{16,20},{20,16},{24,28},{28,24},{32,36},... | collective-permute-start | bytes 1572872 | tf_op jit(solution)/shard_map/ppermute | solution.py:31
  345.8 10.7 %collective-permute-done.17 = f32[2,4,128,128]{3,2,1,0:T(8,128)S(1)} collective-permute-done((f32[2,4,128,128]{3,2,1,0:T(8,128)S(1)}, f32[2,4,128,128]{3,2,1,0:T(8,128)S(1)}, u32[]{:S(2)}, u32[]{:S(2)}) %collective-permute-start.17) | collective-permute-done | bytes 524320 | tf_op jit(solution)/shard_map/ppermute | solution.py:31
  356.6 6.7 %all-to-all-start.5 = ((bf16[4,64,512]{2,1,0:T(8,128)(2,1)}), bf16[4,64,512]{2,1,0:T(8,128)(2,1)S(1)}, u32[]{:S(2)}, u32[]{:S(2)}) async-start(bf16[4,64,512]{2,1,0:T(8,128)(2,1)} %all_to_all.120), calls=%async_computation.5 | async-start | bytes 524288 | tf_op jit(solution)/shard_map/all_to_all | solution.py:195
  364.9 11.2 %all-to-all-done.5 = bf16[4,64,512]{2,1,0:T(8,128)(2,1)S(1)} async-done(((bf16[4,64,512]{2,1,0:T(8,128)(2,1)}), bf16[4,64,512]{2,1,0:T(8,128)(2,1)S(1)}, u32[]{:S(2)}, u32[]{:S(2)}) %all-to-all-start.5) | async-done | bytes 262176 | tf_op jit(solution)/shard_map/all_to_all | solution.py:195
  376.1 3.4 all-to-all-start.6
  380.5 11.6 %all-to-all-done.6 = bf16[4,64,512]{2,1,0:T(8,128)(2,1)S(1)} async-done(((bf16[4,64,512]{2,1,0:T(8,128)(2,1)}), bf16[4,64,512]{2,1,0:T(8,128)(2,1)S(1)}, u32[]{:S(2)}, u32[]{:S(2)}) %all-to-all-start.6) | async-done | bytes 262176 | tf_op jit(solution)/shard_map/all_to_all | solution.py:196
  392.1 3.4 all-to-all-start.7
  398.6 9.6 %all-to-all-done.7 = bf16[4,64,512]{2,1,0:T(8,128)(2,1)S(1)} async-done(((bf16[4,64,512]{2,1,0:T(8,128)(2,1)}), bf16[4,64,512]{2,1,0:T(8,128)(2,1)S(1)}, u32[]{:S(2)}, u32[]{:S(2)}) %all-to-all-start.7) | async-done | bytes 262176 | tf_op jit(solution)/shard_map/all_to_all | solution.py:197
  (259 shorter events, 80.2 us)
Async XLA Ops:
  0.6 22.3 %copy-start.47 = (bf16[64,2048]{1,0:T(8,128)(2,1)S(1)}, bf16[64,2048]{1,0:T(8,128)(2,1)}, u32[]{:S(2)}) copy-start(bf16[64,2048]{1,0:T(8,128)(2,1)} %param.11) | copy-start | bytes 786436
  2.4 17.1 %all-to-all-start.1 = ((bf16[64,4,512]{2,0,1:T(8,128)(2,1)}), bf16[64,4,512]{2,0,1:T(8,128)(2,1)S(1)}, u32[]{:S(2)}, u32[]{:S(2)}) async-start(bf16[64,4,512]{2,0,1:T(8,128)(2,1)} %bitcast.494), calls=%async_computation.1 | async-start | bytes 524288 | tf_op jit(solution)/shard_map/all_to_all | solution.py:61
  19.5 16.1 %all-to-all-start = ((bf16[64,4,512]{2,0,1:T(8,128)(2,1)}), bf16[64,4,512]{2,0,1:T(8,128)(2,1)S(1)}, u32[]{:S(2)}, u32[]{:S(2)}) async-start(bf16[64,4,512]{2,0,1:T(8,128)(2,1)} %bitcast.495), calls=%async_computation | async-start | bytes 524288 | tf_op jit(solution)/shard_map/all_to_all | solution.py:60
  35.7 18.3 %all-to-all-start.4 = ((bf16[64,4,512]{2,0,1:T(8,128)(2,1)}), bf16[64,4,512]{2,0,1:T(8,128)(2,1)S(1)}, u32[]{:S(2)}, u32[]{:S(2)}) async-start(bf16[64,4,512]{2,0,1:T(8,128)(2,1)} %bitcast.492), calls=%async_computation.4 | async-start | bytes 524288 | tf_op jit(solution)/shard_map/all_to_all | solution.py:62
  39.3 13.5 %collective-permute-start.2 = (bf16[2,4,128,128]{3,2,1,0:T(8,128)(2,1)S(1)}, bf16[2,4,128,128]{3,2,1,0:T(8,128)(2,1)S(1)}, u32[]{:S(2)}, u32[]{:S(2)}) collective-permute-start(bf16[2,4,128,128]{3,2,1,0:T(8,128)(2,1)S(1)} %fusion.98), channel_id=1, source_target_pairs={{0,4},{4,0},{8,12},{12,8},{16,20},{20,16},{24,28},{28,24},{32,36},... | collective-permute-start | bytes 786440 | tf_op jit(solution)/shard_map/ppermute | solution.py:31
  43.9 30.6 %collective-permute-start.1 = (bf16[2,4,128,128]{3,1,2,0:T(4,128)(2,1)}, bf16[2,4,128,128]{3,1,2,0:T(4,128)(2,1)}, u32[]{:S(2)}, u32[]{:S(2)}) collective-permute-start(bf16[2,4,128,128]{3,1,2,0:T(4,128)(2,1)} %get-tuple-element.47), channel_id=1, source_target_pairs={{4,0},{8,4},{12,8},{16,12},{20,16},{24,20},{28,24},{32,28},{36,32}... | collective-permute-start | bytes 786440 | tf_op jit(solution)/shard_map/ppermute | solution.py:25
  49.0 25.5 %collective-permute-start = (bf16[2,4,128,128]{3,1,2,0:T(4,128)(2,1)S(1)}, bf16[2,4,128,128]{3,1,2,0:T(4,128)(2,1)}, u32[]{:S(2)}, u32[]{:S(2)}) collective-permute-start(bf16[2,4,128,128]{3,1,2,0:T(4,128)(2,1)S(1)} %get-tuple-element.46), channel_id=1, source_target_pairs={{0,4},{4,8},{8,12},{12,16},{16,20},{20,24},{24,28},{28,32},{32,36}... | collective-permute-start | bytes 786440 | tf_op jit(solution)/shard_map/ppermute | solution.py:22
  52.8 59.2 %copy-start.17 = (bf16[2,4,128,128]{3,2,1,0:T(8,128)(2,1)}, bf16[2,4,128,128]{3,2,1,0:T(8,128)(2,1)S(1)}, u32[]{:S(2)}) copy-start(bf16[2,4,128,128]{3,2,1,0:T(8,128)(2,1)S(1)} %collective-permute-done.2) | copy-start | bytes 786436
  54.0 20.5 %all-to-all-start.2 = ((bf16[64,4,512]{2,0,1:T(8,128)(2,1)}), bf16[64,4,512]{2,0,1:T(8,128)(2,1)S(1)}, u32[]{:S(2)}, u32[]{:S(2)}) async-start(bf16[64,4,512]{2,0,1:T(8,128)(2,1)} %bitcast.493), calls=%async_computation.2 | async-start | bytes 524288 | tf_op jit(solution)/shard_map/all_to_all | solution.py:59
  60.9 22.8 %collective-permute-start.3 = (bf16[2,4,128,128]{3,2,1,0:T(8,128)(2,1)S(1)}, bf16[2,4,128,128]{3,2,1,0:T(8,128)(2,1)S(1)}, u32[]{:S(2)}, u32[]{:S(2)}) collective-permute-start(bf16[2,4,128,128]{3,2,1,0:T(8,128)(2,1)S(1)} %fusion.91), channel_id=1, source_target_pairs={{0,8},{4,12},{8,0},{12,4},{16,24},{20,28},{24,16},{28,20},{32,40},... | collective-permute-start | bytes 786440 | tf_op jit(solution)/shard_map/ppermute | solution.py:31
  74.5 24.4 %copy-start.26 = (bf16[256,4,128]{2,0,1:T(8,128)(2,1)}, bf16[256,4,128]{2,0,1:T(8,128)(2,1)S(1)}, u32[]{:S(2)}) copy-start(bf16[256,4,128]{2,0,1:T(8,128)(2,1)S(1)} %copy.125) | copy-start | bytes 786436
  83.7 28.7 %copy-start.28 = (bf16[2,4,128,128]{3,2,1,0:T(8,128)(2,1)}, bf16[2,4,128,128]{3,2,1,0:T(8,128)(2,1)S(1)}, u32[]{:S(2)}) copy-start(bf16[2,4,128,128]{3,2,1,0:T(8,128)(2,1)S(1)} %collective-permute-done.3) | copy-start | bytes 786436
  84.8 9.8 %collective-permute-start.4 = (bf16[2,4,128,128]{3,2,1,0:T(8,128)(2,1)S(1)}, bf16[2,4,128,128]{3,2,1,0:T(8,128)(2,1)S(1)}, u32[]{:S(2)}, u32[]{:S(2)}) collective-permute-start(bf16[2,4,128,128]{3,2,1,0:T(8,128)(2,1)S(1)} %fusion.92), channel_id=1, source_target_pairs={{0,16},{4,20},{8,24},{12,28},{16,0},{20,4},{24,8},{28,12},{32,48},... | collective-permute-start | bytes 786440 | tf_op jit(solution)/shard_map/ppermute | solution.py:31
  88.0 100.1 %copy-start.1 = (bf16[2,4,2,384,128]{4,3,2,1,0:T(8,128)(2,1)}, bf16[2,4,2,384,128]{4,3,2,1,0:T(8,128)(2,1)S(1)}, u32[]{:S(2)}) copy-start(bf16[2,4,2,384,128]{4,3,2,1,0:T(8,128)(2,1)S(1)} %pad_maximum_fusion) | copy-start | bytes 4718596
  95.7 10.4 %collective-permute-start.5 = (bf16[2,4,128,128]{3,2,1,0:T(8,128)(2,1)S(1)}, bf16[2,4,128,128]{3,2,1,0:T(8,128)(2,1)S(1)}, u32[]{:S(2)}, u32[]{:S(2)}) collective-permute-start(bf16[2,4,128,128]{3,2,1,0:T(8,128)(2,1)S(1)} %fusion.93), channel_id=1, source_target_pairs={{0,32},{4,36},{8,40},{12,44},{16,48},{20,52},{24,56},{28,60},{32,0... | collective-permute-start | bytes 786440 | tf_op jit(solution)/shard_map/ppermute | solution.py:31
  107.8 9.0 %collective-permute-start.6 = (bf16[2,4,128,128]{3,2,1,0:T(8,128)(2,1)}, bf16[2,4,128,128]{3,2,1,0:T(8,128)(2,1)}, u32[]{:S(2)}, u32[]{:S(2)}) collective-permute-start(bf16[2,4,128,128]{3,2,1,0:T(8,128)(2,1)} %fusion.94), channel_id=1, source_target_pairs={{0,64},{4,68},{8,72},{12,76},{16,80},{20,84},{24,88},{28,92},{32,9... | collective-permute-start | bytes 786440 | tf_op jit(solution)/shard_map/ppermute | solution.py:31
  118.1 7.2 %copy-start.32 = (bf16[2,4,128,128]{3,2,1,0:T(8,128)(2,1)S(1)}, bf16[2,4,128,128]{3,2,1,0:T(8,128)(2,1)}, u32[]{:S(2)}) copy-start(bf16[2,4,128,128]{3,2,1,0:T(8,128)(2,1)} %copy-done.31) | copy-start | bytes 786436
  119.1 6.5 %copy-start.36 = (bf16[2,4,128,128]{3,2,1,0:T(8,128)(2,1)S(1)}, bf16[2,4,128,128]{3,2,1,0:T(8,128)(2,1)}, u32[]{:S(2)}) copy-start(bf16[2,4,128,128]{3,2,1,0:T(8,128)(2,1)} %copy-done.35) | copy-start | bytes 786436
  119.2 7.5 %copy-start.39 = (bf16[2,4,128,128]{3,2,1,0:T(8,128)(2,1)}, bf16[2,4,128,128]{3,2,1,0:T(8,128)(2,1)S(1)}, u32[]{:S(2)}) copy-start(bf16[2,4,128,128]{3,2,1,0:T(8,128)(2,1)S(1)} %fusion.95) | copy-start | bytes 786436
  119.2 15.3 %collective-permute-start.7 = (bf16[2,4,128,128]{3,2,1,0:T(8,128)(2,1)S(1)}, bf16[2,4,128,128]{3,2,1,0:T(8,128)(2,1)}, u32[]{:S(2)}, u32[]{:S(2)}) collective-permute-start(bf16[2,4,128,128]{3,2,1,0:T(8,128)(2,1)S(1)} %fusion.95), channel_id=1, source_target_pairs={{0,128},{4,132},{8,136},{12,140},{16,144},{20,148},{24,152},{28,15... | collective-permute-start | bytes 786440 | tf_op jit(solution)/shard_map/ppermute | solution.py:31
  137.7 21.9 %copy-start.3 = (f32[4,256,128]{1,2,0:T(8,128)S(1)}, f32[4,256,128]{1,2,0:T(8,128)}, u32[]{:S(2)}) copy-start(f32[4,256,128]{1,2,0:T(8,128)} %get-tuple-element.67) | copy-start | bytes 1572868
  137.7 19.9 %collective-permute-start.8 = (bf16[2,4,128,128]{3,2,1,0:T(8,128)(2,1)}, bf16[2,4,128,128]{3,2,1,0:T(8,128)(2,1)}, u32[]{:S(2)}, u32[]{:S(2)}) collective-permute-start(bf16[2,4,128,128]{3,2,1,0:T(8,128)(2,1)} %fusion.96), channel_id=1, source_target_pairs={{0,256},{4,260},{8,264},{12,268},{16,272},{20,276},{24,280},{28,28... | collective-permute-start | bytes 786440 | tf_op jit(solution)/shard_map/ppermute | solution.py:31
  182.0 174.6 %all-to-all-start.3 = ((bf16[4,64,512]{2,1,0:T(8,128)(2,1)}), bf16[4,64,512]{2,1,0:T(8,128)(2,1)}, u32[]{:S(2)}, u32[]{:S(2)}) async-start(bf16[4,64,512]{2,1,0:T(8,128)(2,1)} %all_to_all.113), calls=%async_computation.3 | async-start | bytes 524288 | tf_op jit(solution)/shard_map/all_to_all | solution.py:194
  189.9 87.0 %copy-start = (f32[2,4,4,128,128]{4,3,2,1,0:T(8,128)}, f32[2,4,4,128,128]{4,3,2,1,0:T(8,128)S(1)}, u32[]{:S(2)}) copy-start(f32[2,4,4,128,128]{4,3,2,1,0:T(8,128)S(1)} %fusion) | copy-start | bytes 6291460
  190.9 153.6 %collective-permute-start.9 = (f32[2,4,128,128]{3,2,1,0:T(8,128)}, f32[2,4,128,128]{3,2,1,0:T(8,128)}, u32[]{:S(2)}, u32[]{:S(2)}) collective-permute-start(f32[2,4,128,128]{3,2,1,0:T(8,128)} %get-tuple-element.38), channel_id=1, source_target_pairs={{0,4},{4,8},{8,12},{12,16},{16,20},{20,24},{24,28},{28,32},{32,36}... | collective-permute-start | bytes 1572872 | tf_op jit(solution)/shard_map/ppermute | solution.py:22
  198.0 5.1 %copy-start.13 = (f32[4,256,128]{1,2,0:T(8,128)S(1)}, f32[4,256,128]{1,2,0:T(8,128)}, u32[]{:S(2)}) copy-start(f32[4,256,128]{1,2,0:T(8,128)} %get-tuple-element.63) | copy-start | bytes 1572868
  198.3 7.4 %copy-start.10 = (f32[4,256,128]{1,2,0:T(8,128)S(1)}, f32[4,256,128]{1,2,0:T(8,128)}, u32[]{:S(2)}) copy-start(f32[4,256,128]{1,2,0:T(8,128)} %get-tuple-element.65) | copy-start | bytes 1572868
  198.3 29.0 %collective-permute-start.11 = (f32[2,4,128,128]{3,2,1,0:T(8,128)S(1)}, f32[2,4,128,128]{3,2,1,0:T(8,128)S(1)}, u32[]{:S(2)}, u32[]{:S(2)}) collective-permute-start(f32[2,4,128,128]{3,2,1,0:T(8,128)S(1)} %maximum_bitcast_fusion), channel_id=1, source_target_pairs={{0,256},{4,260},{8,264},{12,268},{16,272},{20,276},{24,280},{28,28... | collective-permute-start | bytes 1572872 | tf_op jit(solution)/shard_map/ppermute | solution.py:31
  206.8 20.9 %copy-start.45 = (f32[1,4,1,128,128]{4,3,1,0,2:T(8,128)S(1)}, f32[1,4,1,128,128]{4,3,1,0,2:T(8,128)}, u32[]{:S(2)}) copy-start(f32[1,4,1,128,128]{4,3,1,0,2:T(8,128)} %convolution_bitcast_fusion.12) | copy-start | bytes 786436
  227.7 13.3 %copy-start.4 = (f32[4,256,128]{1,2,0:T(8,128)S(1)}, f32[4,256,128]{1,2,0:T(8,128)}, u32[]{:S(2)}) copy-start(f32[4,256,128]{1,2,0:T(8,128)} %get-tuple-element.67) | copy-start | bytes 1572868
  227.7 13.3 %copy-start.38 = (bf16[2,4,128,128]{3,2,1,0:T(8,128)(2,1)S(1)}, bf16[2,4,128,128]{3,2,1,0:T(8,128)(2,1)}, u32[]{:S(2)}) copy-start(bf16[2,4,128,128]{3,2,1,0:T(8,128)(2,1)} %copy-done.35) | copy-start | bytes 786436
  227.8 29.8 %collective-permute-start.12 = (f32[2,4,128,128]{3,2,1,0:T(8,128)S(1)}, f32[2,4,128,128]{3,2,1,0:T(8,128)S(1)}, u32[]{:S(2)}, u32[]{:S(2)}) collective-permute-start(f32[2,4,128,128]{3,2,1,0:T(8,128)S(1)} %fusion.70), channel_id=1, source_target_pairs={{0,128},{4,132},{8,136},{12,140},{16,144},{20,148},{24,152},{28,15... | collective-permute-start | bytes 1572872 | tf_op jit(solution)/shard_map/ppermute | solution.py:31
  241.3 16.8 %copy-start.44 = (f32[1,4,1,128,128]{4,3,1,0,2:T(8,128)S(1)}, f32[1,4,1,128,128]{4,3,1,0,2:T(8,128)}, u32[]{:S(2)}) copy-start(f32[1,4,1,128,128]{4,3,1,0,2:T(8,128)} %convolution_bitcast_fusion.10) | copy-start | bytes 786436
  258.2 15.7 %collective-permute-start.13 = (f32[2,4,128,128]{3,2,1,0:T(8,128)S(1)}, f32[2,4,128,128]{3,2,1,0:T(8,128)S(1)}, u32[]{:S(2)}, u32[]{:S(2)}) collective-permute-start(f32[2,4,128,128]{3,2,1,0:T(8,128)S(1)} %fusion.71), channel_id=1, source_target_pairs={{0,64},{4,68},{8,72},{12,76},{16,80},{20,84},{24,88},{28,92},{32,9... | collective-permute-start | bytes 1572872 | tf_op jit(solution)/shard_map/ppermute | solution.py:31
  261.8 12.6 %copy-start.43 = (f32[1,4,1,128,128]{4,3,1,0,2:T(8,128)S(1)}, f32[1,4,1,128,128]{4,3,1,0,2:T(8,128)}, u32[]{:S(2)}) copy-start(f32[1,4,1,128,128]{4,3,1,0,2:T(8,128)} %convolution_bitcast_fusion.8) | copy-start | bytes 786436
  274.5 16.4 %collective-permute-start.14 = (f32[2,4,128,128]{3,2,1,0:T(8,128)S(1)}, f32[2,4,128,128]{3,2,1,0:T(8,128)S(1)}, u32[]{:S(2)}, u32[]{:S(2)}) collective-permute-start(f32[2,4,128,128]{3,2,1,0:T(8,128)S(1)} %fusion.72), channel_id=1, source_target_pairs={{0,32},{4,36},{8,40},{12,44},{16,48},{20,52},{24,56},{28,60},{32,0... | collective-permute-start | bytes 1572872 | tf_op jit(solution)/shard_map/ppermute | solution.py:31
  277.5 13.9 %copy-start.42 = (f32[1,4,1,128,128]{4,3,1,0,2:T(8,128)S(1)}, f32[1,4,1,128,128]{4,3,1,0,2:T(8,128)}, u32[]{:S(2)}) copy-start(f32[1,4,1,128,128]{4,3,1,0,2:T(8,128)} %convolution_bitcast_fusion.6) | copy-start | bytes 786436
  291.5 14.1 %collective-permute-start.15 = (f32[2,4,128,128]{3,2,1,0:T(8,128)S(1)}, f32[2,4,128,128]{3,2,1,0:T(8,128)S(1)}, u32[]{:S(2)}, u32[]{:S(2)}) collective-permute-start(f32[2,4,128,128]{3,2,1,0:T(8,128)S(1)} %fusion.73), channel_id=1, source_target_pairs={{0,16},{4,20},{8,24},{12,28},{16,0},{20,4},{24,8},{28,12},{32,48},... | collective-permute-start | bytes 1572872 | tf_op jit(solution)/shard_map/ppermute | solution.py:31
  294.3 11.8 %copy-start.41 = (f32[1,4,1,128,128]{4,3,1,0,2:T(8,128)S(1)}, f32[1,4,1,128,128]{4,3,1,0,2:T(8,128)}, u32[]{:S(2)}) copy-start(f32[1,4,1,128,128]{4,3,1,0,2:T(8,128)} %convolution_bitcast_fusion.4) | copy-start | bytes 786436
  307.0 24.0 %collective-permute-start.16 = (f32[2,4,128,128]{3,2,1,0:T(8,128)}, f32[2,4,128,128]{3,2,1,0:T(8,128)S(1)}, u32[]{:S(2)}, u32[]{:S(2)}) collective-permute-start(f32[2,4,128,128]{3,2,1,0:T(8,128)} %fusion.74), channel_id=1, source_target_pairs={{0,8},{4,12},{8,0},{12,4},{16,24},{20,28},{24,16},{28,20},{32,40},... | collective-permute-start | bytes 1572872 | tf_op jit(solution)/shard_map/ppermute | solution.py:31
  311.3 20.2 %copy-start.22 = (f32[1,4,1,128,128]{4,3,1,0,2:T(8,128)S(1)}, f32[1,4,1,128,128]{4,3,1,0,2:T(8,128)}, u32[]{:S(2)}) copy-start(f32[1,4,1,128,128]{4,3,1,0,2:T(8,128)} %convolution_bitcast_fusion.3) | copy-start | bytes 786436
  311.3 20.2 %copy-start.46 = (f32[1,4,1,128,128]{4,3,1,0,2:T(8,128)S(1)}, f32[1,4,1,128,128]{4,3,1,0,2:T(8,128)}, u32[]{:S(2)}) copy-start(f32[1,4,1,128,128]{4,3,1,0,2:T(8,128)} %convolution_bitcast_fusion.2) | copy-start | bytes 786436
  311.3 34.4 %collective-permute-start.10 = (f32[2,4,128,128]{3,2,1,0:T(8,128)S(1)}, f32[2,4,128,128]{3,2,1,0:T(8,128)S(1)}, u32[]{:S(2)}, u32[]{:S(2)}) collective-permute-start(f32[2,4,128,128]{3,2,1,0:T(8,128)S(1)} %copy-done.40), channel_id=1, source_target_pairs={{4,0},{8,4},{12,8},{16,12},{20,16},{24,20},{28,24},{32,28},{36,32}... | collective-permute-start | bytes 1572872 | tf_op jit(solution)/shard_map/ppermute | solution.py:25
  331.1 13.4 %slice-start = ((f32[2,4,4,128,128]{4,3,2,1,0:T(8,128)}), f32[2,4,2,128,128]{4,3,2,1,0:T(8,128)S(1)}, s32[]{:S(2)}) async-start(f32[2,4,4,128,128]{4,3,2,1,0:T(8,128)} %copy-done), calls=%async_computation.8 | async-start | bytes 2097152 | tf_op jit(solution)/shard_map/slice | solution.py:162
  331.6 24.9 %collective-permute-start.17 = (f32[2,4,128,128]{3,2,1,0:T(8,128)S(1)}, f32[2,4,128,128]{3,2,1,0:T(8,128)S(1)}, u32[]{:S(2)}, u32[]{:S(2)}) collective-permute-start(f32[2,4,128,128]{3,2,1,0:T(8,128)S(1)} %fusion.75), channel_id=1, source_target_pairs={{0,4},{4,0},{8,12},{12,8},{16,20},{20,16},{24,28},{28,24},{32,36},... | collective-permute-start | bytes 1572872 | tf_op jit(solution)/shard_map/ppermute | solution.py:31
  356.6 19.5 %all-to-all-start.5 = ((bf16[4,64,512]{2,1,0:T(8,128)(2,1)}), bf16[4,64,512]{2,1,0:T(8,128)(2,1)S(1)}, u32[]{:S(2)}, u32[]{:S(2)}) async-start(bf16[4,64,512]{2,1,0:T(8,128)(2,1)} %all_to_all.120), calls=%async_computation.5 | async-start | bytes 524288 | tf_op jit(solution)/shard_map/all_to_all | solution.py:195
  376.1 16.0 %all-to-all-start.6 = ((bf16[4,64,512]{2,1,0:T(8,128)(2,1)}), bf16[4,64,512]{2,1,0:T(8,128)(2,1)S(1)}, u32[]{:S(2)}, u32[]{:S(2)}) async-start(bf16[4,64,512]{2,1,0:T(8,128)(2,1)} %all_to_all.124), calls=%async_computation.6 | async-start | bytes 524288 | tf_op jit(solution)/shard_map/all_to_all | solution.py:196
  392.1 16.1 %all-to-all-start.7 = ((bf16[4,64,512]{2,1,0:T(8,128)(2,1)}), bf16[4,64,512]{2,1,0:T(8,128)(2,1)S(1)}, u32[]{:S(2)}, u32[]{:S(2)}) async-start(bf16[4,64,512]{2,1,0:T(8,128)(2,1)} %all_to_all.128), calls=%async_computation.7 | async-start | bytes 524288 | tf_op jit(solution)/shard_map/all_to_all | solution.py:197
  (30 other events, 57.1 us)
where the time goes:
time: 411 us; the launch traced here: 409 us
  waiting for transfers between devices  201 us (49%)
  starting transfers between devices  121 us (29%)
  matrix products  37.6 us (9%)
  local copies, waits for them, and re-layouts  30.6 us (7%)
  other arithmetic  16.2 us (4%)
    ppermute x14, waiting for transfers between devices, partner_2(): lax.ppermute(array, axis, [(i, i ^ 1 << stride) for i in range(lax.axis_s...  140 us
    ppermute x14, starting transfers between devices, partner_2(): lax.ppermute(array, axis, [(i, i ^ 1 << stride) for i in range(lax.axis_s...  68.7 us
    all_to_all x1, waiting for transfers between devices, on_device(): lax.all_to_all(keys, 'head', split_axis=1, concat_axis=0, tiled=True)  11.9 us
    all_to_all x1, waiting for transfers between devices, on_device(): lax.all_to_all(key_out, 'head', split_axis=0, concat_axis=1, tiled=True)  11.6 us
    all_to_all x1, waiting for transfers between devices, on_device(): lax.all_to_all(query_out, 'head', split_axis=0, concat_axis=1, tiled=True)  11.2 us
    dot_general x8, matrix products, on_device(): jnp.einsum('hgqd,hgkd->hgqk', grouped, keyset[0], preferred_element_type=...  10 us
    all_to_all x1, waiting for transfers between devices, on_device(): lax.all_to_all(value_out, 'head', split_axis=0, concat_axis=1, tiled=True)  9.6 us
    all_to_all x1, waiting for transfers between devices, on_device(): lax.all_to_all(queries, 'head', split_axis=1, concat_axis=0, tiled=True)  8.73 us
  transfers between devices with their start and end apart: 26, of which 20 were waited for; matrix products, arithmetic and copies ran while one was open for 11% of the time, Pallas kernels for 0%

commit v1 on v0

v1 whole, which is shorter than its diff:
```python
import functools
import math

import jax
import jax.numpy as jnp
from jax import lax
from jax.experimental import pallas as pl
from jax.experimental.pallas import tpu as pltpu
from jax.sharding import Mesh, PartitionSpec as P

DH = 128
BLOCK = 128
HEADS = 16
TOKENS_IN = 64
TOKENS = 1024
BLOCKS = TOKENS // BLOCK
RANKS = 32
CHUNK = 32
NEG_FILL = -1e30
SCALE = DH ** (-0.5)
SCALE_2 = SCALE * math.log2(math.e)
AXES = ("z", "x", "y_lo", "y_hi", "core")
HEAD_AXES = ("y_lo", "y_hi", "core")
SEQ_AXES = ("z", "x")
BF = jnp.bfloat16
F32 = jnp.float32
VMEM_LIMIT = 56 * 1024 * 1024

NN = (((1,), (0,)), ((), ()))
NT = (((1,), (1,)), ((), ()))


def dot(a, b, dims=NN):
    return lax.dot_general(a, b, dims, preferred_element_type=F32)


def eye(n):
    row = lax.broadcasted_iota(jnp.int32, (n, n), 0)
    col = lax.broadcasted_iota(jnp.int32, (n, n), 1)
    return jnp.where(row == col, 1.0, 0.0).astype(BF)


def kernel_call(body, outs, scratch=(), smem=False, n_in=1, flops=0, bytes_accessed=0):
    specs = [pl.BlockSpec(memory_space=pltpu.VMEM)] * n_in
    if smem:
        specs = [pl.BlockSpec(memory_space=pltpu.SMEM)] + specs
    return pl.pallas_call(
        body,
        out_shape=outs,
        in_specs=specs,
        out_specs=jax.tree.map(lambda _: pl.BlockSpec(memory_space=pltpu.VMEM), outs),
        scratch_shapes=list(scratch),
        compiler_params=pltpu.CompilerParams(vmem_limit_bytes=VMEM_LIMIT),
        cost_estimate=pl.CostEstimate(
            flops=flops, bytes_accessed=bytes_accessed, transcendentals=0
        ),
    )


def shape(*dims, dtype=BF):
    return jax.ShapeDtypeStruct(dims, dtype)


def pack_body(q_ref, k_ref, v_ref, d_ref, out_ref):
    for h in range(HEADS):
        for i, ref in enumerate((q_ref, k_ref, v_ref, d_ref)):
            out_ref[h, i] = ref[:, h * DH : (h + 1) * DH]


def unpack_body(in_ref, o_ref, dq_ref, dk_ref, dv_ref):
    for h in range(HEADS):
        for i, ref in enumerate((o_ref, dq_ref, dk_ref, dv_ref)):
            ref[:, h * DH : (h + 1) * DH] = in_ref[h, i]


def rows_of(ref, i, start, count):
    per = TOKENS_IN
    return ref[start // per : (start + count) // per, i].reshape(count, DH)


def pad_rows(x, rows):
    if x.shape[0] == rows:
        return x
    return jnp.concatenate([x, jnp.zeros((rows - x.shape[0], DH), x.dtype)], axis=0)


def pyramid_body(place_ref, in_ref, pyr_ref, zx_ref, p1_ref, p2_ref, p3_ref, p4_ref, buf):
    s = place_ref[0]
    odd = lax.rem(s, 2)
    for i in range(2):
        buf[...] = in_ref[:, 1 + i].reshape(TOKENS, DH).astype(F32)
        count = TOKENS
        levels = {}
        for level in range(1, 8):
            count //= 2
            mean = (
                (buf[pl.ds(0, count, stride=2), :] + buf[pl.ds(1, count, stride=2), :]) * 0.5
            ).astype(BF)
            mean = mean.astype(F32)
            levels[level] = mean
            if level < 7:
                buf[0:count, :] = mean
        pyr_ref[i, 0:512] = levels[1].astype(BF)
        pyr_ref[i, 512:768] = levels[2].astype(BF)
        p1_ref[i, 0:128] = levels[3].astype(BF)
        p2_ref[i] = levels[4].astype(BF)
        p3_ref[i, 0:64] = levels[4].astype(BF)
        for bit, level in ((2, 5), (3, 6), (4, 7)):
            rows = pad_rows(levels[level], CHUNK).astype(BF)
            for d in range(1 << bit, 2 << bit):
                zx_ref[jnp.bitwise_xor(s, d), i] = rows
        for d in range(4):
            zx_ref[jnp.bitwise_xor(s, d), i] = jnp.zeros((CHUNK, DH), BF)
        first = in_ref[0:2, 1 + i].reshape(BLOCK, DH)
        last = in_ref[14:16, 1 + i].reshape(BLOCK, DH)
        near = jnp.where(odd == 1, first, last)
        other = jnp.where(odd == 1, last, first)
        p1_ref[i, 128:256] = near
        p3_ref[i, 64:192] = other
        p4_ref[i] = other


def attend_body(
    place_ref,
    in_ref,
    pyr_ref,
    zx_ref,
    p1_ref,
    p2_ref,
    p3_ref,
    p4_ref,
    out_ref,
    dkv_ref,
    bzx_ref,
    b1_ref,
    b2_ref,
    b3_ref,
    b4_ref,
    win,
    rem,
    win_t,
    pyr_t,
    rem_t,
    dwin,
    dpyr,
    drem,
    spread,
):
    s = place_ref[0]
    x = lax.rem(s, 4)
    odd = lax.rem(s, 2) == 1
    inner = jnp.logical_or(x == 1, x == 2)
    ident = eye(DH)
    for i in range(2):
        near = p1_ref[i, 128:256]
        other = jnp.where(inner, p3_ref[i, 64:192], p4_ref[i])
        win[i, 0:128] = jnp.where(odd, near, other)
        win[i, 128:1152] = in_ref[:, 1 + i].reshape(TOKENS, DH)
        win[i, 1152:1280] = jnp.where(odd, other, near)
        rem[i, 0:128] = p1_ref[i, 0:128]
        rem[i, 128:192] = p2_ref[i]
        rem[i, 192:256] = p3_ref[i, 0:64]
        for bit, base in ((2, 256), (3, 384), (4, 512)):
            rows = BLOCK >> bit
            parts = []
            for d in range(1 << bit, 2 << bit):
                parts.append(zx_ref[jnp.bitwise_xor(s, d), i].astype(F32)[0:rows])
            rem[i, base : base + 128] = jnp.concatenate(parts, axis=0).astype(BF)
        win_t[i] = dot(ident, win[i], NT).astype(BF)
        pyr_t[i] = dot(ident, pyr_ref[i], NT).astype(BF)
        rem_t[i] = dot(ident, rem[i], NT).astype(BF)
    dwin[...] = jnp.zeros_like(dwin)
    drem[...] = jnp.zeros_like(drem)
    dpyr[...] = jnp.zeros_like(dpyr)
    left_bias = jnp.where(s == 0, NEG_FILL, 0.0).astype(F32)
    right_bias = jnp.where(s == RANKS - 1, NEG_FILL, 0.0).astype(F32)
    row = lax.broadcasted_iota(jnp.int32, (640, 1), 0)
    rem_shift = (row // BLOCK + 3).astype(F32)
    ident2 = eye(2 * BLOCK)
    for p in range(BLOCKS // 2):
        q = in_ref[4 * p : 4 * p + 4, 0].reshape(2 * BLOCK, DH)
        dy = in_ref[4 * p : 4 * p + 4, 3].reshape(2 * BLOCK, DH)
        one = (p ^ 1) * BLOCK
        two = 512 + ((p // 2) ^ 1) * BLOCK
        wide = (
            (pyr_ref, pyr_t, dpyr, one, BLOCK, 1.0),
            (pyr_ref, pyr_t, dpyr, two, BLOCK, 2.0),
            (rem, rem_t, drem, 0, 640, rem_shift),
        )
        score = []
        for ref, _, _, start, count, shift in wide:
            score.append(dot(ref[0, start : start + count], q, NT) * SCALE_2 + shift)
        fine = []
        for j in range(2):
            b = 2 * p + j
            f = dot(win[0, b * BLOCK : (b + 3) * BLOCK], q[j * BLOCK : (j + 1) * BLOCK], NT)
            f = f * SCALE_2
            if b == 0:
                f = jnp.concatenate([f[0:BLOCK] + left_bias, f[BLOCK:]], axis=0)
            if b == BLOCKS - 1:
                f = jnp.concatenate([f[: 2 * BLOCK], f[2 * BLOCK :] + right_bias], axis=0)
            fine.append(f)
        top = jnp.concatenate([jnp.max(f, axis=0, keepdims=True) for f in fine], axis=1)
        for item in score:
            top = jnp.maximum(top, jnp.max(item, axis=0, keepdims=True))
        score = [jnp.exp2(item - top) for item in score]
        fine = [
            jnp.exp2(f - top[:, j * BLOCK : (j + 1) * BLOCK]) for j, f in enumerate(fine)
        ]
        total = jnp.concatenate([jnp.sum(f, axis=0, keepdims=True) for f in fine], axis=1)
        for item in score:
            total = total + jnp.sum(item, axis=0, keepdims=True)
        inverse = 1.0 / total
        score = [item * inverse for item in score]
        fine = [f * inverse[:, j * BLOCK : (j + 1) * BLOCK] for j, f in enumerate(fine)]
        light = [item.astype(BF) for item in score]
        fine_light = [f.astype(BF) for f in fine]
        out_t = jnp.concatenate(
            [
                dot(win_t[1, :, (2 * p + j) * BLOCK : (2 * p + j + 3) * BLOCK], fine_light[j])
                for j in range(2)
            ],
            axis=1,
        )
        for (_, ref_t, _, start, count, _), item in zip(wide, light):
            out_t = out_t + dot(ref_t[1, :, start : start + count], item)
        dy_t = dot(ident, dy, NT)
        delta = jnp.sum(out_t * dy_t, axis=0, keepdims=True)
        out_ref[4 * p : 4 * p + 4, 0] = (
            dot(ident2, out_t.astype(BF), NT).astype(BF).reshape(4, TOKENS_IN, DH)
        )
        dq_t = []
        for j in range(2):
            b = 2 * p + j
            lanes = slice(j * BLOCK, (j + 1) * BLOCK)
            rows = slice(b * BLOCK, (b + 3) * BLOCK)
            pushed = dot(win[1, rows], dy[lanes], NT)
            grad = (fine[j] * ((pushed - delta[:, lanes]) * SCALE)).astype(BF)
            dq_t.append(dot(win_t[0, :, rows], grad))
            dwin[0, rows] += dot(grad, q[lanes])
            dwin[1, rows] += dot(fine_light[j], dy[lanes])
        dq_t = jnp.concatenate(dq_t, axis=1)
        for (ref, ref_t, dref, start, count, _), item, item_light in zip(wide, score, light):
            rows = slice(start, start + count)
            pushed = dot(ref[1, rows], dy, NT)
            grad = (item * ((pushed - delta) * SCALE)).astype(BF)
            dq_t = dq_t + dot(ref_t[0, :, rows], grad)
            dref[0, rows] += dot(grad, q)
            dref[1, rows] += dot(item_light, dy)
        out_ref[4 * p : 4 * p + 4, 1] = (
            dot(ident2, dq_t.astype(BF), NT).astype(BF).reshape(4, TOKENS_IN, DH)
        )
    for i in range(2):
        half = dpyr[i, 512:768] * 0.5
        spread[pl.ds(0, 256, stride=2), :] = half
        spread[pl.ds(1, 256, stride=2), :] = half
        half = (dpyr[i, 0:512] + spread[0:512, :]) * 0.5
        spread[pl.ds(0, 512, stride=2), :] = half
        spread[pl.ds(1, 512, stride=2), :] = half
        dkv_ref[i] = dwin[i, 128:1152] + spread[...]
        left = dwin[i, 0:128].astype(BF)
        right = dwin[i, 1152:1280].astype(BF)
        near = jnp.where(odd, left, right)
        other = jnp.where(odd, right, left)
        b1_ref[i, 0:128] = drem[i, 0:128].astype(BF)
        b1_ref[i, 128:256] = near
        b2_ref[i] = drem[i, 128:192].astype(BF)
        b3_ref[i, 0:64] = drem[i, 192:256].astype(BF)
        b3_ref[i, 64:192] = other
        b4_ref[i] = other
        for d in range(4):
            bzx_ref[jnp.bitwise_xor(s, d), i] = jnp.zeros((CHUNK, DH), BF)
        for bit, base in ((2, 256), (3, 384), (4, 512)):
            rows = BLOCK >> bit
            for d in range(1 << bit, 2 << bit):
                start = base + (d - (1 << bit)) * rows
                bzx_ref[jnp.bitwise_xor(s, d), i] = pad_rows(
                    drem[i, start : start + rows], CHUNK
                ).astype(BF)


def finish_body(
    place_ref, out_ref_in, dkv_ref, zx_ref, p1_ref, p2_ref, p3_ref, p4_ref, out_ref, spread
):
    s = place_ref[0]
    x = lax.rem(s, 4)
    odd = lax.rem(s, 2) == 1
    inner = jnp.logical_or(x == 1, x == 2)
    out_ref[:, 0:2] = out_ref_in[...]
    for i in range(2):
        direct = {
            3: p1_ref[i, 0:128].astype(F32),
            4: p2_ref[i].astype(F32) + p3_ref[i, 0:64].astype(F32),
        }
        for bit in (2, 3, 4):
            total = None
            for d in range(1 << bit, 2 << bit):
                item = zx_ref[jnp.bitwise_xor(s, d), i].astype(F32)
                total = item if total is None else total + item
            direct[bit + 3] = total[0 : BLOCK >> bit]
        carry = direct[7]
        for level in range(6, 2, -1):
            count = carry.shape[0]
            half = carry * 0.5
            spread[pl.ds(0, count, stride=2), :] = half
            spread[pl.ds(1, count, stride=2), :] = half
            carry = direct[level] + spread[0 : 2 * count, :]
        for _ in range(3):
            count = carry.shape[0]
            half = carry * 0.5
            spread[pl.ds(0, count, stride=2), :] = half
            spread[pl.ds(1, count, stride=2), :] = half
            carry = spread[0 : 2 * count, :]
        near = p1_ref[i, 128:256].astype(F32)
        other = jnp.where(inner, p3_ref[i, 64:192], p4_ref[i]).astype(F32)
        first = jnp.where(odd, near, other)
        last = jnp.where(odd, other, near)
        grad = dkv_ref[i] + carry
        grad = jnp.concatenate(
            [grad[0:128] + first, grad[128 : TOKENS - 128], grad[TOKENS - 128 :] + last], axis=0
        )
        out_ref[:, 2 + i] = grad.astype(BF).reshape(HEADS, TOKENS_IN, DH)


def swap(array, axes):
    return lax.all_to_all(array, axes, split_axis=0, concat_axis=0, tiled=True)


def cross_pairs(z_count, x_count):
    pairs = []
    for z in range(z_count - 1):
        low, high = z * x_count + x_count - 1, (z + 1) * x_count
        pairs += [(low, high), (high, low)]
    return pairs


def exchange(zx, p1, p2, p3, p4):
    flip = lambda array, mask: lax.ppermute(array, "x", [(i, i ^ mask) for i in range(4)])
    p1 = flip(p1, 1)
    p3 = flip(p3, 3)
    p2 = flip(p2, 2)
    p4 = lax.ppermute(p4, SEQ_AXES, cross_pairs(8, 4))
    return swap(zx, SEQ_AXES), p1, p2, p3, p4


def on_device(queries, keys, values, cotangent):
    place = (lax.axis_index("z") * 4 + lax.axis_index("x")).reshape(1).astype(jnp.int32)
    mb = 1 << 20
    messages = [
        shape(RANKS, 2, CHUNK, DH),
        shape(2, 256, DH),
        shape(2, 64, DH),
        shape(2, 192, DH),
        shape(2, 128, DH),
    ]
    packed = kernel_call(
        pack_body, shape(HEADS, 4, TOKENS_IN, DH), n_in=4, bytes_accessed=2 * mb
    )(queries, keys, values, cotangent)
    mine = swap(packed, HEAD_AXES)
    pyr, *sent = kernel_call(
        pyramid_body,
        [shape(2, 768, DH)] + messages,
        scratch=[pltpu.VMEM((TOKENS, DH), F32)],
        smem=True,
        n_in=1,
        bytes_accessed=2 * mb,
    )(place, mine)
    got = exchange(*sent)
    out, dkv, *back = kernel_call(
        attend_body,
        [shape(HEADS, 2, TOKENS_IN, DH), shape(2, TOKENS, DH, dtype=F32)] + messages,
        scratch=[
            pltpu.VMEM((2, 1280, DH), BF),
            pltpu.VMEM((2, 640, DH), BF),
            pltpu.VMEM((2, DH, 1280), BF),
            pltpu.VMEM((2, DH, 768), BF),
            pltpu.VMEM((2, DH, 640), BF),
            pltpu.VMEM((2, 1280, DH), F32),
            pltpu.VMEM((2, 768, DH), F32),
            pltpu.VMEM((2, 640, DH), F32),
            pltpu.VMEM((TOKENS, DH), F32),
        ],
        smem=True,
        n_in=7,
        flops=2 * 10**9,
        bytes_accessed=5 * mb,
    )(place, mine, pyr, *got)
    returned = exchange(*back)
    packed = kernel_call(
        finish_body,
        shape(HEADS, 4, TOKENS_IN, DH),
        scratch=[pltpu.VMEM((TOKENS, DH), F32)],
        smem=True,
        n_in=7,
        bytes_accessed=3 * mb,
    )(place, out, dkv, *returned)
    results = swap(packed, HEAD_AXES)
    flat = shape(TOKENS_IN, HEADS * DH)
    return tuple(
        kernel_call(unpack_body, [flat] * 4, n_in=1, bytes_accessed=2 * mb)(results)
    )


def solution(mesh):
    fine = Mesh(mesh.devices.reshape(8, 4, 4, 2, 2), AXES)
    placed = P(AXES, None)
    return jax.shard_map(
        on_device,
        mesh=fine,
        in_specs=(placed,) * 4,
        out_specs=(placed,) * 4,
        check_vma=False,
    )
```

time: 411 us -> 152 us (0.37)
  waiting for transfers between devices: 201 us -> 38.4 us
  starting transfers between devices: 121 us -> 54.8 us
  matrix products: 37.6 us -> 0 us
  blocking collectives: 0 us -> 32.4 us
  local copies, waits for them, and re-layouts: 30.6 us -> 2.69 us
  Pallas kernels: 0 us -> 21.7 us
  other arithmetic: 16.2 us -> 0 us
    ppermute x18 -> x8, waiting for transfers between devices: 140 us -> 10.8 us  [the longest x6 10.8 us: exchange(): lax.ppermute(array, 'x', [(i, i ^ mask) for i in range(4)])]
    ppermute x18 -> x8, starting transfers between devices: 82.8 us -> 25.3 us  [the longest x6 15.5 us: exchange(): lax.ppermute(array, 'x', [(i, i ^ mask) for i in range(4)])]
    dot_general x48 -> x0, matrix products: 37.6 us -> none  [the longest x8 10 us: on_device(): jnp.einsum('hgqd,hgkd->hgqk', grouped, keyset[0], preferred_element_type=...]
    all_to_all x8 -> x3, waiting for transfers between devices: 61.4 us -> 27.6 us  [swap(): return lax.all_to_all(array, axes, split_axis=0, concat_axis=0, tiled=True)]
    all_to_all x0 -> x1, blocking collectives: none -> 32.4 us  [swap(): return lax.all_to_all(array, axes, split_axis=0, concat_axis=0, tiled=True)]
    pallas_call x0 -> x5, Pallas kernels: none -> 21.7 us  [the longest x1 11.4 us: on_device(): kernel_call(attend_body, [shape(HEADS, 2, TOKENS_IN, DH), shape(2, TOKENS...]
    all_to_all x12 -> x0, local copies, waits for them, and re-layouts: 11.9 us -> none  [the longest x2 2.48 us: on_device(): lax.all_to_all(output_rows, 'head', split_axis=0, concat_axis=1, tiled=True)]
    all_to_all x8 -> x3, starting transfers between devices: 38.3 us -> 29.5 us  [swap(): return lax.all_to_all(array, axes, split_axis=0, concat_axis=0, tiled=True)]
  transfers between devices with their start and end apart: 26 -> 11, of which waited for: 20 -> 3; matrix products, arithmetic and copies ran while one was open for 11% -> 0% of each run, Pallas kernels for 0% -> 0%
where the time goes in v1:
time: 152 us; the launch traced here: 151 us
  starting transfers between devices  54.8 us (36%)
  waiting for transfers between devices  38.4 us (25%)
  blocking collectives  32.4 us (21%)
  Pallas kernels  21.7 us (14%)
  local copies, waits for them, and re-layouts  2.69 us (2%)
    all_to_all x1, blocking collectives, swap(): return lax.all_to_all(array, axes, split_axis=0, concat_axis=0, tiled=True)  32.4 us
    all_to_all x3, starting transfers between devices, swap(): return lax.all_to_all(array, axes, split_axis=0, concat_axis=0, tiled=True)  29.5 us
    all_to_all x3, waiting for transfers between devices, swap(): return lax.all_to_all(array, axes, split_axis=0, concat_axis=0, tiled=True)  27.6 us
    ppermute x6, starting transfers between devices, exchange(): lax.ppermute(array, 'x', [(i, i ^ mask) for i in range(4)])  15.5 us
    pallas_call x1, Pallas kernels, on_device(): kernel_call(attend_body, [shape(HEADS, 2, TOKENS_IN, DH), shape(2, TOKENS...  11.4 us
    ppermute x6, waiting for transfers between devices, exchange(): lax.ppermute(array, 'x', [(i, i ^ mask) for i in range(4)])  10.8 us
    ppermute x2, starting transfers between devices, exchange(): p4 = lax.ppermute(p4, SEQ_AXES, cross_pairs(8, 4))  9.76 us
  transfers between devices with their start and end apart: 11, of which 3 were waited for; matrix products, arithmetic and copies ran while one was open for 0% of the time, Pallas kernels for 0%

profile of v1, /device:TPU:6, one launch (start us, length us, event | category | flops | bytes accessed | tf_op | source)
XLA Modules:
  0.0 150.9 jit_solution(8529708987100470709)
XLA Ops:
  0.6 2.4 %shard_map.75 = bf16[16,4,64,128]{3,2,1,0:T(8,128)(2,1)} custom-call(bf16[64,2048]{1,0:T(8,128)(2,1)} %q_ref.1, bf16[64,2048]{1,0:T(8,128)(2,1)} %k_ref.1, bf16[64,2048]{1,0:T(8,128)(2,1)} %v_ref.1, bf16[64,2048]{1,0:T(8,128)(2,1)} %d_ref.1), custom_call_target="tpu_custom_call" | custom-call | bytes 2097152 | tf_op jit(solution)/shard_map/pallas_call | solution.py:356
  3.0 7.2 %all-to-all-start = ((bf16[16,4,64,128]{3,2,1,0:T(8,128)(2,1)}), bf16[16,4,64,128]{3,2,1,0:T(8,128)(2,1)S(1)}, u32[]{:S(2)}, u32[]{:S(2)}) async-start(bf16[16,4,64,128]{3,2,1,0:T(8,128)(2,1)} %shard_map.75), calls=%async_computation | async-start | bytes 2097152 | tf_op jit(solution)/shard_map/all_to_all | solution.py:326
  10.2 27.6 %all-to-all-done.in_ref = bf16[16,4,64,128]{3,2,1,0:T(8,128)(2,1)S(1)} async-done(((bf16[16,4,64,128]{3,2,1,0:T(8,128)(2,1)}), bf16[16,4,64,128]{3,2,1,0:T(8,128)(2,1)S(1)}, u32[]{:S(2)}, u32[]{:S(2)}) %all-to-all-start) | async-done | bytes 1048608 | tf_op jit(solution)/shard_map/all_to_all | solution.py:326
  37.8 1.0 copy-done
  38.8 2.5 %shard_map.76 = (bf16[2,768,128]{2,1,0:T(8,128)(2,1)}, bf16[32,2,32,128]{3,2,1,0:T(8,128)(2,1)}, bf16[2,256,128]{2,1,0:T(8,128)(2,1)}, bf16[2,64,128]{2,1,0:T(8,...) custom-call(s32[1]{0:T(128)} %bitcast.place_ref, bf16[16,4,64,128]{3,2,1,0:T(8,128)(2,1)} %copy-done), custom_call_target="tpu_custom_call" | custom-call | bytes 2097152 | tf_op jit(solution)/shard_map/pallas_call | solution.py:360
  41.3 0.0 copy-start.15
  41.3 0.0 copy-start.18
  41.3 13.6 %all-to-all-start.1 = ((bf16[32,2,32,128]{3,2,1,0:T(8,128)(2,1)}), bf16[32,2,32,128]{3,2,1,0:T(8,128)(2,1)S(1)}, u32[]{:S(2)}, u32[]{:S(2)}) async-start(bf16[32,2,32,128]{3,2,1,0:T(8,128)(2,1)} %get-tuple-element.18), calls=%async_computation.1 | async-start | bytes 1048576 | tf_op jit(solution)/shard_map/all_to_all | solution.py:326
  54.9 0.0 copy-done.9
  54.9 2.8 %collective-permute-start = (bf16[2,256,128]{2,1,0:T(8,128)(2,1)S(1)}, bf16[2,256,128]{2,1,0:T(8,128)(2,1)S(1)}, u32[]{:S(2)}, u32[]{:S(2)}) collective-permute-start(bf16[2,256,128]{2,1,0:T(8,128)(2,1)S(1)} %copy-done.9), channel_id=1, source_target_pairs={{0,16},{16,0},{32,48},{48,32},{1,17},{17,1},{33,49},{49,33},{2,18}... | collective-permute-start | bytes 393224 | tf_op jit(solution)/shard_map/ppermute | solution.py:338
  57.7 3.1 %collective-permute-start.2 = (bf16[2,192,128]{2,1,0:T(8,128)(2,1)S(1)}, bf16[2,192,128]{2,1,0:T(8,128)(2,1)S(1)}, u32[]{:S(2)}, u32[]{:S(2)}) collective-permute-start(bf16[2,192,128]{2,1,0:T(8,128)(2,1)S(1)} %copy-done.12), channel_id=1, source_target_pairs={{0,48},{16,32},{32,16},{48,0},{1,49},{17,33},{33,17},{49,1},{2,50}... | collective-permute-start | bytes 294920 | tf_op jit(solution)/shard_map/ppermute | solution.py:338
  60.8 4.9 %collective-permute-start.3 = (bf16[2,128,128]{2,1,0:T(8,128)(2,1)S(1)}, bf16[2,128,128]{2,1,0:T(8,128)(2,1)S(1)}, u32[]{:S(2)}, u32[]{:S(2)}) collective-permute-start(bf16[2,128,128]{2,1,0:T(8,128)(2,1)S(1)} %copy-done.15), channel_id=1, source_target_pairs={{48,64},{64,48},{112,128},{128,112},{176,192},{192,176},{240,256},... | collective-permute-start | bytes 196616 | tf_op jit(solution)/shard_map/ppermute | solution.py:342
  65.7 1.9 %collective-permute-start.1 = (bf16[2,64,128]{2,1,0:T(8,128)(2,1)S(1)}, bf16[2,64,128]{2,1,0:T(8,128)(2,1)S(1)}, u32[]{:S(2)}, u32[]{:S(2)}) collective-permute-start(bf16[2,64,128]{2,1,0:T(8,128)(2,1)S(1)} %copy-done.18), channel_id=1, source_target_pairs={{0,32},{16,48},{32,0},{48,16},{1,33},{17,49},{33,1},{49,17},{2,34}... | collective-permute-start | bytes 98312 | tf_op jit(solution)/shard_map/ppermute | solution.py:338
  67.6 5.4 %collective-permute-done.1.p2_ref = bf16[2,64,128]{2,1,0:T(8,128)(2,1)S(1)} collective-permute-done((bf16[2,64,128]{2,1,0:T(8,128)(2,1)S(1)}, bf16[2,64,128]{2,1,0:T(8,128)(2,1)S(1)}, u32[]{:S(2)}, u32[]{:S(2)}) %collective-permute-start.1) | collective-permute-done | bytes 32800 | tf_op jit(solution)/shard_map/ppermute | solution.py:338
  73.0 0.0 collective-permute-done.3.p4_ref
  73.0 0.0 collective-permute-done.2.p3_ref
  73.0 0.0 copy-start.10
  73.0 0.0 collective-permute-done.p1_ref
  73.0 0.0 copy-start.7
  73.0 0.0 all-to-all-done.1.zx_ref
  73.1 0.0 copy-start.2
  73.1 0.5 copy-done.16
  73.6 0.1 copy-done.13
  73.7 0.0 copy-done.10
  73.7 0.0 copy-done.7
  73.7 0.2 copy-done.2
  73.9 11.4 %shard_map.77 = (bf16[16,2,64,128]{3,2,1,0:T(8,128)(2,1)}, f32[2,1024,128]{2,1,0:T(8,128)}, bf16[32,2,32,128]{3,2,1,0:T(8,128)(2,1)}, bf16[2,256,128]{2,1,0:T(8,...) custom-call(s32[1]{0:T(128)} %bitcast.place_ref, ...), custom_call_target="tpu_custom_call" | custom-call | flops 2000000000 | bytes 5242880 | tf_op jit(solution)/shard_map/pallas_call | solution.py:369
  85.3 0.0 copy-start.11
  85.3 8.7 %all-to-all-start.2 = ((bf16[32,2,32,128]{3,2,1,0:T(8,128)(2,1)}), bf16[32,2,32,128]{3,2,1,0:T(8,128)(2,1)S(1)}, u32[]{:S(2)}, u32[]{:S(2)}) async-start(bf16[32,2,32,128]{3,2,1,0:T(8,128)(2,1)} %get-tuple-element.25), calls=%async_computation.2 | async-start | bytes 1048576 | tf_op jit(solution)/shard_map/all_to_all | solution.py:326
  94.1 2.8 %collective-permute-start.4 = (bf16[2,256,128]{2,1,0:T(8,128)(2,1)S(1)}, bf16[2,256,128]{2,1,0:T(8,128)(2,1)S(1)}, u32[]{:S(2)}, u32[]{:S(2)}) collective-permute-start(bf16[2,256,128]{2,1,0:T(8,128)(2,1)S(1)} %copy-done.8), channel_id=1, source_target_pairs={{0,16},{16,0},{32,48},{48,32},{1,17},{17,1},{33,49},{49,33},{2,18}... | collective-permute-start | bytes 393224 | tf_op jit(solution)/shard_map/ppermute | solution.py:338
  96.9 3.1 %collective-permute-start.6 = (bf16[2,192,128]{2,1,0:T(8,128)(2,1)S(1)}, bf16[2,192,128]{2,1,0:T(8,128)(2,1)S(1)}, u32[]{:S(2)}, u32[]{:S(2)}) collective-permute-start(bf16[2,192,128]{2,1,0:T(8,128)(2,1)S(1)} %copy-done.11), channel_id=1, source_target_pairs={{0,48},{16,32},{32,16},{48,0},{1,49},{17,33},{33,17},{49,1},{2,50}... | collective-permute-start | bytes 294920 | tf_op jit(solution)/shard_map/ppermute | solution.py:338
  100.0 4.9 %collective-permute-start.7 = (bf16[2,128,128]{2,1,0:T(8,128)(2,1)S(1)}, bf16[2,128,128]{2,1,0:T(8,128)(2,1)S(1)}, u32[]{:S(2)}, u32[]{:S(2)}) collective-permute-start(bf16[2,128,128]{2,1,0:T(8,128)(2,1)S(1)} %copy-done.14), channel_id=1, source_target_pairs={{48,64},{64,48},{112,128},{128,112},{176,192},{192,176},{240,256},... | collective-permute-start | bytes 196616 | tf_op jit(solution)/shard_map/ppermute | solution.py:342
  104.9 1.9 %collective-permute-start.5 = (bf16[2,64,128]{2,1,0:T(8,128)(2,1)S(1)}, bf16[2,64,128]{2,1,0:T(8,128)(2,1)S(1)}, u32[]{:S(2)}, u32[]{:S(2)}) collective-permute-start(bf16[2,64,128]{2,1,0:T(8,128)(2,1)S(1)} %copy-done.17), channel_id=1, source_target_pairs={{0,32},{16,48},{32,0},{48,16},{1,33},{17,49},{33,1},{49,17},{2,34}... | collective-permute-start | bytes 98312 | tf_op jit(solution)/shard_map/ppermute | solution.py:338
  106.8 5.4 %collective-permute-done.5.p2_ref = bf16[2,64,128]{2,1,0:T(8,128)(2,1)S(1)} collective-permute-done((bf16[2,64,128]{2,1,0:T(8,128)(2,1)S(1)}, bf16[2,64,128]{2,1,0:T(8,128)(2,1)S(1)}, u32[]{:S(2)}, u32[]{:S(2)}) %collective-permute-start.5) | collective-permute-done | bytes 32800 | tf_op jit(solution)/shard_map/ppermute | solution.py:338
  112.2 0.0 collective-permute-done.7.p4_ref
  112.2 0.0 collective-permute-done.6.p3_ref
  112.2 0.0 copy-start.4
  112.2 0.0 collective-permute-done.4.p1_ref
  112.2 0.0 copy-start.3
  112.2 0.0 all-to-all-done.2.zx_ref
  112.2 0.5 copy-done.6
  112.8 0.0 copy-done.5
  112.8 0.0 copy-done.4
  112.9 0.0 copy-done.3
  112.9 0.2 copy-done.1
  113.1 2.9 %shard_map.78 = bf16[16,4,64,128]{3,2,1,0:T(8,128)(2,1)} custom-call(s32[1]{0:T(128)} %bitcast.place_ref, bf16[16,2,64,128]{3,2,1,0:T(8,128)(2,1)} %get-tuple-element.23.out_ref_in, f32[2,1024,128]{2,1,0:T(8,128)} %get-tuple-element.24.dkv_ref, bf16[32,2,32,128]{3,2,1,0:T(8,128)(2,1)} %copy-done.1, bf16[2,256,128]{2,1,0:T(8,128)(2,1)} %copy-done.3, ...), custom_call_target="tpu_custom_call" | custom-call | bytes 3145728 | tf_op jit(solution)/shard_map/pallas_call | solution.py:389
  116.0 32.4 %all_to_all.20.in_ref = bf16[16,4,64,128]{3,2,1,0:T(8,128)(2,1)} all-to-all(bf16[16,4,64,128]{3,2,1,0:T(8,128)(2,1)} %shard_map.78), channel_id=1, replica_groups=mesh['z'=8,'x'=4,'y_lo'=4,'y_hi'=2,'core'=2] {'y_lo','y_hi','core'}, dimensions={0} | all-to-all | bytes 2097152 | tf_op jit(solution)/shard_map/all_to_all | solution.py:326
  148.4 2.4 %shard_map.79 = (bf16[64,2048]{1,0:T(8,128)(2,1)}, bf16[64,2048]{1,0:T(8,128)(2,1)}, bf16[64,2048]{1,0:T(8,128)(2,1)}, bf16[64,2048]{1,0:T(8,128)(2,1)}) custom-call(bf16[16,4,64,128]{3,2,1,0:T(8,128)(2,1)} %all_to_all.20.in_ref), custom_call_target="tpu_custom_call" | custom-call | bytes 2097152 | tf_op jit(solution)/shard_map/pallas_call | solution.py:400
  (18 shorter events, 0.0 us)
Async XLA Ops:
  3.0 34.8 %all-to-all-start = ((bf16[16,4,64,128]{3,2,1,0:T(8,128)(2,1)}), bf16[16,4,64,128]{3,2,1,0:T(8,128)(2,1)S(1)}, u32[]{:S(2)}, u32[]{:S(2)}) async-start(bf16[16,4,64,128]{3,2,1,0:T(8,128)(2,1)} %shard_map.75), calls=%async_computation | async-start | bytes 2097152 | tf_op jit(solution)/shard_map/all_to_all | solution.py:326
  37.8 1.0 copy-start
  41.3 13.6 %copy-start.9 = (bf16[2,256,128]{2,1,0:T(8,128)(2,1)S(1)}, bf16[2,256,128]{2,1,0:T(8,128)(2,1)}, u32[]{:S(2)}) copy-start(bf16[2,256,128]{2,1,0:T(8,128)(2,1)} %get-tuple-element.19) | copy-start | bytes 393220
  41.3 16.4 %copy-start.12 = (bf16[2,192,128]{2,1,0:T(8,128)(2,1)S(1)}, bf16[2,192,128]{2,1,0:T(8,128)(2,1)}, u32[]{:S(2)}) copy-start(bf16[2,192,128]{2,1,0:T(8,128)(2,1)} %get-tuple-element.21) | copy-start | bytes 294916
  41.3 19.5 %copy-start.15 = (bf16[2,128,128]{2,1,0:T(8,128)(2,1)S(1)}, bf16[2,128,128]{2,1,0:T(8,128)(2,1)}, u32[]{:S(2)}) copy-start(bf16[2,128,128]{2,1,0:T(8,128)(2,1)} %get-tuple-element.22) | copy-start | bytes 196612
  41.3 24.3 %copy-start.18 = (bf16[2,64,128]{2,1,0:T(8,128)(2,1)S(1)}, bf16[2,64,128]{2,1,0:T(8,128)(2,1)}, u32[]{:S(2)}) copy-start(bf16[2,64,128]{2,1,0:T(8,128)(2,1)} %get-tuple-element.20) | copy-start | bytes 98308
  41.3 31.7 %all-to-all-start.1 = ((bf16[32,2,32,128]{3,2,1,0:T(8,128)(2,1)}), bf16[32,2,32,128]{3,2,1,0:T(8,128)(2,1)S(1)}, u32[]{:S(2)}, u32[]{:S(2)}) async-start(bf16[32,2,32,128]{3,2,1,0:T(8,128)(2,1)} %get-tuple-element.18), calls=%async_computation.1 | async-start | bytes 1048576 | tf_op jit(solution)/shard_map/all_to_all | solution.py:326
  54.9 18.1 %collective-permute-start = (bf16[2,256,128]{2,1,0:T(8,128)(2,1)S(1)}, bf16[2,256,128]{2,1,0:T(8,128)(2,1)S(1)}, u32[]{:S(2)}, u32[]{:S(2)}) collective-permute-start(bf16[2,256,128]{2,1,0:T(8,128)(2,1)S(1)} %copy-done.9), channel_id=1, source_target_pairs={{0,16},{16,0},{32,48},{48,32},{1,17},{17,1},{33,49},{49,33},{2,18}... | collective-permute-start | bytes 393224 | tf_op jit(solution)/shard_map/ppermute | solution.py:338
  57.7 15.3 %collective-permute-start.2 = (bf16[2,192,128]{2,1,0:T(8,128)(2,1)S(1)}, bf16[2,192,128]{2,1,0:T(8,128)(2,1)S(1)}, u32[]{:S(2)}, u32[]{:S(2)}) collective-permute-start(bf16[2,192,128]{2,1,0:T(8,128)(2,1)S(1)} %copy-done.12), channel_id=1, source_target_pairs={{0,48},{16,32},{32,16},{48,0},{1,49},{17,33},{33,17},{49,1},{2,50}... | collective-permute-start | bytes 294920 | tf_op jit(solution)/shard_map/ppermute | solution.py:338
  60.8 12.2 %collective-permute-start.3 = (bf16[2,128,128]{2,1,0:T(8,128)(2,1)S(1)}, bf16[2,128,128]{2,1,0:T(8,128)(2,1)S(1)}, u32[]{:S(2)}, u32[]{:S(2)}) collective-permute-start(bf16[2,128,128]{2,1,0:T(8,128)(2,1)S(1)} %copy-done.15), channel_id=1, source_target_pairs={{48,64},{64,48},{112,128},{128,112},{176,192},{192,176},{240,256},... | collective-permute-start | bytes 196616 | tf_op jit(solution)/shard_map/ppermute | solution.py:342
  65.7 7.3 %collective-permute-start.1 = (bf16[2,64,128]{2,1,0:T(8,128)(2,1)S(1)}, bf16[2,64,128]{2,1,0:T(8,128)(2,1)S(1)}, u32[]{:S(2)}, u32[]{:S(2)}) collective-permute-start(bf16[2,64,128]{2,1,0:T(8,128)(2,1)S(1)} %copy-done.18), channel_id=1, source_target_pairs={{0,32},{16,48},{32,0},{48,16},{1,33},{17,49},{33,1},{49,17},{2,34}... | collective-permute-start | bytes 98312 | tf_op jit(solution)/shard_map/ppermute | solution.py:338
  73.0 0.6 copy-start.16
  73.0 0.7 copy-start.13
  73.0 0.7 copy-start.10
  73.0 0.7 copy-start.7
  73.1 0.8 copy-start.2
  85.3 8.8 %copy-start.8 = (bf16[2,256,128]{2,1,0:T(8,128)(2,1)S(1)}, bf16[2,256,128]{2,1,0:T(8,128)(2,1)}, u32[]{:S(2)}) copy-start(bf16[2,256,128]{2,1,0:T(8,128)(2,1)} %get-tuple-element.26) | copy-start | bytes 393220
  85.3 11.6 %copy-start.11 = (bf16[2,192,128]{2,1,0:T(8,128)(2,1)S(1)}, bf16[2,192,128]{2,1,0:T(8,128)(2,1)}, u32[]{:S(2)}) copy-start(bf16[2,192,128]{2,1,0:T(8,128)(2,1)} %get-tuple-element.28) | copy-start | bytes 294916
  85.3 14.6 %copy-start.14 = (bf16[2,128,128]{2,1,0:T(8,128)(2,1)S(1)}, bf16[2,128,128]{2,1,0:T(8,128)(2,1)}, u32[]{:S(2)}) copy-start(bf16[2,128,128]{2,1,0:T(8,128)(2,1)} %get-tuple-element.29) | copy-start | bytes 196612
  85.3 19.5 %copy-start.17 = (bf16[2,64,128]{2,1,0:T(8,128)(2,1)S(1)}, bf16[2,64,128]{2,1,0:T(8,128)(2,1)}, u32[]{:S(2)}) copy-start(bf16[2,64,128]{2,1,0:T(8,128)(2,1)} %get-tuple-element.27) | copy-start | bytes 98308
  85.3 26.9 %all-to-all-start.2 = ((bf16[32,2,32,128]{3,2,1,0:T(8,128)(2,1)}), bf16[32,2,32,128]{3,2,1,0:T(8,128)(2,1)S(1)}, u32[]{:S(2)}, u32[]{:S(2)}) async-start(bf16[32,2,32,128]{3,2,1,0:T(8,128)(2,1)} %get-tuple-element.25), calls=%async_computation.2 | async-start | bytes 1048576 | tf_op jit(solution)/shard_map/all_to_all | solution.py:326
  94.1 18.1 %collective-permute-start.4 = (bf16[2,256,128]{2,1,0:T(8,128)(2,1)S(1)}, bf16[2,256,128]{2,1,0:T(8,128)(2,1)S(1)}, u32[]{:S(2)}, u32[]{:S(2)}) collective-permute-start(bf16[2,256,128]{2,1,0:T(8,128)(2,1)S(1)} %copy-done.8), channel_id=1, source_target_pairs={{0,16},{16,0},{32,48},{48,32},{1,17},{17,1},{33,49},{49,33},{2,18}... | collective-permute-start | bytes 393224 | tf_op jit(solution)/shard_map/ppermute | solution.py:338
  96.9 15.3 %collective-permute-start.6 = (bf16[2,192,128]{2,1,0:T(8,128)(2,1)S(1)}, bf16[2,192,128]{2,1,0:T(8,128)(2,1)S(1)}, u32[]{:S(2)}, u32[]{:S(2)}) collective-permute-start(bf16[2,192,128]{2,1,0:T(8,128)(2,1)S(1)} %copy-done.11), channel_id=1, source_target_pairs={{0,48},{16,32},{32,16},{48,0},{1,49},{17,33},{33,17},{49,1},{2,50}... | collective-permute-start | bytes 294920 | tf_op jit(solution)/shard_map/ppermute | solution.py:338
  100.0 12.2 %collective-permute-start.7 = (bf16[2,128,128]{2,1,0:T(8,128)(2,1)S(1)}, bf16[2,128,128]{2,1,0:T(8,128)(2,1)S(1)}, u32[]{:S(2)}, u32[]{:S(2)}) collective-permute-start(bf16[2,128,128]{2,1,0:T(8,128)(2,1)S(1)} %copy-done.14), channel_id=1, source_target_pairs={{48,64},{64,48},{112,128},{128,112},{176,192},{192,176},{240,256},... | collective-permute-start | bytes 196616 | tf_op jit(solution)/shard_map/ppermute | solution.py:342
  104.9 7.3 %collective-permute-start.5 = (bf16[2,64,128]{2,1,0:T(8,128)(2,1)S(1)}, bf16[2,64,128]{2,1,0:T(8,128)(2,1)S(1)}, u32[]{:S(2)}, u32[]{:S(2)}) collective-permute-start(bf16[2,64,128]{2,1,0:T(8,128)(2,1)S(1)} %copy-done.17), channel_id=1, source_target_pairs={{0,32},{16,48},{32,0},{48,16},{1,33},{17,49},{33,1},{49,17},{2,34}... | collective-permute-start | bytes 98312 | tf_op jit(solution)/shard_map/ppermute | solution.py:338
  112.2 0.6 copy-start.6
  112.2 0.6 copy-start.5
  112.2 0.7 copy-start.4
  112.2 0.7 copy-start.3
  112.2 0.8 copy-start.1

commit v2 on v1

v2 whole, which is shorter than its diff:
```python
import functools
import math

import jax
import jax.numpy as jnp
from jax import lax
from jax.experimental import pallas as pl
from jax.experimental.pallas import tpu as pltpu
from jax.sharding import Mesh, PartitionSpec as P

DH = 128
BLOCK = 128
HEADS = 16
TOKENS_IN = 64
TOKENS = 1024
BLOCKS = TOKENS // BLOCK
RANKS = 32
CHUNK = 32
NEG_FILL = -1e30
SCALE = DH ** (-0.5)
SCALE_2 = SCALE * math.log2(math.e)
AXES = ("z", "x", "y_lo", "y_hi", "core")
HEAD_AXES = ("y_lo", "y_hi", "core")
SEQ_AXES = ("z", "x")
BF = jnp.bfloat16
F32 = jnp.float32
SMALL, MIDDLE, LARGE = 4, 16, 56
VMEM, HBM, SMEM = pltpu.VMEM, pltpu.HBM, pltpu.SMEM

NN = (((1,), (0,)), ((), ()))
NT = (((1,), (1,)), ((), ()))


def dot(a, b, dims=NN):
    return lax.dot_general(a, b, dims, preferred_element_type=F32)


def eye(n):
    row = lax.broadcasted_iota(jnp.int32, (n, n), 0)
    col = lax.broadcasted_iota(jnp.int32, (n, n), 1)
    return jnp.where(row == col, 1.0, 0.0).astype(BF)


def kernel_call(body, ins, outs, scratch=(), flops=0, bytes_accessed=0, mib=SMALL):
    space = lambda kind: pl.BlockSpec(memory_space=kind)
    many = len(outs) > 1
    return pl.pallas_call(
        body,
        out_shape=[item for _, item in outs] if many else outs[0][1],
        in_specs=[space(kind) for kind in ins],
        out_specs=[space(kind) for kind, _ in outs] if many else space(outs[0][0]),
        scratch_shapes=list(scratch),
        compiler_params=pltpu.CompilerParams(vmem_limit_bytes=mib << 20),
        cost_estimate=pl.CostEstimate(
            flops=flops, bytes_accessed=bytes_accessed, transcendentals=0
        ),
    )


def shape(*dims, dtype=BF):
    return jax.ShapeDtypeStruct(dims, dtype)


def pack_body(q_ref, k_ref, v_ref, d_ref, out_ref, held, packed, in_sem, out_sem):
    refs = (q_ref, k_ref, v_ref, d_ref)
    loads = [pltpu.make_async_copy(ref, held.at[i], in_sem.at[i]) for i, ref in enumerate(refs)]
    stores = [
        pltpu.make_async_copy(packed.at[i], out_ref.at[:, i], out_sem.at[i]) for i in range(4)
    ]
    for load in loads:
        load.start()
    for i in range(4):
        loads[i].wait()
        for h in range(HEADS):
            packed[i, h] = held[i, :, h * DH : (h + 1) * DH]
        stores[i].start()
    for store in stores:
        store.wait()


def unpack_body(in_ref, o_ref, dq_ref, dk_ref, dv_ref):
    for h in range(HEADS):
        for i, ref in enumerate((o_ref, dq_ref, dk_ref, dv_ref)):
            ref[:, h * DH : (h + 1) * DH] = in_ref[h, i]


def rows_of(ref, i, start, count):
    per = TOKENS_IN
    return ref[start // per : (start + count) // per, i].reshape(count, DH)


def pad_rows(x, rows):
    if x.shape[0] == rows:
        return x
    return jnp.concatenate([x, jnp.zeros((rows - x.shape[0], DH), x.dtype)], axis=0)


def pyramid_body(place_ref, in_ref, pyr_ref, zx_ref, p1_ref, p2_ref, p3_ref, p4_ref, buf):
    s = place_ref[0]
    odd = lax.rem(s, 2)
    for i in range(2):
        buf[...] = in_ref[:, 1 + i].reshape(TOKENS, DH).astype(F32)
        count = TOKENS
        levels = {}
        for level in range(1, 8):
            count //= 2
            mean = (
                (buf[pl.ds(0, count, stride=2), :] + buf[pl.ds(1, count, stride=2), :]) * 0.5
            ).astype(BF)
            mean = mean.astype(F32)
            levels[level] = mean
            if level < 7:
                buf[0:count, :] = mean
        pyr_ref[i, 0:512] = levels[1].astype(BF)
        pyr_ref[i, 512:768] = levels[2].astype(BF)
        p1_ref[i, 0:128] = levels[3].astype(BF)
        p2_ref[i] = levels[4].astype(BF)
        p3_ref[i] = levels[4].astype(BF)
        for bit, level in ((2, 5), (3, 6), (4, 7)):
            rows = pad_rows(levels[level], CHUNK).astype(BF)
            for d in range(1 << bit, 2 << bit):
                zx_ref[jnp.bitwise_xor(s, d), i] = rows
        for d in range(4):
            zx_ref[jnp.bitwise_xor(s, d), i] = jnp.zeros((CHUNK, DH), BF)
        first = in_ref[0:2, 1 + i].reshape(BLOCK, DH)
        last = in_ref[14:16, 1 + i].reshape(BLOCK, DH)
        near = jnp.where(odd == 1, first, last)
        other = jnp.where(odd == 1, last, first)
        p1_ref[i, 128:256] = near
        p4_ref[i] = other


def merge_body(place_ref, zx_ref, p1_ref, p2_ref, p3_ref, p4_ref, rem_ref, edge_ref):
    s = place_ref[0]
    odd = lax.rem(s, 2) == 1
    for i in range(2):
        near = p1_ref[i, 128:256]
        other = p4_ref[i]
        edge_ref[i, 0:128] = jnp.where(odd, near, other)
        edge_ref[i, 128:256] = jnp.where(odd, other, near)
        rem_ref[i, 0:128] = p1_ref[i, 0:128]
        rem_ref[i, 128:192] = p2_ref[i]
        rem_ref[i, 192:256] = p3_ref[i]
        for bit, base in ((2, 256), (3, 384), (4, 512)):
            rows = BLOCK >> bit
            parts = []
            for d in range(1 << bit, 2 << bit):
                parts.append(zx_ref[jnp.bitwise_xor(s, d), i].astype(F32)[0:rows])
            rem_ref[i, base : base + 128] = jnp.concatenate(parts, axis=0).astype(BF)


def part_body(place_ref, drem_ref, dedge_ref, bzx_ref, b1_ref, b2_ref, b3_ref, b4_ref):
    s = place_ref[0]
    odd = lax.rem(s, 2) == 1
    for i in range(2):
        left = dedge_ref[i, 0:128]
        right = dedge_ref[i, 128:256]
        b1_ref[i, 0:128] = drem_ref[i, 0:128]
        b1_ref[i, 128:256] = jnp.where(odd, left, right)
        b2_ref[i] = drem_ref[i, 128:192]
        b3_ref[i] = drem_ref[i, 192:256]
        b4_ref[i] = jnp.where(odd, right, left)
        for d in range(4):
            bzx_ref[jnp.bitwise_xor(s, d), i] = jnp.zeros((CHUNK, DH), BF)
        for bit, base in ((2, 256), (3, 384), (4, 512)):
            rows = BLOCK >> bit
            block = drem_ref[i, base : base + 128].astype(F32)
            for d in range(1 << bit, 2 << bit):
                start = (d - (1 << bit)) * rows
                bzx_ref[jnp.bitwise_xor(s, d), i] = pad_rows(
                    block[start : start + rows], CHUNK
                ).astype(BF)


def attend_body(
    place_ref,
    in_ref,
    pyr_ref,
    rem,
    edge_ref,
    out_ref,
    dkv_ref,
    drem_ref,
    dedge_ref,
    win,
    win_t,
    pyr_t,
    rem_t,
    dwin,
    dpyr,
    drem,
    spread,
):
    s = place_ref[0]
    ident = eye(DH)
    for i in range(2):
        win[i, 0:128] = edge_ref[i, 0:128]
        win[i, 128:1152] = in_ref[:, 1 + i].reshape(TOKENS, DH)
        win[i, 1152:1280] = edge_ref[i, 128:256]
        win_t[i] = dot(ident, win[i], NT).astype(BF)
        pyr_t[i] = dot(ident, pyr_ref[i], NT).astype(BF)
        rem_t[i] = dot(ident, rem[i], NT).astype(BF)
    dwin[...] = jnp.zeros_like(dwin)
    drem[...] = jnp.zeros_like(drem)
    dpyr[...] = jnp.zeros_like(dpyr)
    second = lax.broadcasted_iota(jnp.int32, (1, 2 * BLOCK), 1) >= BLOCK
    ident2 = eye(2 * BLOCK)

    def load(p):
        q = in_ref[4 * p : 4 * p + 4, 0].reshape(2 * BLOCK, DH)
        dy = in_ref[4 * p : 4 * p + 4, 3].reshape(2 * BLOCK, DH)
        one = (p ^ 1) * BLOCK
        two = 512 + ((p // 2) ^ 1) * BLOCK
        groups = (
            (win, win_t, dwin, 2 * p * BLOCK, (0, 0, 0, 0)),
            (pyr_ref, pyr_t, dpyr, one, (1,)),
            (pyr_ref, pyr_t, dpyr, two, (2,)),
            (rem, rem_t, drem, 0, (3, 4, 5, 6, 7)),
        )
        raws = [dot(ref[0, start : start + BLOCK * len(shifts)], q, NT) for ref, _, _, start, shifts in groups]
        pushes = [dot(ref[1, start : start + BLOCK * len(shifts)], dy, NT) for ref, _, _, start, shifts in groups] if True else None
        dy_t = dot(ident, dy, NT)
        return q, dy, groups, raws, pushes, dy_t
    def soft(p, state):
        q, dy, groups, raws, pushes, dy_t = state
        first_gap = jnp.where(second, NEG_FILL, 0.0).astype(F32)
        last_gap = jnp.where(second, 0.0, NEG_FILL).astype(F32)
        if p == 0:
            first_gap = jnp.where(s == 0, NEG_FILL, first_gap)
        if p == BLOCKS // 2 - 1:
            last_gap = jnp.where(s == RANKS - 1, NEG_FILL, last_gap)
        score = []
        top = None
        for raw, (ref, _, _, start, shifts) in zip(raws, groups):
            blocks = [raw[n * BLOCK : (n + 1) * BLOCK] for n in range(len(shifts))]
            if len(shifts) == 4:
                blocks[0] = blocks[0] + first_gap
                blocks[3] = blocks[3] + last_gap
            for item, shift in zip(blocks, shifts):
                peak = jnp.max(item, axis=0, keepdims=True) * SCALE_2 + float(shift)
                top = peak if top is None else jnp.maximum(top, peak)
            score.append(blocks)
        total = jnp.zeros((1, 2 * BLOCK), F32)
        for blocks, group in zip(score, groups):
            for n, shift in enumerate(group[4]):
                blocks[n] = jnp.exp2(blocks[n] * SCALE_2 + (float(shift) - top))
                total = total + jnp.sum(blocks[n], axis=0, keepdims=True)
        inverse = 1.0 / total
        score = [jnp.concatenate(blocks, axis=0) * inverse for blocks in score]
        light = [item.astype(BF) for item in score]
        return score, light
    def tail(p, state, weights):
        q, dy, groups, raws, pushes, dy_t = state
        score, light = weights
        out_t = jnp.zeros((DH, 2 * BLOCK), F32)
        for (_, ref_t, _, start, shifts), item in zip(groups, light):
            out_t = out_t + dot(ref_t[1, :, start : start + BLOCK * len(shifts)], item)
        delta = jnp.sum(out_t * dy_t, axis=0, keepdims=True)
        out_ref[4 * p : 4 * p + 4, 0] = (
            dot(ident2, out_t.astype(BF), NT).astype(BF).reshape(4, TOKENS_IN, DH)
        )
        dq_t = jnp.zeros((DH, 2 * BLOCK), F32)
        for n, ((ref, ref_t, dref, start, shifts), item, item_light) in enumerate(zip(groups, score, light)):
            rows = slice(start, start + BLOCK * len(shifts))
            pushed = pushes[n] if True else dot(ref[1, rows], dy, NT)
            grad = (item * (pushed - delta)).astype(BF)
            dq_t = dq_t + dot(ref_t[0, :, rows], grad)
            dref[0, rows] += dot(grad, q)
            dref[1, rows] += dot(item_light, dy)
        out_ref[4 * p : 4 * p + 4, 1] = (
            dot(ident2, (dq_t * SCALE).astype(BF), NT).astype(BF).reshape(4, TOKENS_IN, DH)
        )
    state = load(0)
    weights = soft(0, state)
    for p in range(4):
        following = load(p + 1) if p < 3 else None
        after = soft(p + 1, following) if p < 3 else None
        tail(p, state, weights)
        state, weights = following, after
    dwin[0] = dwin[0] * SCALE
    dpyr[0] = dpyr[0] * SCALE
    drem[0] = drem[0] * SCALE
    for i in range(2):
        drem_ref[i] = drem[i].astype(BF)
        dedge_ref[i, 0:128] = dwin[i, 0:128].astype(BF)
        dedge_ref[i, 128:256] = dwin[i, 1152:1280].astype(BF)
        half = dpyr[i, 512:768] * 0.5
        spread[pl.ds(0, 256, stride=2), :] = half
        spread[pl.ds(1, 256, stride=2), :] = half
        half = (dpyr[i, 0:512] + spread[0:512, :]) * 0.5
        spread[pl.ds(0, 512, stride=2), :] = half
        spread[pl.ds(1, 512, stride=2), :] = half
        dkv_ref[i] = dwin[i, 128:1152] + spread[...]


def finish_body(
    place_ref, out_ref_in, dkv_ref, zx_ref, p1_ref, p2_ref, p3_ref, p4_ref, out_ref, spread
):
    s = place_ref[0]
    odd = lax.rem(s, 2) == 1
    out_ref[:, 0:2] = out_ref_in[...]
    for i in range(2):
        direct = {
            3: p1_ref[i, 0:128].astype(F32),
            4: p2_ref[i].astype(F32) + p3_ref[i].astype(F32),
        }
        for bit in (2, 3, 4):
            total = None
            for d in range(1 << bit, 2 << bit):
                item = zx_ref[jnp.bitwise_xor(s, d), i].astype(F32)
                total = item if total is None else total + item
            direct[bit + 3] = total[0 : BLOCK >> bit]
        carry = direct[7]
        for level in range(6, 2, -1):
            count = carry.shape[0]
            half = carry * 0.5
            spread[pl.ds(0, count, stride=2), :] = half
            spread[pl.ds(1, count, stride=2), :] = half
            carry = direct[level] + spread[0 : 2 * count, :]
        for _ in range(3):
            count = carry.shape[0]
            half = carry * 0.5
            spread[pl.ds(0, count, stride=2), :] = half
            spread[pl.ds(1, count, stride=2), :] = half
            carry = spread[0 : 2 * count, :]
        near = p1_ref[i, 128:256].astype(F32)
        other = p4_ref[i].astype(F32)
        first = jnp.where(odd, near, other)
        last = jnp.where(odd, other, near)
        grad = dkv_ref[i] + carry
        grad = jnp.concatenate(
            [grad[0:128] + first, grad[128 : TOKENS - 128], grad[TOKENS - 128 :] + last], axis=0
        )
        out_ref[:, 2 + i] = grad.astype(BF).reshape(HEADS, TOKENS_IN, DH)


def swap(array, axes):
    return lax.all_to_all(array, axes, split_axis=0, concat_axis=0, tiled=True)


def odd_pairs(count):
    pairs = []
    for low in range(1, count - 1, 2):
        pairs += [(low, low + 1), (low + 1, low)]
    return pairs


def exchange(zx, p1, p2, p3, p4):
    flip = lambda array, mask: lax.ppermute(array, "x", [(i, i ^ mask) for i in range(4)])
    p1 = flip(p1, 1)
    p2 = flip(p2, 2)
    p3 = flip(p3, 3)
    p4 = lax.ppermute(p4, SEQ_AXES, odd_pairs(RANKS))
    return swap(zx, SEQ_AXES), p1, p2, p3, p4


def on_device(queries, keys, values, cotangent):
    place = (lax.axis_index("z") * 4 + lax.axis_index("x")).reshape(1).astype(jnp.int32)
    mb = 1 << 20
    messages = [
        shape(RANKS, 2, CHUNK, DH),
        shape(2, 256, DH),
        shape(2, 64, DH),
        shape(2, 64, DH),
        shape(2, 128, DH),
    ]
    split = shape(HEADS, 4, TOKENS_IN, DH)
    packed = kernel_call(
        pack_body,
        [HBM] * 4,
        [(HBM, split)],
        scratch=[
            VMEM((4, TOKENS_IN, HEADS * DH), BF),
            VMEM((4, HEADS, TOKENS_IN, DH), BF),
            pltpu.SemaphoreType.DMA((4,)),
            pltpu.SemaphoreType.DMA((4,)),
        ],
        mib=LARGE,
        bytes_accessed=2 * mb,
    )(queries, keys, values, cotangent)
    mine = swap(packed, HEAD_AXES)
    pyr, *sent = kernel_call(
        pyramid_body,
        [SMEM, VMEM],
        [(VMEM, shape(2, 768, DH))] + [(VMEM, item) for item in messages],
        scratch=[VMEM((TOKENS, DH), F32)],
        bytes_accessed=2 * mb,
    )(place, mine)
    got = exchange(*sent)
    rows = [shape(2, 640, DH), shape(2, 256, DH)]
    far = kernel_call(merge_body, [SMEM] + [VMEM] * 5, [(VMEM, item) for item in rows])(
        place, *got
    )
    out, dkv, *grads = kernel_call(
        attend_body,
        [SMEM] + [VMEM] * 4,
        [
            (VMEM, shape(HEADS, 2, TOKENS_IN, DH)),
            (VMEM, shape(2, TOKENS, DH, dtype=F32)),
        ]
        + [(VMEM, item) for item in rows],
        scratch=[
            VMEM((2, 1280, DH), BF),
            VMEM((2, DH, 1280), BF),
            VMEM((2, DH, 768), BF),
            VMEM((2, DH, 640), BF),
            VMEM((2, 1280, DH), F32),
            VMEM((2, 768, DH), F32),
            VMEM((2, 640, DH), F32),
            VMEM((TOKENS, DH), F32),
        ],
        mib=MIDDLE,
        flops=2 * 10**9,
        bytes_accessed=5 * mb,
    )(place, mine, pyr, *far)
    back = kernel_call(part_body, [SMEM] + [VMEM] * 2, [(VMEM, item) for item in messages])(
        place, *grads
    )
    returned = exchange(*back)
    packed = kernel_call(
        finish_body,
        [SMEM] + [VMEM] * 7,
        [(VMEM, split)],
        scratch=[VMEM((TOKENS, DH), F32)],
        bytes_accessed=3 * mb,
    )(place, out, dkv, *returned)
    results = swap(packed, HEAD_AXES)
    flat = shape(TOKENS_IN, HEADS * DH)
    return tuple(
        kernel_call(unpack_body, [VMEM], [(VMEM, flat)] * 4, bytes_accessed=2 * mb)(results)
    )


def solution(mesh):
    fine = Mesh(mesh.devices.reshape(8, 4, 4, 2, 2), AXES)
    placed = P(AXES, None)
    return jax.shard_map(
        on_device,
        mesh=fine,
        in_specs=(placed,) * 4,
        out_specs=(placed,) * 4,
        check_vma=False,
    )
```

time: 152 us -> 140 us (0.921)
  Pallas kernels: 21.7 us -> 13.6 us
  local copies, waits for them, and re-layouts: 2.69 us -> 0 us
    pallas_call x5 -> x7, Pallas kernels: 21.7 us -> 13.6 us  [the longest x1 7.82 us: on_device(): kernel_call(attend_body, [SMEM] + [VMEM] * 4, [(VMEM, shape(HEADS, 2, TOK...]
    unnamed x38 -> x0, local copies, waits for them, and re-layouts: 2.69 us -> none
    ppermute x6, waiting for transfers between devices: 10.8 us -> 8.97 us  [exchange(): lax.ppermute(array, 'x', [(i, i ^ mask) for i in range(4)])]
    ppermute x2, starting transfers between devices: 9.76 us -> 7.96 us  [exchange(): p4 = lax.ppermute(p4, SEQ_AXES, odd_pairs(RANKS))]
  transfers between devices with their start and end apart: 11 -> 11, of which waited for: 3 -> 6; matrix products, arithmetic and copies ran while one was open for 0% -> 0% of each run, Pallas kernels for 0% -> 0%
where the time goes in v2:
time: 140 us; the launch traced here: 138 us
  starting transfers between devices  54 us (39%)
  waiting for transfers between devices  37.4 us (27%)
  blocking collectives  32 us (23%)
  Pallas kernels  13.6 us (10%)
    all_to_all x1, blocking collectives, swap(): return lax.all_to_all(array, axes, split_axis=0, concat_axis=0, tiled=True)  32 us
    all_to_all x3, starting transfers between devices, swap(): return lax.all_to_all(array, axes, split_axis=0, concat_axis=0, tiled=True)  29.3 us
    all_to_all x3, waiting for transfers between devices, swap(): return lax.all_to_all(array, axes, split_axis=0, concat_axis=0, tiled=True)  28.5 us
    ppermute x6, starting transfers between devices, exchange(): lax.ppermute(array, 'x', [(i, i ^ mask) for i in range(4)])  16.7 us
    ppermute x6, waiting for transfers between devices, exchange(): lax.ppermute(array, 'x', [(i, i ^ mask) for i in range(4)])  8.97 us
    ppermute x2, starting transfers between devices, exchange(): p4 = lax.ppermute(p4, SEQ_AXES, odd_pairs(RANKS))  7.96 us
    pallas_call x1, Pallas kernels, on_device(): kernel_call(attend_body, [SMEM] + [VMEM] * 4, [(VMEM, shape(HEADS, 2, TOK...  7.82 us
  transfers between devices with their start and end apart: 11, of which 6 were waited for; matrix products, arithmetic and copies ran while one was open for 0% of the time, Pallas kernels for 0%

profile of v2, /device:TPU:6, one launch (start us, length us, event | category | flops | bytes accessed | tf_op | source)
XLA Modules:
  0.0 137.7 jit_solution(11368852775805053661)
XLA Ops:
  0.6 2.1 %shard_map.75 = bf16[16,4,64,128]{3,2,1,0:T(8,128)(2,1)} custom-call(bf16[64,2048]{1,0:T(8,128)(2,1)} %q_ref.1, bf16[64,2048]{1,0:T(8,128)(2,1)} %k_ref.1, bf16[64,2048]{1,0:T(8,128)(2,1)} %v_ref.1, bf16[64,2048]{1,0:T(8,128)(2,1)} %d_ref.1), custom_call_target="tpu_custom_call" | custom-call | bytes 2097152 | tf_op jit(solution)/shard_map/pallas_call | solution.py:368
  2.7 7.2 %all-to-all-start = ((bf16[16,4,64,128]{3,2,1,0:T(8,128)(2,1)}), bf16[16,4,64,128]{3,2,1,0:T(8,128)(2,1)S(1)}, u32[]{:S(2)}, u32[]{:S(2)}) async-start(bf16[16,4,64,128]{3,2,1,0:T(8,128)(2,1)} %shard_map.75), calls=%async_computation | async-start | bytes 2097152 | tf_op jit(solution)/shard_map/all_to_all | solution.py:338
  9.9 27.6 %all-to-all-done.in_ref = bf16[16,4,64,128]{3,2,1,0:T(8,128)(2,1)S(1)} async-done(((bf16[16,4,64,128]{3,2,1,0:T(8,128)(2,1)}), bf16[16,4,64,128]{3,2,1,0:T(8,128)(2,1)S(1)}, u32[]{:S(2)}, u32[]{:S(2)}) %all-to-all-start) | async-done | bytes 1048608 | tf_op jit(solution)/shard_map/all_to_all | solution.py:338
  37.6 1.2 shard_map.76
  38.7 13.4 %all-to-all-start.1 = ((bf16[32,2,32,128]{3,2,1,0:T(8,128)(2,1)}), bf16[32,2,32,128]{3,2,1,0:T(8,128)(2,1)S(1)}, u32[]{:S(2)}, u32[]{:S(2)}) async-start(bf16[32,2,32,128]{3,2,1,0:T(8,128)(2,1)} %get-tuple-element.22), calls=%async_computation.1 | async-start | bytes 1048576 | tf_op jit(solution)/shard_map/all_to_all | solution.py:338
  52.1 2.8 %collective-permute-start = (bf16[2,256,128]{2,1,0:T(8,128)(2,1)S(1)}, bf16[2,256,128]{2,1,0:T(8,128)(2,1)S(1)}, u32[]{:S(2)}, u32[]{:S(2)}) collective-permute-start(bf16[2,256,128]{2,1,0:T(8,128)(2,1)S(1)} %get-tuple-element.23), channel_id=1, source_target_pairs={{0,16},{16,0},{32,48},{48,32},{1,17},{17,1},{33,49},{49,33},{2,18}... | collective-permute-start | bytes 393224 | tf_op jit(solution)/shard_map/ppermute | solution.py:349
  54.9 4.0 %collective-permute-start.3 = (bf16[2,128,128]{2,1,0:T(8,128)(2,1)S(1)}, bf16[2,128,128]{2,1,0:T(8,128)(2,1)S(1)}, u32[]{:S(2)}, u32[]{:S(2)}) collective-permute-start(bf16[2,128,128]{2,1,0:T(8,128)(2,1)S(1)} %get-tuple-element.26), channel_id=1, source_target_pairs={{16,32},{32,16},{48,64},{64,48},{80,96},{96,80},{112,128},{128,112... | collective-permute-start | bytes 196616 | tf_op jit(solution)/shard_map/ppermute | solution.py:353
  58.9 3.1 %collective-permute-start.1 = (bf16[2,64,128]{2,1,0:T(8,128)(2,1)S(1)}, bf16[2,64,128]{2,1,0:T(8,128)(2,1)S(1)}, u32[]{:S(2)}, u32[]{:S(2)}) collective-permute-start(bf16[2,64,128]{2,1,0:T(8,128)(2,1)S(1)} %get-tuple-element.24), channel_id=1, source_target_pairs={{0,32},{16,48},{32,0},{48,16},{1,33},{17,49},{33,1},{49,17},{2,34}... | collective-permute-start | bytes 98312 | tf_op jit(solution)/shard_map/ppermute | solution.py:349
  62.0 2.5 %collective-permute-start.2 = (bf16[2,64,128]{2,1,0:T(8,128)(2,1)S(1)}, bf16[2,64,128]{2,1,0:T(8,128)(2,1)S(1)}, u32[]{:S(2)}, u32[]{:S(2)}) collective-permute-start(bf16[2,64,128]{2,1,0:T(8,128)(2,1)S(1)} %get-tuple-element.25), channel_id=1, source_target_pairs={{0,48},{16,32},{32,16},{48,0},{1,49},{17,33},{33,17},{49,1},{2,50}... | collective-permute-start | bytes 98312 | tf_op jit(solution)/shard_map/ppermute | solution.py:349
  64.5 2.2 %collective-permute-done.1.p2_ref = bf16[2,64,128]{2,1,0:T(8,128)(2,1)S(1)} collective-permute-done((bf16[2,64,128]{2,1,0:T(8,128)(2,1)S(1)}, bf16[2,64,128]{2,1,0:T(8,128)(2,1)S(1)}, u32[]{:S(2)}, u32[]{:S(2)}) %collective-permute-start.1) | collective-permute-done | bytes 32800 | tf_op jit(solution)/shard_map/ppermute | solution.py:349
  66.7 2.3 %collective-permute-done.2.p3_ref = bf16[2,64,128]{2,1,0:T(8,128)(2,1)S(1)} collective-permute-done((bf16[2,64,128]{2,1,0:T(8,128)(2,1)S(1)}, bf16[2,64,128]{2,1,0:T(8,128)(2,1)S(1)}, u32[]{:S(2)}, u32[]{:S(2)}) %collective-permute-start.2) | collective-permute-done | bytes 32800 | tf_op jit(solution)/shard_map/ppermute | solution.py:349
  69.0 0.0 collective-permute-done.3.p4_ref
  69.0 0.0 collective-permute-done.p1_ref
  69.0 0.8 all-to-all-done.1.zx_ref
  69.8 0.1 shard_map.77
  69.9 7.8 %shard_map.78 = (bf16[16,2,64,128]{3,2,1,0:T(8,128)(2,1)S(1)}, f32[2,1024,128]{2,1,0:T(8,128)S(1)}, bf16[2,640,128]{2,1,0:T(8,128)(2,1)S(1)}, bf16[2,256,128]{2,1,0:T(8,128)(2,1)S(1)}) custom-call(s32[1]{0:T(128)} %bitcast.place_ref, bf16[16,4,64,128]{3,2,1,0:T(8,128)(2,1)S(1)} %all-to-all-done.in_ref, bf16[2,768,128]{2,1,0:T(8,128)(2,1)S(1)} %get-tuple-element.21.pyr_ref, ...), custom_call_target="tpu_custom_call" | custom-call | flops 2000000000 | bytes 5242880 | tf_op jit(solution)/shard_map/pallas_call | solution.py:394
  77.7 0.9 shard_map.79
  78.6 8.7 %all-to-all-start.2 = ((bf16[32,2,32,128]{3,2,1,0:T(8,128)(2,1)}), bf16[32,2,32,128]{3,2,1,0:T(8,128)(2,1)S(1)}, u32[]{:S(2)}, u32[]{:S(2)}) async-start(bf16[32,2,32,128]{3,2,1,0:T(8,128)(2,1)} %get-tuple-element.33), calls=%async_computation.2 | async-start | bytes 1048576 | tf_op jit(solution)/shard_map/all_to_all | solution.py:338
  87.3 2.8 %collective-permute-start.4 = (bf16[2,256,128]{2,1,0:T(8,128)(2,1)S(1)}, bf16[2,256,128]{2,1,0:T(8,128)(2,1)S(1)}, u32[]{:S(2)}, u32[]{:S(2)}) collective-permute-start(bf16[2,256,128]{2,1,0:T(8,128)(2,1)S(1)} %get-tuple-element.34), channel_id=1, source_target_pairs={{0,16},{16,0},{32,48},{48,32},{1,17},{17,1},{33,49},{49,33},{2,18}... | collective-permute-start | bytes 393224 | tf_op jit(solution)/shard_map/ppermute | solution.py:349
  90.1 4.0 %collective-permute-start.7 = (bf16[2,128,128]{2,1,0:T(8,128)(2,1)S(1)}, bf16[2,128,128]{2,1,0:T(8,128)(2,1)S(1)}, u32[]{:S(2)}, u32[]{:S(2)}) collective-permute-start(bf16[2,128,128]{2,1,0:T(8,128)(2,1)S(1)} %get-tuple-element.37), channel_id=1, source_target_pairs={{16,32},{32,16},{48,64},{64,48},{80,96},{96,80},{112,128},{128,112... | collective-permute-start | bytes 196616 | tf_op jit(solution)/shard_map/ppermute | solution.py:353
  94.1 3.1 %collective-permute-start.5 = (bf16[2,64,128]{2,1,0:T(8,128)(2,1)S(1)}, bf16[2,64,128]{2,1,0:T(8,128)(2,1)S(1)}, u32[]{:S(2)}, u32[]{:S(2)}) collective-permute-start(bf16[2,64,128]{2,1,0:T(8,128)(2,1)S(1)} %get-tuple-element.35), channel_id=1, source_target_pairs={{0,32},{16,48},{32,0},{48,16},{1,33},{17,49},{33,1},{49,17},{2,34}... | collective-permute-start | bytes 98312 | tf_op jit(solution)/shard_map/ppermute | solution.py:349
  97.1 2.5 %collective-permute-start.6 = (bf16[2,64,128]{2,1,0:T(8,128)(2,1)S(1)}, bf16[2,64,128]{2,1,0:T(8,128)(2,1)S(1)}, u32[]{:S(2)}, u32[]{:S(2)}) collective-permute-start(bf16[2,64,128]{2,1,0:T(8,128)(2,1)S(1)} %get-tuple-element.36), channel_id=1, source_target_pairs={{0,48},{16,32},{32,16},{48,0},{1,49},{17,33},{33,17},{49,1},{2,50}... | collective-permute-start | bytes 98312 | tf_op jit(solution)/shard_map/ppermute | solution.py:349
  99.7 1.9 %collective-permute-done.5.p2_ref = bf16[2,64,128]{2,1,0:T(8,128)(2,1)S(1)} collective-permute-done((bf16[2,64,128]{2,1,0:T(8,128)(2,1)S(1)}, bf16[2,64,128]{2,1,0:T(8,128)(2,1)S(1)}, u32[]{:S(2)}, u32[]{:S(2)}) %collective-permute-start.5) | collective-permute-done | bytes 32800 | tf_op jit(solution)/shard_map/ppermute | solution.py:349
  101.5 2.6 %collective-permute-done.6.p3_ref = bf16[2,64,128]{2,1,0:T(8,128)(2,1)S(1)} collective-permute-done((bf16[2,64,128]{2,1,0:T(8,128)(2,1)S(1)}, bf16[2,64,128]{2,1,0:T(8,128)(2,1)S(1)}, u32[]{:S(2)}, u32[]{:S(2)}) %collective-permute-start.6) | collective-permute-done | bytes 32800 | tf_op jit(solution)/shard_map/ppermute | solution.py:349
  104.2 0.0 collective-permute-done.7.p4_ref
  104.2 0.0 collective-permute-done.4.p1_ref
  104.2 0.0 all-to-all-done.2.zx_ref
  104.2 0.4 shard_map.80
  104.6 32.0 %all_to_all.20.in_ref = bf16[16,4,64,128]{3,2,1,0:T(8,128)(2,1)S(1)} all-to-all(bf16[16,4,64,128]{3,2,1,0:T(8,128)(2,1)S(1)} %shard_map.80), channel_id=1, replica_groups=mesh['z'=8,'x'=4,'y_lo'=4,'y_hi'=2,'core'=2] {'y_lo','y_hi','core'}, dimensions={0} | all-to-all | bytes 2097152 | tf_op jit(solution)/shard_map/all_to_all | solution.py:338
  136.5 1.2 shard_map.81
Async XLA Ops:
  2.7 34.8 %all-to-all-start = ((bf16[16,4,64,128]{3,2,1,0:T(8,128)(2,1)}), bf16[16,4,64,128]{3,2,1,0:T(8,128)(2,1)S(1)}, u32[]{:S(2)}, u32[]{:S(2)}) async-start(bf16[16,4,64,128]{3,2,1,0:T(8,128)(2,1)} %shard_map.75), calls=%async_computation | async-start | bytes 2097152 | tf_op jit(solution)/shard_map/all_to_all | solution.py:338
  38.7 31.1 %all-to-all-start.1 = ((bf16[32,2,32,128]{3,2,1,0:T(8,128)(2,1)}), bf16[32,2,32,128]{3,2,1,0:T(8,128)(2,1)S(1)}, u32[]{:S(2)}, u32[]{:S(2)}) async-start(bf16[32,2,32,128]{3,2,1,0:T(8,128)(2,1)} %get-tuple-element.22), calls=%async_computation.1 | async-start | bytes 1048576 | tf_op jit(solution)/shard_map/all_to_all | solution.py:338
  52.1 16.9 %collective-permute-start = (bf16[2,256,128]{2,1,0:T(8,128)(2,1)S(1)}, bf16[2,256,128]{2,1,0:T(8,128)(2,1)S(1)}, u32[]{:S(2)}, u32[]{:S(2)}) collective-permute-start(bf16[2,256,128]{2,1,0:T(8,128)(2,1)S(1)} %get-tuple-element.23), channel_id=1, source_target_pairs={{0,16},{16,0},{32,48},{48,32},{1,17},{17,1},{33,49},{49,33},{2,18}... | collective-permute-start | bytes 393224 | tf_op jit(solution)/shard_map/ppermute | solution.py:349
  54.9 14.1 %collective-permute-start.3 = (bf16[2,128,128]{2,1,0:T(8,128)(2,1)S(1)}, bf16[2,128,128]{2,1,0:T(8,128)(2,1)S(1)}, u32[]{:S(2)}, u32[]{:S(2)}) collective-permute-start(bf16[2,128,128]{2,1,0:T(8,128)(2,1)S(1)} %get-tuple-element.26), channel_id=1, source_target_pairs={{16,32},{32,16},{48,64},{64,48},{80,96},{96,80},{112,128},{128,112... | collective-permute-start | bytes 196616 | tf_op jit(solution)/shard_map/ppermute | solution.py:353
  58.9 7.8 %collective-permute-start.1 = (bf16[2,64,128]{2,1,0:T(8,128)(2,1)S(1)}, bf16[2,64,128]{2,1,0:T(8,128)(2,1)S(1)}, u32[]{:S(2)}, u32[]{:S(2)}) collective-permute-start(bf16[2,64,128]{2,1,0:T(8,128)(2,1)S(1)} %get-tuple-element.24), channel_id=1, source_target_pairs={{0,32},{16,48},{32,0},{48,16},{1,33},{17,49},{33,1},{49,17},{2,34}... | collective-permute-start | bytes 98312 | tf_op jit(solution)/shard_map/ppermute | solution.py:349
  62.0 7.0 %collective-permute-start.2 = (bf16[2,64,128]{2,1,0:T(8,128)(2,1)S(1)}, bf16[2,64,128]{2,1,0:T(8,128)(2,1)S(1)}, u32[]{:S(2)}, u32[]{:S(2)}) collective-permute-start(bf16[2,64,128]{2,1,0:T(8,128)(2,1)S(1)} %get-tuple-element.25), channel_id=1, source_target_pairs={{0,48},{16,32},{32,16},{48,0},{1,49},{17,33},{33,17},{49,1},{2,50}... | collective-permute-start | bytes 98312 | tf_op jit(solution)/shard_map/ppermute | solution.py:349
  78.6 25.5 %all-to-all-start.2 = ((bf16[32,2,32,128]{3,2,1,0:T(8,128)(2,1)}), bf16[32,2,32,128]{3,2,1,0:T(8,128)(2,1)S(1)}, u32[]{:S(2)}, u32[]{:S(2)}) async-start(bf16[32,2,32,128]{3,2,1,0:T(8,128)(2,1)} %get-tuple-element.33), calls=%async_computation.2 | async-start | bytes 1048576 | tf_op jit(solution)/shard_map/all_to_all | solution.py:338
  87.3 16.9 %collective-permute-start.4 = (bf16[2,256,128]{2,1,0:T(8,128)(2,1)S(1)}, bf16[2,256,128]{2,1,0:T(8,128)(2,1)S(1)}, u32[]{:S(2)}, u32[]{:S(2)}) collective-permute-start(bf16[2,256,128]{2,1,0:T(8,128)(2,1)S(1)} %get-tuple-element.34), channel_id=1, source_target_pairs={{0,16},{16,0},{32,48},{48,32},{1,17},{17,1},{33,49},{49,33},{2,18}... | collective-permute-start | bytes 393224 | tf_op jit(solution)/shard_map/ppermute | solution.py:349
  90.1 14.1 %collective-permute-start.7 = (bf16[2,128,128]{2,1,0:T(8,128)(2,1)S(1)}, bf16[2,128,128]{2,1,0:T(8,128)(2,1)S(1)}, u32[]{:S(2)}, u32[]{:S(2)}) collective-permute-start(bf16[2,128,128]{2,1,0:T(8,128)(2,1)S(1)} %get-tuple-element.37), channel_id=1, source_target_pairs={{16,32},{32,16},{48,64},{64,48},{80,96},{96,80},{112,128},{128,112... | collective-permute-start | bytes 196616 | tf_op jit(solution)/shard_map/ppermute | solution.py:353
  94.1 7.5 %collective-permute-start.5 = (bf16[2,64,128]{2,1,0:T(8,128)(2,1)S(1)}, bf16[2,64,128]{2,1,0:T(8,128)(2,1)S(1)}, u32[]{:S(2)}, u32[]{:S(2)}) collective-permute-start(bf16[2,64,128]{2,1,0:T(8,128)(2,1)S(1)} %get-tuple-element.35), channel_id=1, source_target_pairs={{0,32},{16,48},{32,0},{48,16},{1,33},{17,49},{33,1},{49,17},{2,34}... | collective-permute-start | bytes 98312 | tf_op jit(solution)/shard_map/ppermute | solution.py:349
  97.1 7.0 %collective-permute-start.6 = (bf16[2,64,128]{2,1,0:T(8,128)(2,1)S(1)}, bf16[2,64,128]{2,1,0:T(8,128)(2,1)S(1)}, u32[]{:S(2)}, u32[]{:S(2)}) collective-permute-start(bf16[2,64,128]{2,1,0:T(8,128)(2,1)S(1)} %get-tuple-element.36), channel_id=1, source_target_pairs={{0,48},{16,32},{32,16},{48,0},{1,49},{17,33},{33,17},{49,1},{2,50}... | collective-permute-start | bytes 98312 | tf_op jit(solution)/shard_map/ppermute | solution.py:349

commit v3 on v2

--- a/solution.py
+++ b/solution.py
@@ -29,16 +29,11 @@
 
 NN = (((1,), (0,)), ((), ()))
 NT = (((1,), (1,)), ((), ()))
+TN = (((0,), (0,)), ((), ()))
 
 
 def dot(a, b, dims=NN):
     return lax.dot_general(a, b, dims, preferred_element_type=F32)
-
-
-def eye(n):
-    row = lax.broadcasted_iota(jnp.int32, (n, n), 0)
-    col = lax.broadcasted_iota(jnp.int32, (n, n), 1)
-    return jnp.where(row == col, 1.0, 0.0).astype(BF)
 
 
 def kernel_call(body, ins, outs, scratch=(), flops=0, bytes_accessed=0, mib=SMALL):
@@ -78,10 +73,15 @@
         store.wait()
 
 
-def unpack_body(in_ref, o_ref, dq_ref, dk_ref, dv_ref):
-    for h in range(HEADS):
-        for i, ref in enumerate((o_ref, dq_ref, dk_ref, dv_ref)):
-            ref[:, h * DH : (h + 1) * DH] = in_ref[h, i]
+def unpack_body(in_ref, o_ref, dq_ref, dk_ref, dv_ref, held, out_sem):
+    refs = (o_ref, dq_ref, dk_ref, dv_ref)
+    stores = [pltpu.make_async_copy(held.at[i], ref, out_sem.at[i]) for i, ref in enumerate(refs)]
+    for i in range(4):
+        for h in range(HEADS):
+            held[i, :, h * DH : (h + 1) * DH] = in_ref[h, i]
+        stores[i].start()
+    for store in stores:
+        store.wait()
 
 
 def rows_of(ref, i, start, count):
@@ -183,46 +183,38 @@
     drem_ref,
     dedge_ref,
     win,
-    win_t,
-    pyr_t,
-    rem_t,
     dwin,
     dpyr,
     drem,
     spread,
 ):
     s = place_ref[0]
-    ident = eye(DH)
     for i in range(2):
         win[i, 0:128] = edge_ref[i, 0:128]
         win[i, 128:1152] = in_ref[:, 1 + i].reshape(TOKENS, DH)
         win[i, 1152:1280] = edge_ref[i, 128:256]
-        win_t[i] = dot(ident, win[i], NT).astype(BF)
-        pyr_t[i] = dot(ident, pyr_ref[i], NT).astype(BF)
-        rem_t[i] = dot(ident, rem[i], NT).astype(BF)
     dwin[...] = jnp.zeros_like(dwin)
     drem[...] = jnp.zeros_like(drem)
     dpyr[...] = jnp.zeros_like(dpyr)
     second = lax.broadcasted_iota(jnp.int32, (1, 2 * BLOCK), 1) >= BLOCK
-    ident2 = eye(2 * BLOCK)
-
-    def load(p):
+
+    def products(p):
         q = in_ref[4 * p : 4 * p + 4, 0].reshape(2 * BLOCK, DH)
         dy = in_ref[4 * p : 4 * p + 4, 3].reshape(2 * BLOCK, DH)
         one = (p ^ 1) * BLOCK
         two = 512 + ((p // 2) ^ 1) * BLOCK
         groups = (
-            (win, win_t, dwin, 2 * p * BLOCK, (0, 0, 0, 0)),
-            (pyr_ref, pyr_t, dpyr, one, (1,)),
-            (pyr_ref, pyr_t, dpyr, two, (2,)),
-            (rem, rem_t, drem, 0, (3, 4, 5, 6, 7)),
+            (win, dwin, slice(2 * p * BLOCK, (2 * p + 4) * BLOCK), (0, 0, 0, 0)),
+            (pyr_ref, dpyr, slice(one, one + BLOCK), (1,)),
+            (pyr_ref, dpyr, slice(two, two + BLOCK), (2,)),
+            (rem, drem, slice(0, 640), (3, 4, 5, 6, 7)),
         )
-        raws = [dot(ref[0, start : start + BLOCK * len(shifts)], q, NT) for ref, _, _, start, shifts in groups]
-        pushes = [dot(ref[1, start : start + BLOCK * len(shifts)], dy, NT) for ref, _, _, start, shifts in groups] if True else None
-        dy_t = dot(ident, dy, NT)
-        return q, dy, groups, raws, pushes, dy_t
-    def soft(p, state):
-        q, dy, groups, raws, pushes, dy_t = state
+        raws = [dot(ref[0, rows], q, NT) for ref, _, rows, _ in groups]
+        pushes = [dot(ref[1, rows], dy, NT) for ref, _, rows, _ in groups]
+        return q, dy, groups, raws, pushes
+
+    def softmax(p, state):
+        _, _, groups, raws, _ = state
         first_gap = jnp.where(second, NEG_FILL, 0.0).astype(F32)
         last_gap = jnp.where(second, 0.0, NEG_FILL).astype(F32)
         if p == 0:
@@ -231,7 +223,7 @@
             last_gap = jnp.where(s == RANKS - 1, NEG_FILL, last_gap)
         score = []
         top = None
-        for raw, (ref, _, _, start, shifts) in zip(raws, groups):
+        for raw, (_, _, _, shifts) in zip(raws, groups):
             blocks = [raw[n * BLOCK : (n + 1) * BLOCK] for n in range(len(shifts))]
             if len(shifts) == 4:
                 blocks[0] = blocks[0] + first_gap
@@ -241,41 +233,42 @@
                 top = peak if top is None else jnp.maximum(top, peak)
             score.append(blocks)
         total = jnp.zeros((1, 2 * BLOCK), F32)
-        for blocks, group in zip(score, groups):
-            for n, shift in enumerate(group[4]):
+        for blocks, (_, _, _, shifts) in zip(score, groups):
+            for n, shift in enumerate(shifts):
                 blocks[n] = jnp.exp2(blocks[n] * SCALE_2 + (float(shift) - top))
                 total = total + jnp.sum(blocks[n], axis=0, keepdims=True)
         inverse = 1.0 / total
         score = [jnp.concatenate(blocks, axis=0) * inverse for blocks in score]
-        light = [item.astype(BF) for item in score]
-        return score, light
-    def tail(p, state, weights):
-        q, dy, groups, raws, pushes, dy_t = state
+        return score, [item.astype(BF) for item in score]
+
+    def gradients(p, state, weights):
+        q, dy, groups, _, pushes = state
         score, light = weights
-        out_t = jnp.zeros((DH, 2 * BLOCK), F32)
-        for (_, ref_t, _, start, shifts), item in zip(groups, light):
-            out_t = out_t + dot(ref_t[1, :, start : start + BLOCK * len(shifts)], item)
-        delta = jnp.sum(out_t * dy_t, axis=0, keepdims=True)
-        out_ref[4 * p : 4 * p + 4, 0] = (
-            dot(ident2, out_t.astype(BF), NT).astype(BF).reshape(4, TOKENS_IN, DH)
-        )
-        dq_t = jnp.zeros((DH, 2 * BLOCK), F32)
-        for n, ((ref, ref_t, dref, start, shifts), item, item_light) in enumerate(zip(groups, score, light)):
-            rows = slice(start, start + BLOCK * len(shifts))
-            pushed = pushes[n] if True else dot(ref[1, rows], dy, NT)
+        slots = slice(4 * p, 4 * p + 4)
+        tall = None
+        for item, pushed in zip(score, pushes):
+            for n in range(0, item.shape[0], BLOCK):
+                term = item[n : n + BLOCK] * pushed[n : n + BLOCK]
+                tall = term if tall is None else tall + term
+        delta = jnp.sum(tall, axis=0, keepdims=True)
+        out = jnp.zeros((2 * BLOCK, DH), F32)
+        dq = jnp.zeros((2 * BLOCK, DH), F32)
+        for (ref, dref, rows, _), item, item_light, pushed in zip(groups, score, light, pushes):
+            out = out + dot(item_light, ref[1, rows], TN)
             grad = (item * (pushed - delta)).astype(BF)
-            dq_t = dq_t + dot(ref_t[0, :, rows], grad)
+            dq = dq + dot(grad, ref[0, rows], TN)
             dref[0, rows] += dot(grad, q)
             dref[1, rows] += dot(item_light, dy)
-        out_ref[4 * p : 4 * p + 4, 1] = (
-            dot(ident2, (dq_t * SCALE).astype(BF), NT).astype(BF).reshape(4, TOKENS_IN, DH)
-        )
-    state = load(0)
-    weights = soft(0, state)
-    for p in range(4):
-        following = load(p + 1) if p < 3 else None
-        after = soft(p + 1, following) if p < 3 else None
-        tail(p, state, weights)
+        out_ref[slots, 0] = out.astype(BF).reshape(4, TOKENS_IN, DH)
+        out_ref[slots, 1] = (dq * SCALE).astype(BF).reshape(4, TOKENS_IN, DH)
+
+    state = products(0)
+    weights = softmax(0, state)
+    for p in range(BLOCKS // 2):
+        last = p == BLOCKS // 2 - 1
+        following = None if last else products(p + 1)
+        after = None if last else softmax(p + 1, following)
+        gradients(p, state, weights)
         state, weights = following, after
     dwin[0] = dwin[0] * SCALE
     dpyr[0] = dpyr[0] * SCALE
@@ -401,9 +394,6 @@
         + [(VMEM, item) for item in rows],
         scratch=[
             VMEM((2, 1280, DH), BF),
-            VMEM((2, DH, 1280), BF),
-            VMEM((2, DH, 768), BF),
-            VMEM((2, DH, 640), BF),
             VMEM((2, 1280, DH), F32),
             VMEM((2, 768, DH), F32),
             VMEM((2, 640, DH), F32),
@@ -427,7 +417,13 @@
     results = swap(packed, HEAD_AXES)
     flat = shape(TOKENS_IN, HEADS * DH)
     return tuple(
-        kernel_call(unpack_body, [VMEM], [(VMEM, flat)] * 4, bytes_accessed=2 * mb)(results)
+        kernel_call(
+            unpack_body,
+            [VMEM],
+            [(HBM, flat)] * 4,
+            scratch=[VMEM((4, TOKENS_IN, HEADS * DH), BF), pltpu.SemaphoreType.DMA((4,))],
+            bytes_accessed=2 * mb,
+        )(results)
     )
 
 

time: 140 us -> 138 us (0.986)
  no operation moved by 1% of the time
where the time goes in v3:
time: 138 us; the launch traced here: 136 us
  starting transfers between devices  54 us (39%)
  waiting for transfers between devices  37.4 us (27%)
  blocking collectives  32 us (23%)
  Pallas kernels  12.3 us (9%)
    all_to_all x1, blocking collectives, swap(): return lax.all_to_all(array, axes, split_axis=0, concat_axis=0, tiled=True)  32 us
    all_to_all x3, starting transfers between devices, swap(): return lax.all_to_all(array, axes, split_axis=0, concat_axis=0, tiled=True)  29.3 us
    all_to_all x3, waiting for transfers between devices, swap(): return lax.all_to_all(array, axes, split_axis=0, concat_axis=0, tiled=True)  28.5 us
    ppermute x6, starting transfers between devices, exchange(): lax.ppermute(array, 'x', [(i, i ^ mask) for i in range(4)])  16.7 us
    ppermute x6, waiting for transfers between devices, exchange(): lax.ppermute(array, 'x', [(i, i ^ mask) for i in range(4)])  8.97 us
    ppermute x2, starting transfers between devices, exchange(): p4 = lax.ppermute(p4, SEQ_AXES, odd_pairs(RANKS))  7.96 us
    pallas_call x1, Pallas kernels, on_device(): kernel_call(attend_body, [SMEM] + [VMEM] * 4, [(VMEM, shape(HEADS, 2, TOK...  6.63 us
  transfers between devices with their start and end apart: 11, of which 6 were waited for; matrix products, arithmetic and copies ran while one was open for 0% of the time, Pallas kernels for 0%

profile of v3, /device:TPU:6, one launch (start us, length us, event | category | flops | bytes accessed | tf_op | source)
XLA Modules:
  0.0 136.4 jit_solution(13407024535045456963)
XLA Ops:
  0.6 2.1 %shard_map.75 = bf16[16,4,64,128]{3,2,1,0:T(8,128)(2,1)} custom-call(bf16[64,2048]{1,0:T(8,128)(2,1)} %q_ref.1, bf16[64,2048]{1,0:T(8,128)(2,1)} %k_ref.1, bf16[64,2048]{1,0:T(8,128)(2,1)} %v_ref.1, bf16[64,2048]{1,0:T(8,128)(2,1)} %d_ref.1), custom_call_target="tpu_custom_call" | custom-call | bytes 2097152 | tf_op jit(solution)/shard_map/pallas_call | solution.py:361
  2.7 7.2 %all-to-all-start = ((bf16[16,4,64,128]{3,2,1,0:T(8,128)(2,1)}), bf16[16,4,64,128]{3,2,1,0:T(8,128)(2,1)S(1)}, u32[]{:S(2)}, u32[]{:S(2)}) async-start(bf16[16,4,64,128]{3,2,1,0:T(8,128)(2,1)} %shard_map.75), calls=%async_computation | async-start | bytes 2097152 | tf_op jit(solution)/shard_map/all_to_all | solution.py:331
  9.9 27.6 %all-to-all-done.in_ref = bf16[16,4,64,128]{3,2,1,0:T(8,128)(2,1)S(1)} async-done(((bf16[16,4,64,128]{3,2,1,0:T(8,128)(2,1)}), bf16[16,4,64,128]{3,2,1,0:T(8,128)(2,1)S(1)}, u32[]{:S(2)}, u32[]{:S(2)}) %all-to-all-start) | async-done | bytes 1048608 | tf_op jit(solution)/shard_map/all_to_all | solution.py:331
  37.6 1.2 shard_map.76
  38.7 13.4 %all-to-all-start.1 = ((bf16[32,2,32,128]{3,2,1,0:T(8,128)(2,1)}), bf16[32,2,32,128]{3,2,1,0:T(8,128)(2,1)S(1)}, u32[]{:S(2)}, u32[]{:S(2)}) async-start(bf16[32,2,32,128]{3,2,1,0:T(8,128)(2,1)} %get-tuple-element.22), calls=%async_computation.1 | async-start | bytes 1048576 | tf_op jit(solution)/shard_map/all_to_all | solution.py:331
  52.1 2.8 %collective-permute-start = (bf16[2,256,128]{2,1,0:T(8,128)(2,1)S(1)}, bf16[2,256,128]{2,1,0:T(8,128)(2,1)S(1)}, u32[]{:S(2)}, u32[]{:S(2)}) collective-permute-start(bf16[2,256,128]{2,1,0:T(8,128)(2,1)S(1)} %get-tuple-element.23), channel_id=1, source_target_pairs={{0,16},{16,0},{32,48},{48,32},{1,17},{17,1},{33,49},{49,33},{2,18}... | collective-permute-start | bytes 393224 | tf_op jit(solution)/shard_map/ppermute | solution.py:342
  54.9 4.0 %collective-permute-start.3 = (bf16[2,128,128]{2,1,0:T(8,128)(2,1)S(1)}, bf16[2,128,128]{2,1,0:T(8,128)(2,1)S(1)}, u32[]{:S(2)}, u32[]{:S(2)}) collective-permute-start(bf16[2,128,128]{2,1,0:T(8,128)(2,1)S(1)} %get-tuple-element.26), channel_id=1, source_target_pairs={{16,32},{32,16},{48,64},{64,48},{80,96},{96,80},{112,128},{128,112... | collective-permute-start | bytes 196616 | tf_op jit(solution)/shard_map/ppermute | solution.py:346
  58.9 3.1 %collective-permute-start.1 = (bf16[2,64,128]{2,1,0:T(8,128)(2,1)S(1)}, bf16[2,64,128]{2,1,0:T(8,128)(2,1)S(1)}, u32[]{:S(2)}, u32[]{:S(2)}) collective-permute-start(bf16[2,64,128]{2,1,0:T(8,128)(2,1)S(1)} %get-tuple-element.24), channel_id=1, source_target_pairs={{0,32},{16,48},{32,0},{48,16},{1,33},{17,49},{33,1},{49,17},{2,34}... | collective-permute-start | bytes 98312 | tf_op jit(solution)/shard_map/ppermute | solution.py:342
  62.0 2.5 %collective-permute-start.2 = (bf16[2,64,128]{2,1,0:T(8,128)(2,1)S(1)}, bf16[2,64,128]{2,1,0:T(8,128)(2,1)S(1)}, u32[]{:S(2)}, u32[]{:S(2)}) collective-permute-start(bf16[2,64,128]{2,1,0:T(8,128)(2,1)S(1)} %get-tuple-element.25), channel_id=1, source_target_pairs={{0,48},{16,32},{32,16},{48,0},{1,49},{17,33},{33,17},{49,1},{2,50}... | collective-permute-start | bytes 98312 | tf_op jit(solution)/shard_map/ppermute | solution.py:342
  64.5 2.2 %collective-permute-done.1.p2_ref = bf16[2,64,128]{2,1,0:T(8,128)(2,1)S(1)} collective-permute-done((bf16[2,64,128]{2,1,0:T(8,128)(2,1)S(1)}, bf16[2,64,128]{2,1,0:T(8,128)(2,1)S(1)}, u32[]{:S(2)}, u32[]{:S(2)}) %collective-permute-start.1) | collective-permute-done | bytes 32800 | tf_op jit(solution)/shard_map/ppermute | solution.py:342
  66.7 2.3 %collective-permute-done.2.p3_ref = bf16[2,64,128]{2,1,0:T(8,128)(2,1)S(1)} collective-permute-done((bf16[2,64,128]{2,1,0:T(8,128)(2,1)S(1)}, bf16[2,64,128]{2,1,0:T(8,128)(2,1)S(1)}, u32[]{:S(2)}, u32[]{:S(2)}) %collective-permute-start.2) | collective-permute-done | bytes 32800 | tf_op jit(solution)/shard_map/ppermute | solution.py:342
  69.0 0.0 collective-permute-done.3.p4_ref
  69.0 0.0 collective-permute-done.p1_ref
  69.0 0.8 all-to-all-done.1.zx_ref
  69.8 0.1 shard_map.77
  69.9 6.6 %shard_map.78 = (bf16[16,2,64,128]{3,2,1,0:T(8,128)(2,1)S(1)}, f32[2,1024,128]{2,1,0:T(8,128)S(1)}, bf16[2,640,128]{2,1,0:T(8,128)(2,1)S(1)}, bf16[2,256,128]{2,1,0:T(8,128)(2,1)S(1)}) custom-call(s32[1]{0:T(128)} %bitcast.place_ref, bf16[16,4,64,128]{3,2,1,0:T(8,128)(2,1)S(1)} %all-to-all-done.in_ref, bf16[2,768,128]{2,1,0:T(8,128)(2,1)S(1)} %get-tuple-element.21.pyr_ref, ...), custom_call_target="tpu_custom_call" | custom-call | flops 2000000000 | bytes 5242880 | tf_op jit(solution)/shard_map/pallas_call | solution.py:387
  76.6 0.9 shard_map.79
  77.4 8.7 %all-to-all-start.2 = ((bf16[32,2,32,128]{3,2,1,0:T(8,128)(2,1)}), bf16[32,2,32,128]{3,2,1,0:T(8,128)(2,1)S(1)}, u32[]{:S(2)}, u32[]{:S(2)}) async-start(bf16[32,2,32,128]{3,2,1,0:T(8,128)(2,1)} %get-tuple-element.33), calls=%async_computation.2 | async-start | bytes 1048576 | tf_op jit(solution)/shard_map/all_to_all | solution.py:331
  86.1 2.8 %collective-permute-start.4 = (bf16[2,256,128]{2,1,0:T(8,128)(2,1)S(1)}, bf16[2,256,128]{2,1,0:T(8,128)(2,1)S(1)}, u32[]{:S(2)}, u32[]{:S(2)}) collective-permute-start(bf16[2,256,128]{2,1,0:T(8,128)(2,1)S(1)} %get-tuple-element.34), channel_id=1, source_target_pairs={{0,16},{16,0},{32,48},{48,32},{1,17},{17,1},{33,49},{49,33},{2,18}... | collective-permute-start | bytes 393224 | tf_op jit(solution)/shard_map/ppermute | solution.py:342
  88.9 4.0 %collective-permute-start.7 = (bf16[2,128,128]{2,1,0:T(8,128)(2,1)S(1)}, bf16[2,128,128]{2,1,0:T(8,128)(2,1)S(1)}, u32[]{:S(2)}, u32[]{:S(2)}) collective-permute-start(bf16[2,128,128]{2,1,0:T(8,128)(2,1)S(1)} %get-tuple-element.37), channel_id=1, source_target_pairs={{16,32},{32,16},{48,64},{64,48},{80,96},{96,80},{112,128},{128,112... | collective-permute-start | bytes 196616 | tf_op jit(solution)/shard_map/ppermute | solution.py:346
  92.9 3.1 %collective-permute-start.5 = (bf16[2,64,128]{2,1,0:T(8,128)(2,1)S(1)}, bf16[2,64,128]{2,1,0:T(8,128)(2,1)S(1)}, u32[]{:S(2)}, u32[]{:S(2)}) collective-permute-start(bf16[2,64,128]{2,1,0:T(8,128)(2,1)S(1)} %get-tuple-element.35), channel_id=1, source_target_pairs={{0,32},{16,48},{32,0},{48,16},{1,33},{17,49},{33,1},{49,17},{2,34}... | collective-permute-start | bytes 98312 | tf_op jit(solution)/shard_map/ppermute | solution.py:342
  95.9 2.5 %collective-permute-start.6 = (bf16[2,64,128]{2,1,0:T(8,128)(2,1)S(1)}, bf16[2,64,128]{2,1,0:T(8,128)(2,1)S(1)}, u32[]{:S(2)}, u32[]{:S(2)}) collective-permute-start(bf16[2,64,128]{2,1,0:T(8,128)(2,1)S(1)} %get-tuple-element.36), channel_id=1, source_target_pairs={{0,48},{16,32},{32,16},{48,0},{1,49},{17,33},{33,17},{49,1},{2,50}... | collective-permute-start | bytes 98312 | tf_op jit(solution)/shard_map/ppermute | solution.py:342
  98.5 1.9 %collective-permute-done.5.p2_ref = bf16[2,64,128]{2,1,0:T(8,128)(2,1)S(1)} collective-permute-done((bf16[2,64,128]{2,1,0:T(8,128)(2,1)S(1)}, bf16[2,64,128]{2,1,0:T(8,128)(2,1)S(1)}, u32[]{:S(2)}, u32[]{:S(2)}) %collective-permute-start.5) | collective-permute-done | bytes 32800 | tf_op jit(solution)/shard_map/ppermute | solution.py:342
  100.4 2.6 %collective-permute-done.6.p3_ref = bf16[2,64,128]{2,1,0:T(8,128)(2,1)S(1)} collective-permute-done((bf16[2,64,128]{2,1,0:T(8,128)(2,1)S(1)}, bf16[2,64,128]{2,1,0:T(8,128)(2,1)S(1)}, u32[]{:S(2)}, u32[]{:S(2)}) %collective-permute-start.6) | collective-permute-done | bytes 32800 | tf_op jit(solution)/shard_map/ppermute | solution.py:342
  103.0 0.0 collective-permute-done.7.p4_ref
  103.0 0.0 collective-permute-done.4.p1_ref
  103.0 0.0 all-to-all-done.2.zx_ref
  103.0 0.4 shard_map.80
  103.4 32.0 %all_to_all.20.in_ref = bf16[16,4,64,128]{3,2,1,0:T(8,128)(2,1)S(1)} all-to-all(bf16[16,4,64,128]{3,2,1,0:T(8,128)(2,1)S(1)} %shard_map.80), channel_id=1, replica_groups=mesh['z'=8,'x'=4,'y_lo'=4,'y_hi'=2,'core'=2] {'y_lo','y_hi','core'}, dimensions={0} | all-to-all | bytes 2097152 | tf_op jit(solution)/shard_map/all_to_all | solution.py:331
  135.3 1.0 shard_map.81
Async XLA Ops:
  2.7 34.8 %all-to-all-start = ((bf16[16,4,64,128]{3,2,1,0:T(8,128)(2,1)}), bf16[16,4,64,128]{3,2,1,0:T(8,128)(2,1)S(1)}, u32[]{:S(2)}, u32[]{:S(2)}) async-start(bf16[16,4,64,128]{3,2,1,0:T(8,128)(2,1)} %shard_map.75), calls=%async_computation | async-start | bytes 2097152 | tf_op jit(solution)/shard_map/all_to_all | solution.py:331
  38.7 31.1 %all-to-all-start.1 = ((bf16[32,2,32,128]{3,2,1,0:T(8,128)(2,1)}), bf16[32,2,32,128]{3,2,1,0:T(8,128)(2,1)S(1)}, u32[]{:S(2)}, u32[]{:S(2)}) async-start(bf16[32,2,32,128]{3,2,1,0:T(8,128)(2,1)} %get-tuple-element.22), calls=%async_computation.1 | async-start | bytes 1048576 | tf_op jit(solution)/shard_map/all_to_all | solution.py:331
  52.1 16.9 %collective-permute-start = (bf16[2,256,128]{2,1,0:T(8,128)(2,1)S(1)}, bf16[2,256,128]{2,1,0:T(8,128)(2,1)S(1)}, u32[]{:S(2)}, u32[]{:S(2)}) collective-permute-start(bf16[2,256,128]{2,1,0:T(8,128)(2,1)S(1)} %get-tuple-element.23), channel_id=1, source_target_pairs={{0,16},{16,0},{32,48},{48,32},{1,17},{17,1},{33,49},{49,33},{2,18}... | collective-permute-start | bytes 393224 | tf_op jit(solution)/shard_map/ppermute | solution.py:342
  54.9 14.1 %collective-permute-start.3 = (bf16[2,128,128]{2,1,0:T(8,128)(2,1)S(1)}, bf16[2,128,128]{2,1,0:T(8,128)(2,1)S(1)}, u32[]{:S(2)}, u32[]{:S(2)}) collective-permute-start(bf16[2,128,128]{2,1,0:T(8,128)(2,1)S(1)} %get-tuple-element.26), channel_id=1, source_target_pairs={{16,32},{32,16},{48,64},{64,48},{80,96},{96,80},{112,128},{128,112... | collective-permute-start | bytes 196616 | tf_op jit(solution)/shard_map/ppermute | solution.py:346
  58.9 7.8 %collective-permute-start.1 = (bf16[2,64,128]{2,1,0:T(8,128)(2,1)S(1)}, bf16[2,64,128]{2,1,0:T(8,128)(2,1)S(1)}, u32[]{:S(2)}, u32[]{:S(2)}) collective-permute-start(bf16[2,64,128]{2,1,0:T(8,128)(2,1)S(1)} %get-tuple-element.24), channel_id=1, source_target_pairs={{0,32},{16,48},{32,0},{48,16},{1,33},{17,49},{33,1},{49,17},{2,34}... | collective-permute-start | bytes 98312 | tf_op jit(solution)/shard_map/ppermute | solution.py:342
  62.0 7.0 %collective-permute-start.2 = (bf16[2,64,128]{2,1,0:T(8,128)(2,1)S(1)}, bf16[2,64,128]{2,1,0:T(8,128)(2,1)S(1)}, u32[]{:S(2)}, u32[]{:S(2)}) collective-permute-start(bf16[2,64,128]{2,1,0:T(8,128)(2,1)S(1)} %get-tuple-element.25), channel_id=1, source_target_pairs={{0,48},{16,32},{32,16},{48,0},{1,49},{17,33},{33,17},{49,1},{2,50}... | collective-permute-start | bytes 98312 | tf_op jit(solution)/shard_map/ppermute | solution.py:342
  77.4 25.5 %all-to-all-start.2 = ((bf16[32,2,32,128]{3,2,1,0:T(8,128)(2,1)}), bf16[32,2,32,128]{3,2,1,0:T(8,128)(2,1)S(1)}, u32[]{:S(2)}, u32[]{:S(2)}) async-start(bf16[32,2,32,128]{3,2,1,0:T(8,128)(2,1)} %get-tuple-element.33), calls=%async_computation.2 | async-start | bytes 1048576 | tf_op jit(solution)/shard_map/all_to_all | solution.py:331
  86.1 16.9 %collective-permute-start.4 = (bf16[2,256,128]{2,1,0:T(8,128)(2,1)S(1)}, bf16[2,256,128]{2,1,0:T(8,128)(2,1)S(1)}, u32[]{:S(2)}, u32[]{:S(2)}) collective-permute-start(bf16[2,256,128]{2,1,0:T(8,128)(2,1)S(1)} %get-tuple-element.34), channel_id=1, source_target_pairs={{0,16},{16,0},{32,48},{48,32},{1,17},{17,1},{33,49},{49,33},{2,18}... | collective-permute-start | bytes 393224 | tf_op jit(solution)/shard_map/ppermute | solution.py:342
  88.9 14.1 %collective-permute-start.7 = (bf16[2,128,128]{2,1,0:T(8,128)(2,1)S(1)}, bf16[2,128,128]{2,1,0:T(8,128)(2,1)S(1)}, u32[]{:S(2)}, u32[]{:S(2)}) collective-permute-start(bf16[2,128,128]{2,1,0:T(8,128)(2,1)S(1)} %get-tuple-element.37), channel_id=1, source_target_pairs={{16,32},{32,16},{48,64},{64,48},{80,96},{96,80},{112,128},{128,112... | collective-permute-start | bytes 196616 | tf_op jit(solution)/shard_map/ppermute | solution.py:346
  92.9 7.5 %collective-permute-start.5 = (bf16[2,64,128]{2,1,0:T(8,128)(2,1)S(1)}, bf16[2,64,128]{2,1,0:T(8,128)(2,1)S(1)}, u32[]{:S(2)}, u32[]{:S(2)}) collective-permute-start(bf16[2,64,128]{2,1,0:T(8,128)(2,1)S(1)} %get-tuple-element.35), channel_id=1, source_target_pairs={{0,32},{16,48},{32,0},{48,16},{1,33},{17,49},{33,1},{49,17},{2,34}... | collective-permute-start | bytes 98312 | tf_op jit(solution)/shard_map/ppermute | solution.py:342
  95.9 7.0 %collective-permute-start.6 = (bf16[2,64,128]{2,1,0:T(8,128)(2,1)S(1)}, bf16[2,64,128]{2,1,0:T(8,128)(2,1)S(1)}, u32[]{:S(2)}, u32[]{:S(2)}) collective-permute-start(bf16[2,64,128]{2,1,0:T(8,128)(2,1)S(1)} %get-tuple-element.36), channel_id=1, source_target_pairs={{0,48},{16,32},{32,16},{48,0},{1,49},{17,33},{33,17},{49,1},{2,50}... | collective-permute-start | bytes 98312 | tf_op jit(solution)/shard_map/ppermute | solution.py:342

commit v4 on v3

--- a/solution.py
+++ b/solution.py
@@ -56,15 +56,15 @@
     return jax.ShapeDtypeStruct(dims, dtype)
 
 
-def pack_body(q_ref, k_ref, v_ref, d_ref, out_ref, held, packed, in_sem, out_sem):
-    refs = (q_ref, k_ref, v_ref, d_ref)
+def pack_body(a_ref, b_ref, out_ref, held, packed, in_sem, out_sem):
+    refs = (a_ref, b_ref)
     loads = [pltpu.make_async_copy(ref, held.at[i], in_sem.at[i]) for i, ref in enumerate(refs)]
     stores = [
-        pltpu.make_async_copy(packed.at[i], out_ref.at[:, i], out_sem.at[i]) for i in range(4)
+        pltpu.make_async_copy(packed.at[i], out_ref.at[:, i], out_sem.at[i]) for i in range(2)
     ]
     for load in loads:
         load.start()
-    for i in range(4):
+    for i in range(2):
         loads[i].wait()
         for h in range(HEADS):
             packed[i, h] = held[i, :, h * DH : (h + 1) * DH]
@@ -95,11 +95,12 @@
     return jnp.concatenate([x, jnp.zeros((rows - x.shape[0], DH), x.dtype)], axis=0)
 
 
-def pyramid_body(place_ref, in_ref, pyr_ref, zx_ref, p1_ref, p2_ref, p3_ref, p4_ref, buf):
+def pyramid_body(place_ref, in_ref, pyr_ref, z_ref, p1_ref, p2_ref, p4_ref, buf):
     s = place_ref[0]
+    z = s // 4
     odd = lax.rem(s, 2)
     for i in range(2):
-        buf[...] = in_ref[:, 1 + i].reshape(TOKENS, DH).astype(F32)
+        buf[...] = in_ref[:, i].reshape(TOKENS, DH).astype(F32)
         count = TOKENS
         levels = {}
         for level in range(1, 8):
@@ -115,38 +116,49 @@
         pyr_ref[i, 512:768] = levels[2].astype(BF)
         p1_ref[i, 0:128] = levels[3].astype(BF)
         p2_ref[i] = levels[4].astype(BF)
-        p3_ref[i] = levels[4].astype(BF)
-        for bit, level in ((2, 5), (3, 6), (4, 7)):
-            rows = pad_rows(levels[level], CHUNK).astype(BF)
+        z_ref[z, i] = jnp.zeros((CHUNK, DH), BF)
+        for bit in range(3):
+            rows = pad_rows(levels[5 + bit], CHUNK).astype(BF)
             for d in range(1 << bit, 2 << bit):
-                zx_ref[jnp.bitwise_xor(s, d), i] = rows
-        for d in range(4):
-            zx_ref[jnp.bitwise_xor(s, d), i] = jnp.zeros((CHUNK, DH), BF)
-        first = in_ref[0:2, 1 + i].reshape(BLOCK, DH)
-        last = in_ref[14:16, 1 + i].reshape(BLOCK, DH)
-        near = jnp.where(odd == 1, first, last)
-        other = jnp.where(odd == 1, last, first)
-        p1_ref[i, 128:256] = near
-        p4_ref[i] = other
-
-
-def merge_body(place_ref, zx_ref, p1_ref, p2_ref, p3_ref, p4_ref, rem_ref, edge_ref):
-    s = place_ref[0]
-    odd = lax.rem(s, 2) == 1
+                z_ref[jnp.bitwise_xor(z, d), i] = rows
+        first = in_ref[0:2, i].reshape(BLOCK, DH)
+        last = in_ref[14:16, i].reshape(BLOCK, DH)
+        p1_ref[i, 128:256] = jnp.where(odd == 1, first, last)
+        p4_ref[i] = jnp.where(odd == 1, last, first)
+
+
+def join_body(place_ref, z_ref, p1_ref, p2_ref, own_ref, out1_ref, out2_ref):
+    z = place_ref[0] // 4
+    for i in range(2):
+        for bit in range(3):
+            parts = [
+                z_ref[jnp.bitwise_xor(z, d), i].astype(F32)[0 : CHUNK >> bit]
+                for d in range(1 << bit, 2 << bit)
+            ]
+            rows = parts[0] if bit == 0 else jnp.concatenate(parts, axis=0)
+            own_ref[i, bit * CHUNK : (bit + 1) * CHUNK] = rows.astype(BF)
+        out1_ref[i, 0:256] = p1_ref[i]
+        out1_ref[i, 256:352] = own_ref[i]
+        out2_ref[i, 0:64] = p2_ref[i]
+        out2_ref[i, 64:160] = own_ref[i]
+
+
+def merge_body(place_ref, own_ref, p1_ref, p2_ref, p3_ref, p4_ref, rem_ref, edge_ref):
+    odd = lax.rem(place_ref[0], 2) == 1
     for i in range(2):
         near = p1_ref[i, 128:256]
         other = p4_ref[i]
         edge_ref[i, 0:128] = jnp.where(odd, near, other)
         edge_ref[i, 128:256] = jnp.where(odd, other, near)
         rem_ref[i, 0:128] = p1_ref[i, 0:128]
-        rem_ref[i, 128:192] = p2_ref[i]
-        rem_ref[i, 192:256] = p3_ref[i]
-        for bit, base in ((2, 256), (3, 384), (4, 512)):
-            rows = BLOCK >> bit
-            parts = []
-            for d in range(1 << bit, 2 << bit):
-                parts.append(zx_ref[jnp.bitwise_xor(s, d), i].astype(F32)[0:rows])
-            rem_ref[i, base : base + 128] = jnp.concatenate(parts, axis=0).astype(BF)
+        rem_ref[i, 128:192] = p2_ref[i, 0:64]
+        rem_ref[i, 192:256] = p3_ref[i, 0:64]
+        for e, (ref, base) in enumerate(((own_ref, 0), (p1_ref, 256), (p2_ref, 64), (p3_ref, 64))):
+            for bit in range(3):
+                start = 256 + bit * BLOCK + e * CHUNK
+                rem_ref[i, start : start + CHUNK] = ref[
+                    i, base + bit * CHUNK : base + (bit + 1) * CHUNK
+                ]
 
 
 def part_body(place_ref, drem_ref, dedge_ref, bzx_ref, b1_ref, b2_ref, b3_ref, b4_ref):
@@ -162,19 +174,22 @@
         b4_ref[i] = jnp.where(odd, right, left)
         for d in range(4):
             bzx_ref[jnp.bitwise_xor(s, d), i] = jnp.zeros((CHUNK, DH), BF)
-        for bit, base in ((2, 256), (3, 384), (4, 512)):
-            rows = BLOCK >> bit
-            block = drem_ref[i, base : base + 128].astype(F32)
+        for bit in range(3):
+            count = CHUNK >> bit
+            base = 256 + bit * BLOCK
+            block = drem_ref[i, base : base + BLOCK].astype(F32)
             for d in range(1 << bit, 2 << bit):
-                start = (d - (1 << bit)) * rows
-                bzx_ref[jnp.bitwise_xor(s, d), i] = pad_rows(
-                    block[start : start + rows], CHUNK
-                ).astype(BF)
+                for e in range(4):
+                    start = e * CHUNK + (d - (1 << bit)) * count
+                    bzx_ref[jnp.bitwise_xor(s, 4 * d + e), i] = pad_rows(
+                        block[start : start + count], CHUNK
+                    ).astype(BF)
 
 
 def attend_body(
     place_ref,
-    in_ref,
+    kv_ref,
+    qd_ref,
     pyr_ref,
     rem,
     edge_ref,
@@ -191,49 +206,67 @@
     s = place_ref[0]
     for i in range(2):
         win[i, 0:128] = edge_ref[i, 0:128]
-        win[i, 128:1152] = in_ref[:, 1 + i].reshape(TOKENS, DH)
+        win[i, 128:1152] = kv_ref[:, i].reshape(TOKENS, DH)
         win[i, 1152:1280] = edge_ref[i, 128:256]
-    dwin[...] = jnp.zeros_like(dwin)
-    drem[...] = jnp.zeros_like(drem)
-    dpyr[...] = jnp.zeros_like(dpyr)
+    written = set()
+
+    def accumulate(ref, rows, key_grad, value_grad):
+        for base in range(rows.start, rows.stop, BLOCK):
+            block = slice(base, base + BLOCK)
+            part = slice(base - rows.start, base - rows.start + BLOCK)
+            for i, grad in enumerate((key_grad, value_grad)):
+                if (id(ref), base) in written:
+                    ref[i, block] += grad[part]
+                else:
+                    ref[i, block] = grad[part]
+            written.add((id(ref), base))
+
     second = lax.broadcasted_iota(jnp.int32, (1, 2 * BLOCK), 1) >= BLOCK
+    halves = (slice(0, BLOCK), slice(BLOCK, 2 * BLOCK))
 
     def products(p):
-        q = in_ref[4 * p : 4 * p + 4, 0].reshape(2 * BLOCK, DH)
-        dy = in_ref[4 * p : 4 * p + 4, 3].reshape(2 * BLOCK, DH)
+        q = qd_ref[4 * p : 4 * p + 4, 0].reshape(2 * BLOCK, DH)
+        dy = qd_ref[4 * p : 4 * p + 4, 1].reshape(2 * BLOCK, DH)
         one = (p ^ 1) * BLOCK
         two = 512 + ((p // 2) ^ 1) * BLOCK
+        outer = [slice((2 * p + n) * BLOCK, (2 * p + n + 1) * BLOCK) for n in (0, 3)]
         groups = (
-            (win, dwin, slice(2 * p * BLOCK, (2 * p + 4) * BLOCK), (0, 0, 0, 0)),
+            (win, dwin, slice((2 * p + 1) * BLOCK, (2 * p + 3) * BLOCK), (0, 0)),
             (pyr_ref, dpyr, slice(one, one + BLOCK), (1,)),
             (pyr_ref, dpyr, slice(two, two + BLOCK), (2,)),
             (rem, drem, slice(0, 640), (3, 4, 5, 6, 7)),
         )
-        raws = [dot(ref[0, rows], q, NT) for ref, _, rows, _ in groups]
-        pushes = [dot(ref[1, rows], dy, NT) for ref, _, rows, _ in groups]
-        return q, dy, groups, raws, pushes
+
+        def scored(i, other):
+            tiles = [dot(win[i, rows], other[half], NT) for rows, half in zip(outer, halves)]
+            return [jnp.concatenate(tiles, axis=1)] + [
+                dot(ref[i, rows], other, NT) for ref, _, rows, _ in groups
+            ]
+
+        return q, dy, outer, groups, scored(0, q), scored(1, dy)
 
     def softmax(p, state):
-        _, _, groups, raws, _ = state
-        first_gap = jnp.where(second, NEG_FILL, 0.0).astype(F32)
-        last_gap = jnp.where(second, 0.0, NEG_FILL).astype(F32)
+        _, _, _, groups, raws, _ = state
+        raws = list(raws)
         if p == 0:
-            first_gap = jnp.where(s == 0, NEG_FILL, first_gap)
+            raws[0] = raws[0] + jnp.where(
+                jnp.logical_and(s == 0, jnp.logical_not(second)), NEG_FILL, 0.0
+            ).astype(F32)
         if p == BLOCKS // 2 - 1:
-            last_gap = jnp.where(s == RANKS - 1, NEG_FILL, last_gap)
+            raws[0] = raws[0] + jnp.where(
+                jnp.logical_and(s == RANKS - 1, second), NEG_FILL, 0.0
+            ).astype(F32)
         score = []
         top = None
-        for raw, (_, _, _, shifts) in zip(raws, groups):
+        every = [(0,)] + [shifts for _, _, _, shifts in groups]
+        for raw, shifts in zip(raws, every):
             blocks = [raw[n * BLOCK : (n + 1) * BLOCK] for n in range(len(shifts))]
-            if len(shifts) == 4:
-                blocks[0] = blocks[0] + first_gap
-                blocks[3] = blocks[3] + last_gap
             for item, shift in zip(blocks, shifts):
                 peak = jnp.max(item, axis=0, keepdims=True) * SCALE_2 + float(shift)
                 top = peak if top is None else jnp.maximum(top, peak)
             score.append(blocks)
         total = jnp.zeros((1, 2 * BLOCK), F32)
-        for blocks, (_, _, _, shifts) in zip(score, groups):
+        for blocks, shifts in zip(score, every):
             for n, shift in enumerate(shifts):
                 blocks[n] = jnp.exp2(blocks[n] * SCALE_2 + (float(shift) - top))
                 total = total + jnp.sum(blocks[n], axis=0, keepdims=True)
@@ -242,7 +275,7 @@
         return score, [item.astype(BF) for item in score]
 
     def gradients(p, state, weights):
-        q, dy, groups, _, pushes = state
+        q, dy, outer, groups, _, pushes = state
         score, light = weights
         slots = slice(4 * p, 4 * p + 4)
         tall = None
@@ -251,14 +284,21 @@
                 term = item[n : n + BLOCK] * pushed[n : n + BLOCK]
                 tall = term if tall is None else tall + term
         delta = jnp.sum(tall, axis=0, keepdims=True)
-        out = jnp.zeros((2 * BLOCK, DH), F32)
-        dq = jnp.zeros((2 * BLOCK, DH), F32)
-        for (ref, dref, rows, _), item, item_light, pushed in zip(groups, score, light, pushes):
+        grads = [(item * (pushed - delta)).astype(BF) for item, pushed in zip(score, pushes)]
+        out = []
+        dq = []
+        for rows, half in zip(outer, halves):
+            out.append(dot(light[0][:, half], win[1, rows], TN))
+            dq.append(dot(grads[0][:, half], win[0, rows], TN))
+            accumulate(
+                dwin, rows, dot(grads[0][:, half], q[half]), dot(light[0][:, half], dy[half])
+            )
+        out = jnp.concatenate(out, axis=0)
+        dq = jnp.concatenate(dq, axis=0)
+        for (ref, dref, rows, _), item_light, grad in zip(groups, light[1:], grads[1:]):
             out = out + dot(item_light, ref[1, rows], TN)
-            grad = (item * (pushed - delta)).astype(BF)
             dq = dq + dot(grad, ref[0, rows], TN)
-            dref[0, rows] += dot(grad, q)
-            dref[1, rows] += dot(item_light, dy)
+            accumulate(dref, rows, dot(grad, q), dot(item_light, dy))
         out_ref[slots, 0] = out.astype(BF).reshape(4, TOKENS_IN, DH)
         out_ref[slots, 1] = (dq * SCALE).astype(BF).reshape(4, TOKENS_IN, DH)
 
@@ -338,60 +378,59 @@
     return pairs
 
 
-def exchange(zx, p1, p2, p3, p4):
-    flip = lambda array, mask: lax.ppermute(array, "x", [(i, i ^ mask) for i in range(4)])
-    p1 = flip(p1, 1)
-    p2 = flip(p2, 2)
-    p3 = flip(p3, 3)
-    p4 = lax.ppermute(p4, SEQ_AXES, odd_pairs(RANKS))
-    return swap(zx, SEQ_AXES), p1, p2, p3, p4
+def flip(array, mask):
+    return lax.ppermute(array, "x", [(i, i ^ mask) for i in range(4)])
+
+
+def after(array, other):
+    return lax.optimization_barrier((array, other))
 
 
 def on_device(queries, keys, values, cotangent):
     place = (lax.axis_index("z") * 4 + lax.axis_index("x")).reshape(1).astype(jnp.int32)
     mb = 1 << 20
-    messages = [
-        shape(RANKS, 2, CHUNK, DH),
-        shape(2, 256, DH),
-        shape(2, 64, DH),
-        shape(2, 64, DH),
-        shape(2, 128, DH),
-    ]
-    split = shape(HEADS, 4, TOKENS_IN, DH)
-    packed = kernel_call(
+    dma = pltpu.SemaphoreType.DMA
+    half = shape(HEADS, 2, TOKENS_IN, DH)
+    along_z = shape(8, 2, CHUNK, DH)
+    first, second, block = shape(2, 352, DH), shape(2, 160, DH), shape(2, BLOCK, DH)
+    own_rows, far_rows, edges = shape(2, 96, DH), shape(2, 640, DH), shape(2, 256, DH)
+    pack = kernel_call(
         pack_body,
-        [HBM] * 4,
-        [(HBM, split)],
+        [HBM] * 2,
+        [(HBM, half)],
         scratch=[
-            VMEM((4, TOKENS_IN, HEADS * DH), BF),
-            VMEM((4, HEADS, TOKENS_IN, DH), BF),
-            pltpu.SemaphoreType.DMA((4,)),
-            pltpu.SemaphoreType.DMA((4,)),
+            VMEM((2, TOKENS_IN, HEADS * DH), BF),
+            VMEM((2, HEADS, TOKENS_IN, DH), BF),
+            dma((2,)),
+            dma((2,)),
         ],
         mib=LARGE,
-        bytes_accessed=2 * mb,
-    )(queries, keys, values, cotangent)
-    mine = swap(packed, HEAD_AXES)
-    pyr, *sent = kernel_call(
+        bytes_accessed=mb,
+    )
+    packed_kv = pack(keys, values)
+    packed_qd = pack(queries, cotangent)
+    kv, packed_qd = after(swap(packed_kv, HEAD_AXES), packed_qd)
+    pyr, sent_z, p1, p2, p4 = kernel_call(
         pyramid_body,
         [SMEM, VMEM],
-        [(VMEM, shape(2, 768, DH))] + [(VMEM, item) for item in messages],
+        [(VMEM, item) for item in (shape(2, 768, DH), along_z, edges, shape(2, 64, DH), block)],
         scratch=[VMEM((TOKENS, DH), F32)],
         bytes_accessed=2 * mb,
-    )(place, mine)
-    got = exchange(*sent)
-    rows = [shape(2, 640, DH), shape(2, 256, DH)]
-    far = kernel_call(merge_body, [SMEM] + [VMEM] * 5, [(VMEM, item) for item in rows])(
-        place, *got
-    )
+    )(place, kv)
+    p4 = lax.ppermute(p4, SEQ_AXES, odd_pairs(RANKS))
+    got_z = swap(sent_z, "z")
+    packed_qd, got_z = after(packed_qd, got_z)
+    own, p1, p2 = kernel_call(
+        join_body, [SMEM] + [VMEM] * 3, [(VMEM, item) for item in (own_rows, first, second)]
+    )(place, got_z, p1, p2)
+    qd = swap(packed_qd, HEAD_AXES)
+    far = kernel_call(
+        merge_body, [SMEM] + [VMEM] * 5, [(VMEM, item) for item in (far_rows, edges)]
+    )(place, own, flip(p1, 1), flip(p2, 2), flip(p2, 3), p4)
     out, dkv, *grads = kernel_call(
         attend_body,
-        [SMEM] + [VMEM] * 4,
-        [
-            (VMEM, shape(HEADS, 2, TOKENS_IN, DH)),
-            (VMEM, shape(2, TOKENS, DH, dtype=F32)),
-        ]
-        + [(VMEM, item) for item in rows],
+        [SMEM] + [VMEM] * 5,
+        [(VMEM, half), (VMEM, shape(2, TOKENS, DH, dtype=F32)), (VMEM, far_rows), (VMEM, edges)],
         scratch=[
             VMEM((2, 1280, DH), BF),
             VMEM((2, 1280, DH), F32),
@@ -402,18 +441,22 @@
         mib=MIDDLE,
         flops=2 * 10**9,
         bytes_accessed=5 * mb,
-    )(place, mine, pyr, *far)
-    back = kernel_call(part_body, [SMEM] + [VMEM] * 2, [(VMEM, item) for item in messages])(
-        place, *grads
-    )
-    returned = exchange(*back)
+    )(place, kv, qd, pyr, *far)
+    small = shape(2, 64, DH)
+    zx, b1, b2, b3, b4 = kernel_call(
+        part_body,
+        [SMEM] + [VMEM] * 2,
+        [(VMEM, item) for item in (shape(RANKS, 2, CHUNK, DH), edges, small, small, block)],
+    )(place, *grads)
+    b1, b2, b3 = flip(b1, 1), flip(b2, 2), flip(b3, 3)
+    b4 = lax.ppermute(b4, SEQ_AXES, odd_pairs(RANKS))
     packed = kernel_call(
         finish_body,
         [SMEM] + [VMEM] * 7,
-        [(VMEM, split)],
+        [(VMEM, shape(HEADS, 4, TOKENS_IN, DH))],
         scratch=[VMEM((TOKENS, DH), F32)],
         bytes_accessed=3 * mb,
-    )(place, out, dkv, *returned)
+    )(place, out, dkv, swap(zx, SEQ_AXES), b1, b2, b3, b4)
     results = swap(packed, HEAD_AXES)
     flat = shape(TOKENS_IN, HEADS * DH)
     return tuple(
@@ -421,7 +464,7 @@
             unpack_body,
             [VMEM],
             [(HBM, flat)] * 4,
-            scratch=[VMEM((4, TOKENS_IN, HEADS * DH), BF), pltpu.SemaphoreType.DMA((4,))],
+            scratch=[VMEM((4, TOKENS_IN, HEADS * DH), BF), dma((4,))],
             bytes_accessed=2 * mb,
         )(results)
     )

time: 138 us -> 137 us (level)
  blocking collectives: 32 us -> 54.9 us
  starting transfers between devices: 54 us -> 41.2 us
  waiting for transfers between devices: 37.4 us -> 25.5 us
    all_to_all x1 -> x2, blocking collectives: 32 us -> 54.9 us  [swap(): return lax.all_to_all(array, axes, split_axis=0, concat_axis=0, tiled=True)]
    all_to_all x3, waiting for transfers between devices: 28.5 us -> 15.2 us  [swap(): return lax.all_to_all(array, axes, split_axis=0, concat_axis=0, tiled=True)]
    all_to_all x3, starting transfers between devices: 29.3 us -> 16.5 us  [swap(): return lax.all_to_all(array, axes, split_axis=0, concat_axis=0, tiled=True)]
    pallas_call x6 -> x8, Pallas kernels: 11.2 us -> 11.7 us  [the longest x1 6.27 us: on_device(): kernel_call(attend_body, [SMEM] + [VMEM] * 5, [(VMEM, half), (VMEM, shape...]
  transfers between devices with their start and end apart: 11 -> 11, of which waited for: 6 -> 4; matrix products, arithmetic and copies ran while one was open for 0% -> 0% of each run, Pallas kernels for 0% -> 1%
where the time goes in v4:
time: 137 us; the launch traced here: 135 us
  blocking collectives  54.9 us (40%)
  starting transfers between devices  41.2 us (30%)
  waiting for transfers between devices  25.5 us (19%)
  Pallas kernels  12.7 us (9%)
    all_to_all x2, blocking collectives, swap(): return lax.all_to_all(array, axes, split_axis=0, concat_axis=0, tiled=True)  54.9 us
    ppermute x6, starting transfers between devices, flip(): return lax.ppermute(array, 'x', [(i, i ^ mask) for i in range(4)])  18.2 us
    all_to_all x3, starting transfers between devices, swap(): return lax.all_to_all(array, axes, split_axis=0, concat_axis=0, tiled=True)  16.5 us
    all_to_all x3, waiting for transfers between devices, swap(): return lax.all_to_all(array, axes, split_axis=0, concat_axis=0, tiled=True)  15.2 us
    pallas_call x1, Pallas kernels, on_device(): kernel_call(attend_body, [SMEM] + [VMEM] * 5, [(VMEM, half), (VMEM, shape...  6.27 us
    ppermute x1, waiting for transfers between devices, on_device(): p4 = lax.ppermute(p4, SEQ_AXES, odd_pairs(RANKS))  5.73 us
    ppermute x6, waiting for transfers between devices, flip(): return lax.ppermute(array, 'x', [(i, i ^ mask) for i in range(4)])  4.5 us
    ppermute x1, starting transfers between devices, on_device(): b4 = lax.ppermute(b4, SEQ_AXES, odd_pairs(RANKS))  3.98 us
  transfers between devices with their start and end apart: 11, of which 4 were waited for; matrix products, arithmetic and copies ran while one was open for 0% of the time, Pallas kernels for 1%

profile of v4, /device:TPU:6, one launch (start us, length us, event | category | flops | bytes accessed | tf_op | source)
XLA Modules:
  0.0 135.0 jit_solution(16880652946253403961)
XLA Ops:
  0.6 1.9 %shard_map.75 = bf16[16,2,64,128]{3,2,1,0:T(8,128)(2,1)} custom-call(bf16[64,2048]{1,0:T(8,128)(2,1)} %a_ref.2, bf16[64,2048]{1,0:T(8,128)(2,1)} %b_ref.2), custom_call_target="tpu_custom_call" | custom-call | bytes 1048576 | tf_op jit(solution)/shard_map/pallas_call | solution.py:410
  2.5 7.2 %all-to-all-start = ((bf16[16,2,64,128]{3,2,1,0:T(8,128)(2,1)}), bf16[16,2,64,128]{3,2,1,0:T(8,128)(2,1)S(1)}, u32[]{:S(2)}, u32[]{:S(2)}) async-start(bf16[16,2,64,128]{3,2,1,0:T(8,128)(2,1)} %shard_map.75), calls=%async_computation | async-start | bytes 1048576 | tf_op jit(solution)/shard_map/all_to_all | solution.py:371
  9.7 1.9 %shard_map.76 = bf16[16,2,64,128]{3,2,1,0:T(8,128)(2,1)} custom-call(bf16[64,2048]{1,0:T(8,128)(2,1)} %a_ref.3, bf16[64,2048]{1,0:T(8,128)(2,1)} %b_ref.3), custom_call_target="tpu_custom_call" | custom-call | bytes 1048576 | tf_op jit(solution)/shard_map/pallas_call | solution.py:411
  11.6 15.2 %all-to-all-done.in_ref.kv_ref = bf16[16,2,64,128]{3,2,1,0:T(8,128)(2,1)S(1)} async-done(((bf16[16,2,64,128]{3,2,1,0:T(8,128)(2,1)}), bf16[16,2,64,128]{3,2,1,0:T(8,128)(2,1)S(1)}, u32[]{:S(2)}, u32[]{:S(2)}) %all-to-all-start) | async-done | bytes 524320 | tf_op jit(solution)/shard_map/all_to_all | solution.py:371
  26.8 0.3 shard_map.77
  27.1 19.6 %all_to_all.25.z_ref = bf16[8,2,32,128]{3,2,1,0:T(8,128)(2,1)S(1)} all-to-all(bf16[8,2,32,128]{3,2,1,0:T(8,128)(2,1)S(1)} %get-tuple-element.29), channel_id=1, replica_groups=mesh['z'=8,'x'=4,'y_lo'=4,'y_hi'=2,'core'=2] {'z'}, dimensions={0} | all-to-all | bytes 262144 | tf_op jit(solution)/shard_map/all_to_all | solution.py:371
  46.8 3.6 %all-to-all-start.2 = ((bf16[16,2,64,128]{3,2,1,0:T(8,128)(2,1)}), bf16[16,2,64,128]{3,2,1,0:T(8,128)(2,1)S(1)}, u32[]{:S(2)}, u32[]{:S(2)}) async-start(bf16[16,2,64,128]{3,2,1,0:T(8,128)(2,1)} %shard_map.76), calls=%async_computation.2 | async-start | bytes 1048576 | tf_op jit(solution)/shard_map/all_to_all | solution.py:371
  50.4 2.7 %collective-permute-start = (bf16[2,352,128]{2,1,0:T(8,128)(2,1)S(1)}, bf16[2,352,128]{2,1,0:T(8,128)(2,1)S(1)}, u32[]{:S(2)}, u32[]{:S(2)}) collective-permute-start(bf16[2,352,128]{2,1,0:T(8,128)(2,1)S(1)} %get-tuple-element.36), channel_id=1, source_target_pairs={{0,16},{16,0},{32,48},{48,32},{1,17},{17,1},{33,49},{49,33},{2,18}... | collective-permute-start | bytes 540680 | tf_op jit(solution)/shard_map/ppermute | solution.py:382
  53.2 3.0 %collective-permute-start.2 = (bf16[2,160,128]{2,1,0:T(8,128)(2,1)S(1)}, bf16[2,160,128]{2,1,0:T(8,128)(2,1)S(1)}, u32[]{:S(2)}, u32[]{:S(2)}) collective-permute-start(bf16[2,160,128]{2,1,0:T(8,128)(2,1)S(1)} %get-tuple-element.37), channel_id=1, source_target_pairs={{0,48},{16,32},{32,16},{48,0},{1,49},{17,33},{33,17},{49,1},{2,50}... | collective-permute-start | bytes 245768 | tf_op jit(solution)/shard_map/ppermute | solution.py:382
  56.2 4.0 %collective-permute-start.1 = (bf16[2,160,128]{2,1,0:T(8,128)(2,1)S(1)}, bf16[2,160,128]{2,1,0:T(8,128)(2,1)S(1)}, u32[]{:S(2)}, u32[]{:S(2)}) collective-permute-start(bf16[2,160,128]{2,1,0:T(8,128)(2,1)S(1)} %get-tuple-element.37), channel_id=1, source_target_pairs={{0,32},{16,48},{32,0},{48,16},{1,33},{17,49},{33,1},{49,17},{2,34}... | collective-permute-start | bytes 245768 | tf_op jit(solution)/shard_map/ppermute | solution.py:382
  60.3 2.5 %collective-permute-start.3 = (bf16[2,128,128]{2,1,0:T(8,128)(2,1)S(1)}, bf16[2,128,128]{2,1,0:T(8,128)(2,1)S(1)}, u32[]{:S(2)}, u32[]{:S(2)}) collective-permute-start(bf16[2,128,128]{2,1,0:T(8,128)(2,1)S(1)} %get-tuple-element.38), channel_id=1, source_target_pairs={{16,32},{32,16},{48,64},{64,48},{80,96},{96,80},{112,128},{128,112... | collective-permute-start | bytes 196616 | tf_op jit(solution)/shard_map/ppermute | solution.py:420
  62.8 5.7 %collective-permute-done.3.p4_ref = bf16[2,128,128]{2,1,0:T(8,128)(2,1)S(1)} collective-permute-done((bf16[2,128,128]{2,1,0:T(8,128)(2,1)S(1)}, bf16[2,128,128]{2,1,0:T(8,128)(2,1)S(1)}, u32[]{:S(2)}, u32[]{:S(2)}) %collective-permute-start.3) | collective-permute-done | bytes 65568 | tf_op jit(solution)/shard_map/ppermute | solution.py:420
  68.5 0.0 collective-permute-done.2.p3_ref
  68.5 0.0 collective-permute-done.1.p2_ref
  68.5 0.0 collective-permute-done.p1_ref
  68.6 0.0 all-to-all-done.2.qd_ref
  68.6 6.3 %shard_map.80 = (bf16[16,2,64,128]{3,2,1,0:T(8,128)(2,1)S(1)}, f32[2,1024,128]{2,1,0:T(8,128)S(1)}, bf16[2,640,128]{2,1,0:T(8,128)(2,1)S(1)}, bf16[2,256,128]{2,1,0:T(8,128)(2,1)S(1)}) custom-call(s32[1]{0:T(128)} %bitcast.place_ref, bf16[16,2,64,128]{3,2,1,0:T(8,128)(2,1)S(1)} %all-to-all-done.in_ref.kv_ref, ...), custom_call_target="tpu_custom_call" | custom-call | flops 2000000000 | bytes 5242880 | tf_op jit(solution)/shard_map/pallas_call | solution.py:430
  74.9 0.9 shard_map.81
  75.8 5.7 %all-to-all-start.3 = ((bf16[32,2,32,128]{3,2,1,0:T(8,128)(2,1)}), bf16[32,2,32,128]{3,2,1,0:T(8,128)(2,1)S(1)}, u32[]{:S(2)}, u32[]{:S(2)}) async-start(bf16[32,2,32,128]{3,2,1,0:T(8,128)(2,1)} %get-tuple-element.45), calls=%async_computation.3 | async-start | bytes 1048576 | tf_op jit(solution)/shard_map/all_to_all | solution.py:371
  81.5 2.8 %collective-permute-start.4 = (bf16[2,256,128]{2,1,0:T(8,128)(2,1)S(1)}, bf16[2,256,128]{2,1,0:T(8,128)(2,1)S(1)}, u32[]{:S(2)}, u32[]{:S(2)}) collective-permute-start(bf16[2,256,128]{2,1,0:T(8,128)(2,1)S(1)} %get-tuple-element.46), channel_id=1, source_target_pairs={{0,16},{16,0},{32,48},{48,32},{1,17},{17,1},{33,49},{49,33},{2,18}... | collective-permute-start | bytes 393224 | tf_op jit(solution)/shard_map/ppermute | solution.py:382
  84.3 4.0 %collective-permute-start.7 = (bf16[2,128,128]{2,1,0:T(8,128)(2,1)S(1)}, bf16[2,128,128]{2,1,0:T(8,128)(2,1)S(1)}, u32[]{:S(2)}, u32[]{:S(2)}) collective-permute-start(bf16[2,128,128]{2,1,0:T(8,128)(2,1)S(1)} %get-tuple-element.49), channel_id=1, source_target_pairs={{16,32},{32,16},{48,64},{64,48},{80,96},{96,80},{112,128},{128,112... | collective-permute-start | bytes 196616 | tf_op jit(solution)/shard_map/ppermute | solution.py:452
  88.3 3.1 %collective-permute-start.5 = (bf16[2,64,128]{2,1,0:T(8,128)(2,1)S(1)}, bf16[2,64,128]{2,1,0:T(8,128)(2,1)S(1)}, u32[]{:S(2)}, u32[]{:S(2)}) collective-permute-start(bf16[2,64,128]{2,1,0:T(8,128)(2,1)S(1)} %get-tuple-element.47), channel_id=1, source_target_pairs={{0,32},{16,48},{32,0},{48,16},{1,33},{17,49},{33,1},{49,17},{2,34}... | collective-permute-start | bytes 98312 | tf_op jit(solution)/shard_map/ppermute | solution.py:382
  91.3 2.5 %collective-permute-start.6 = (bf16[2,64,128]{2,1,0:T(8,128)(2,1)S(1)}, bf16[2,64,128]{2,1,0:T(8,128)(2,1)S(1)}, u32[]{:S(2)}, u32[]{:S(2)}) collective-permute-start(bf16[2,64,128]{2,1,0:T(8,128)(2,1)S(1)} %get-tuple-element.48), channel_id=1, source_target_pairs={{0,48},{16,32},{32,16},{48,0},{1,49},{17,33},{33,17},{49,1},{2,50}... | collective-permute-start | bytes 98312 | tf_op jit(solution)/shard_map/ppermute | solution.py:382
  93.9 1.7 %collective-permute-done.5.p2_ref = bf16[2,64,128]{2,1,0:T(8,128)(2,1)S(1)} collective-permute-done((bf16[2,64,128]{2,1,0:T(8,128)(2,1)S(1)}, bf16[2,64,128]{2,1,0:T(8,128)(2,1)S(1)}, u32[]{:S(2)}, u32[]{:S(2)}) %collective-permute-start.5) | collective-permute-done | bytes 32800 | tf_op jit(solution)/shard_map/ppermute | solution.py:382
  95.6 2.8 %collective-permute-done.6.p3_ref = bf16[2,64,128]{2,1,0:T(8,128)(2,1)S(1)} collective-permute-done((bf16[2,64,128]{2,1,0:T(8,128)(2,1)S(1)}, bf16[2,64,128]{2,1,0:T(8,128)(2,1)S(1)}, u32[]{:S(2)}, u32[]{:S(2)}) %collective-permute-start.6) | collective-permute-done | bytes 32800 | tf_op jit(solution)/shard_map/ppermute | solution.py:382
  98.4 0.0 collective-permute-done.7.p4_ref
  98.4 0.0 collective-permute-done.4.p1_ref
  98.4 0.0 all-to-all-done.3.zx_ref
  98.4 0.4 shard_map.82
  98.8 35.2 %all_to_all.26.in_ref = bf16[16,4,64,128]{3,2,1,0:T(8,128)(2,1)S(1)} all-to-all(bf16[16,4,64,128]{3,2,1,0:T(8,128)(2,1)S(1)} %shard_map.82), channel_id=1, replica_groups=mesh['z'=8,'x'=4,'y_lo'=4,'y_hi'=2,'core'=2] {'y_lo','y_hi','core'}, dimensions={0} | all-to-all | bytes 2097152 | tf_op jit(solution)/shard_map/all_to_all | solution.py:371
  134.0 1.0 shard_map.83
  (2 shorter events, 0.1 us)
Async XLA Ops:
  2.5 24.3 %all-to-all-start = ((bf16[16,2,64,128]{3,2,1,0:T(8,128)(2,1)}), bf16[16,2,64,128]{3,2,1,0:T(8,128)(2,1)S(1)}, u32[]{:S(2)}, u32[]{:S(2)}) async-start(bf16[16,2,64,128]{3,2,1,0:T(8,128)(2,1)} %shard_map.75), calls=%async_computation | async-start | bytes 1048576 | tf_op jit(solution)/shard_map/all_to_all | solution.py:371
  46.8 21.8 %all-to-all-start.2 = ((bf16[16,2,64,128]{3,2,1,0:T(8,128)(2,1)}), bf16[16,2,64,128]{3,2,1,0:T(8,128)(2,1)S(1)}, u32[]{:S(2)}, u32[]{:S(2)}) async-start(bf16[16,2,64,128]{3,2,1,0:T(8,128)(2,1)} %shard_map.76), calls=%async_computation.2 | async-start | bytes 1048576 | tf_op jit(solution)/shard_map/all_to_all | solution.py:371
  50.4 18.1 %collective-permute-start = (bf16[2,352,128]{2,1,0:T(8,128)(2,1)S(1)}, bf16[2,352,128]{2,1,0:T(8,128)(2,1)S(1)}, u32[]{:S(2)}, u32[]{:S(2)}) collective-permute-start(bf16[2,352,128]{2,1,0:T(8,128)(2,1)S(1)} %get-tuple-element.36), channel_id=1, source_target_pairs={{0,16},{16,0},{32,48},{48,32},{1,17},{17,1},{33,49},{49,33},{2,18}... | collective-permute-start | bytes 540680 | tf_op jit(solution)/shard_map/ppermute | solution.py:382
  53.2 15.4 %collective-permute-start.2 = (bf16[2,160,128]{2,1,0:T(8,128)(2,1)S(1)}, bf16[2,160,128]{2,1,0:T(8,128)(2,1)S(1)}, u32[]{:S(2)}, u32[]{:S(2)}) collective-permute-start(bf16[2,160,128]{2,1,0:T(8,128)(2,1)S(1)} %get-tuple-element.37), channel_id=1, source_target_pairs={{0,48},{16,32},{32,16},{48,0},{1,49},{17,33},{33,17},{49,1},{2,50}... | collective-permute-start | bytes 245768 | tf_op jit(solution)/shard_map/ppermute | solution.py:382
  56.2 12.3 %collective-permute-start.1 = (bf16[2,160,128]{2,1,0:T(8,128)(2,1)S(1)}, bf16[2,160,128]{2,1,0:T(8,128)(2,1)S(1)}, u32[]{:S(2)}, u32[]{:S(2)}) collective-permute-start(bf16[2,160,128]{2,1,0:T(8,128)(2,1)S(1)} %get-tuple-element.37), channel_id=1, source_target_pairs={{0,32},{16,48},{32,0},{48,16},{1,33},{17,49},{33,1},{49,17},{2,34}... | collective-permute-start | bytes 245768 | tf_op jit(solution)/shard_map/ppermute | solution.py:382
  60.3 8.3 %collective-permute-start.3 = (bf16[2,128,128]{2,1,0:T(8,128)(2,1)S(1)}, bf16[2,128,128]{2,1,0:T(8,128)(2,1)S(1)}, u32[]{:S(2)}, u32[]{:S(2)}) collective-permute-start(bf16[2,128,128]{2,1,0:T(8,128)(2,1)S(1)} %get-tuple-element.38), channel_id=1, source_target_pairs={{16,32},{32,16},{48,64},{64,48},{80,96},{96,80},{112,128},{128,112... | collective-permute-start | bytes 196616 | tf_op jit(solution)/shard_map/ppermute | solution.py:420
  75.8 22.6 %all-to-all-start.3 = ((bf16[32,2,32,128]{3,2,1,0:T(8,128)(2,1)}), bf16[32,2,32,128]{3,2,1,0:T(8,128)(2,1)S(1)}, u32[]{:S(2)}, u32[]{:S(2)}) async-start(bf16[32,2,32,128]{3,2,1,0:T(8,128)(2,1)} %get-tuple-element.45), calls=%async_computation.3 | async-start | bytes 1048576 | tf_op jit(solution)/shard_map/all_to_all | solution.py:371
  81.5 16.9 %collective-permute-start.4 = (bf16[2,256,128]{2,1,0:T(8,128)(2,1)S(1)}, bf16[2,256,128]{2,1,0:T(8,128)(2,1)S(1)}, u32[]{:S(2)}, u32[]{:S(2)}) collective-permute-start(bf16[2,256,128]{2,1,0:T(8,128)(2,1)S(1)} %get-tuple-element.46), channel_id=1, source_target_pairs={{0,16},{16,0},{32,48},{48,32},{1,17},{17,1},{33,49},{49,33},{2,18}... | collective-permute-start | bytes 393224 | tf_op jit(solution)/shard_map/ppermute | solution.py:382
  84.3 14.1 %collective-permute-start.7 = (bf16[2,128,128]{2,1,0:T(8,128)(2,1)S(1)}, bf16[2,128,128]{2,1,0:T(8,128)(2,1)S(1)}, u32[]{:S(2)}, u32[]{:S(2)}) collective-permute-start(bf16[2,128,128]{2,1,0:T(8,128)(2,1)S(1)} %get-tuple-element.49), channel_id=1, source_target_pairs={{16,32},{32,16},{48,64},{64,48},{80,96},{96,80},{112,128},{128,112... | collective-permute-start | bytes 196616 | tf_op jit(solution)/shard_map/ppermute | solution.py:452
  88.3 7.3 %collective-permute-start.5 = (bf16[2,64,128]{2,1,0:T(8,128)(2,1)S(1)}, bf16[2,64,128]{2,1,0:T(8,128)(2,1)S(1)}, u32[]{:S(2)}, u32[]{:S(2)}) collective-permute-start(bf16[2,64,128]{2,1,0:T(8,128)(2,1)S(1)} %get-tuple-element.47), channel_id=1, source_target_pairs={{0,32},{16,48},{32,0},{48,16},{1,33},{17,49},{33,1},{49,17},{2,34}... | collective-permute-start | bytes 98312 | tf_op jit(solution)/shard_map/ppermute | solution.py:382
  91.3 7.0 %collective-permute-start.6 = (bf16[2,64,128]{2,1,0:T(8,128)(2,1)S(1)}, bf16[2,64,128]{2,1,0:T(8,128)(2,1)S(1)}, u32[]{:S(2)}, u32[]{:S(2)}) collective-permute-start(bf16[2,64,128]{2,1,0:T(8,128)(2,1)S(1)} %get-tuple-element.48), channel_id=1, source_target_pairs={{0,48},{16,32},{32,16},{48,0},{1,49},{17,33},{33,17},{49,1},{2,50}... | collective-permute-start | bytes 98312 | tf_op jit(solution)/shard_map/ppermute | solution.py:382
